TPU v7x, 32 devices: a whole 2x2x4 slice. The times are simulated.
32 devices in a mesh: ctx: 16 (over z, y, x), tp: 2 (over core).
Axes of the slice: x: 2, y: 2, z: 4, core: 2. Of those that a mesh axis runs over, the one named last changes fastest.
Arguments:
- queries: bfloat16 [4096, 4096], P('ctx', 'tp'), may hold values from -6 to 6
- keys: bfloat16 [4096, 4096], P('ctx', 'tp'), may hold values from -6 to 6
- values: bfloat16 [4096, 4096], P('ctx', 'tp'), may hold values from -6 to 6
- gain: float32 [4096], P('tp'), may hold values from 0.5 to 1.5
- out_weight: bfloat16 [4096, 6144], P('ctx', 'tp'), may hold values from -0.125 to 0.125
- cotangent: bfloat16 [4096, 6144], P('ctx', 'tp'), may hold values from -6 to 6
Outputs:
- mixed: bfloat16 [4096, 6144], P('ctx', 'tp')
- grad_queries: bfloat16 [4096, 4096], P('ctx', 'tp')
- grad_keys: bfloat16 [4096, 4096], P('ctx', 'tp')
- grad_values: bfloat16 [4096, 4096], P('ctx', 'tp')
All inputs are finite; a program needn't handle non-finite values.
Results may differ from a plain program's by a relative error of at most 0.005.
Values may be sent and summed in bfloat16 or wider, within the bound.
No kernel may reach another device: no remote copies, remote signals or barrier semaphores. Data moves between devices by JAX's collectives and lax.ppermute only.
A program may use at most 192 MiB of HBM per device.

v0:
```python
import jax
import jax.numpy as jnp
from jax import lax
from jax.sharding import PartitionSpec as P

DH = 128


def entering(value, axis, join, neutral, backward):
    count, mine = (lax.axis_size(axis), lax.axis_index(axis))
    pieces = lax.all_gather(value, axis)
    if backward:
        pieces = pieces[::-1]
        mine = count - 1 - mine
    running = jnp.full_like(value, 0) + jnp.asarray(neutral, value.dtype)

    def lap(position, running):
        longer = join(running, pieces[position])
        return jnp.where(position < mine, longer, running)

    return lax.fori_loop(0, count - 1, lap, running)


def add_states(earlier, later):
    return earlier + later


def local(queries, keys, values, gain, out_weight, cotangent):
    highest = lax.Precision.HIGHEST
    rows = queries.shape[0]
    heads = queries.shape[1] // DH
    q_heads = queries.reshape(rows, heads, DH)
    k_heads = keys.reshape(rows, heads, DH)
    v_heads = values.reshape(rows, heads, DH)
    q_float = q_heads.astype(jnp.float32)
    k_float = k_heads.astype(jnp.float32)
    v_float = v_heads.astype(jnp.float32)
    row_ids = lax.broadcasted_iota(jnp.int32, (rows, rows), 0)
    col_ids = lax.broadcasted_iota(jnp.int32, (rows, rows), 1)
    mask = (row_ids >= col_ids).astype(jnp.float32)
    zero_state = jnp.zeros((heads, DH, DH), jnp.float32)
    own_state = jnp.einsum("thd,the->hde", k_heads, v_heads, preferred_element_type=jnp.float32)
    prefix = entering(own_state, "ctx", add_states, zero_state, False)
    scores = (
        jnp.einsum("thd,shd->hts", q_heads, k_heads, preferred_element_type=jnp.float32)
        * mask[None]
    )
    attn = jnp.einsum("hts,shd->thd", scores, v_float, precision=highest)
    attn = attn + jnp.einsum("thd,hde->the", q_float, prefix, precision=highest)
    gain_heads = gain.reshape(heads, DH)
    rnorm = lax.rsqrt(jnp.mean(attn * attn, axis=-1, keepdims=True) + 1e-06)
    normed = attn * rnorm
    heads_out = (normed * gain_heads[None]).astype(jnp.bfloat16).reshape(rows, heads * DH)
    weight_all = lax.all_gather(out_weight, "ctx", axis=0, tiled=True)
    mixed = jnp.dot(
        lax.all_gather(heads_out, "tp", axis=1, tiled=True),
        weight_all,
        preferred_element_type=jnp.float32,
    ).astype(jnp.bfloat16)
    partial_grads = lax.dot_general(
        cotangent, weight_all, (((1,), (1,)), ((), ())), preferred_element_type=jnp.float32
    )
    grad_heads = lax.psum_scatter(partial_grads, "tp", scatter_dimension=1, tiled=True).reshape(
        rows, heads, DH
    )
    scaled = grad_heads * gain_heads[None]
    grad_attn = rnorm * (scaled - normed * jnp.mean(scaled * normed, axis=-1, keepdims=True))
    own_grad = jnp.einsum("thd,the->hde", q_float, grad_attn, precision=highest)
    later = entering(own_grad, "ctx", add_states, zero_state, True)
    weights = jnp.einsum("the,she->hts", grad_attn, v_float, precision=highest) * mask[None]
    grad_q = jnp.einsum("the,hde->thd", grad_attn, prefix, precision=highest)
    grad_q = grad_q + jnp.einsum("hts,shd->thd", weights, k_float, precision=highest)
    grad_k = jnp.einsum("she,hde->shd", v_float, later, precision=highest)
    grad_k = grad_k + jnp.einsum("hts,thd->shd", weights, q_float, precision=highest)
    grad_v = jnp.einsum("shd,hde->she", k_float, later, precision=highest)
    grad_v = grad_v + jnp.einsum("hts,the->she", scores, grad_attn, precision=highest)
    grad_queries = grad_q.reshape(rows, heads * DH).astype(jnp.bfloat16)
    grad_keys = grad_k.reshape(rows, heads * DH).astype(jnp.bfloat16)
    grad_values = grad_v.reshape(rows, heads * DH).astype(jnp.bfloat16)
    return (mixed, grad_queries, grad_keys, grad_values)


def solution(mesh):
    placed = (
        P("ctx", "tp"),
        P("ctx", "tp"),
        P("ctx", "tp"),
        P("tp"),
        P("ctx", "tp"),
        P("ctx", "tp"),
    )
    return jax.shard_map(
        local,
        mesh=mesh,
        in_specs=placed,
        out_specs=(P("ctx", "tp"), P("ctx", "tp"), P("ctx", "tp"), P("ctx", "tp")),
        check_vma=False,
    )
```

profile of v0, /device:TPU:0, one launch (start us, length us, event | category | flops | bytes accessed | tf_op | source)
XLA Modules:
  0.0 774.8 jit_solution(8741243820047883774)
XLA Ops:
  7.2 0.7 all-gather.9.cloned.1.call-update
  8.0 2.5 copy.59
  10.5 2.4 copy.34
  12.9 2.6 fusion.20
  15.6 269.2 %all-gather.9.cloned.1.call-done = bf16[4096,3072]{1,0:T(8,128)(2,1)} async-done(((bf16[256,3072]{1,0:T(8,128)(2,1)}), bf16[4096,3072]{1,0:T(8,128)(2,1)}) %all-gather.9.cloned.1.call-update) | async-done | bytes 25165840 | tf_op jit(solution)/shard_map/all_gather | solution.py:54
  284.8 13.6 %fusion.33 = f32[256,4096]{1,0:T(8,128)} fusion(bf16[256,3072]{1,0:T(8,128)(2,1)S(1)} %copy-done, bf16[4096,3072]{1,0:T(8,128)(2,1)} %all-gather.9.cloned.1.call-done), kind=kOutput, calls=%fused_computation.46 | convolution fusion | flops 6442450944 | bytes 30932992 | tf_op jit(solution)/shard_map/dot_general | solution.py:60
  298.4 1.6 copy.56
  300.0 2.7 fusion.23
  302.7 175.2 %all-gather.11.cloned.1.call-done = f32[256,128,128]{2,1,0:T(8,128)} async-done(((f32[16,128,128]{2,1,0:T(8,128)}), f32[256,128,128]{2,1,0:T(8,128)}) %all-gather.11.cloned.1.call-update) | async-done | bytes 16777232 | tf_op jit(solution)/shard_map/all_gather | solution.py:11
  477.9 24.7 %while.28 = (s32[]{:T(128)}, f32[16,128,128]{2,1,0:T(8,128)S(1)}, s32[]{:T(128)}, f32[16,16,128,128]{3,2,1,0:T(8,128)}, s32[]{:T(128)}, /*index=5*/s32[]{:T(128)}) while((s32[]{:T(128)}, f32[16,128,128]{2,1,0:T(8,128)S(1)}, s32[]{:T(128)}, f32[16,16,128,128]{3,2,1,0:T(8,128)}, s32[]{:T(128)}, /*index=5*/s32[]{:T(128)}) %tuple.83), condition=%wide.region_1.2_spmd.clone, body=%wide.region_0.1_spmd.clone.sunk | while | flops 786436 | bytes 3145829 | solution.py:21
  477.9 1.7 add_select_fusion.4
  479.6 1.6 add_select_fusion.4
  481.2 1.6 add_select_fusion.4
  482.9 1.6 add_select_fusion.4
  484.5 1.6 add_select_fusion.4
  486.1 1.9 add_select_fusion.4
  488.0 1.7 add_select_fusion.4
  489.7 1.6 add_select_fusion.4
  491.4 1.6 add_select_fusion.4
  493.0 1.6 add_select_fusion.4
  494.6 1.6 add_select_fusion.4
  496.2 1.6 add_select_fusion.4
  497.8 1.6 add_select_fusion.4
  499.5 1.6 add_select_fusion.4
  501.1 1.6 add_select_fusion.4
  502.7 1.1 fusion.32
  503.8 1.5 copy-done.4
  505.3 4.2 multiply_reduce_fusion.1
  509.5 3.0 copy.38
  512.6 2.2 multiply_reduce_fusion
  514.8 0.6 copy-done.10
  515.4 1.6 subtract_multiply_fusion
  517.0 0.2 all-gather.13.cloned.1.call-start
  517.3 2.1 convolution_bitcast_fusion
  519.3 2.6 copy.44
  522.0 3.3 fusion.18
  525.3 2.6 fusion.2
  527.9 2.9 fusion.9
  530.8 2.3 copy.49
  533.0 5.8 fusion
  538.8 4.1 fusion.4
  542.9 13.2 %convolution_convert_fusion = bf16[256,3072]{1,0:T(8,128)(2,1)} fusion(bf16[256,4096]{0,1:T(8,128)(2,1)} %all-gather.7.cloned.1.call-done, bf16[4096,3072]{1,0:T(8,128)(2,1)} %all-gather.9.cloned.1.call-done), kind=kOutput, calls=%fused_computation.10 | convolution fusion | flops 6443237376 | bytes 28835840 | tf_op jit(solution)/shard_map/dot_general | solution.py:55
  556.1 165.9 %all-gather.13.cloned.1.call-done = f32[256,128,128]{2,1,0:T(8,128)} async-done(((f32[16,128,128]{2,1,0:T(8,128)}), f32[256,128,128]{2,1,0:T(8,128)}) %all-gather.13.cloned.1.call-update) | async-done | bytes 16777232 | tf_op jit(solution)/shard_map/all_gather | solution.py:11
  722.0 11.6 %rev.3 = f32[16,16,128,128]{3,2,1,0:T(8,128)} reverse(f32[16,16,128,128]{3,2,1,0:T(8,128)} %bitcast.99), dimensions={0} | reverse | bytes 33554432 | tf_op jit(solution)/shard_map/rev | solution.py:13
  733.6 24.3 %while.29 = (s32[]{:T(128)}, f32[16,128,128]{2,1,0:T(8,128)S(1)}, s32[]{:T(128)}, f32[16,16,128,128]{3,2,1,0:T(8,128)}, s32[]{:T(128)}, /*index=5*/s32[]{:T(128)}) while((s32[]{:T(128)}, f32[16,128,128]{2,1,0:T(8,128)S(1)}, s32[]{:T(128)}, f32[16,16,128,128]{3,2,1,0:T(8,128)}, s32[]{:T(128)}, /*index=5*/s32[]{:T(128)}) %tuple.70), condition=%wide.region_6.7_spmd.clone, body=%wide.region_5.6_spmd.clone.sunk | while | flops 786436 | bytes 3145829 | solution.py:21
  733.6 1.7 add_select_fusion.5
  735.3 1.6 add_select_fusion.5
  736.9 1.6 add_select_fusion.5
  738.5 1.6 add_select_fusion.5
  740.1 1.6 add_select_fusion.5
  741.7 1.6 add_select_fusion.5
  743.4 1.6 add_select_fusion.5
  745.0 1.6 add_select_fusion.5
  746.6 1.6 add_select_fusion.5
  748.2 1.6 add_select_fusion.5
  749.8 1.6 add_select_fusion.5
  751.4 1.6 add_select_fusion.5
  753.0 1.6 add_select_fusion.5
  754.7 1.6 add_select_fusion.5
  756.3 1.6 add_select_fusion.5
  757.9 2.6 fusion.8
  760.5 1.4 copy.50
  761.9 4.1 add_convert_fusion
  766.0 2.3 copy.51
  (47 shorter events, 0.4 us)
Async XLA Ops:
  7.2 277.6 %copy-start = (bf16[256,3072]{1,0:T(8,128)(2,1)S(1)}, bf16[256,3072]{1,0:T(8,128)(2,1)}, u32[]{:S(2)}) copy-start(bf16[256,3072]{1,0:T(8,128)(2,1)} %param.15) | copy-start | bytes 4718596
  7.2 277.6 %all-gather.9.cloned.1.call-start = ((), (), s32[]{:S(2)}) async-start(), calls=%async_computation.2 | async-start | bytes 26738688 | tf_op jit(solution)/shard_map/all_gather | solution.py:54
  7.9 470.0 %all-gather.11.cloned.1.call-start = ((), (), s32[]{:S(2)}) async-start(), calls=%async_computation.4 | async-start | bytes 17825792 | tf_op jit(solution)/shard_map/all_gather | solution.py:11
  8.0 4.9 copy-start.11
  15.5 494.0 %reduce-scatter.2.cloned.1.call-start = ((), (), s32[]{:S(2)}) async-start(), calls=%async_computation.3 | async-start | bytes 6291456 | tf_op jit(solution)/shard_map/reduce_scatter | solution.py:63
  298.3 1.7 copy-start.14
  298.4 244.6 %all-gather.7.cloned.1.call-start = ((), (), s32[]{:S(2)}) async-start(), calls=%async_computation.1 | async-start | bytes 3145728 | tf_op jit(solution)/shard_map/all_gather | solution.py:56
  300.0 217.3 %copy-start.7 = (bf16[256,2048]{0,1:T(8,128)(2,1)}, bf16[256,2048]{0,1:T(8,128)(2,1)S(1)}, u32[]{:S(2)}) copy-start(bf16[256,2048]{0,1:T(8,128)(2,1)S(1)} %copy.56) | copy-start | bytes 3145732
  477.9 25.8 %copy-start.12 = (bf16[256,2048]{1,0:T(8,128)(2,1)S(1)}, bf16[256,2048]{1,0:T(8,128)(2,1)}, u32[]{:S(2)}) copy-start(bf16[256,2048]{1,0:T(8,128)(2,1)} %param.12) | copy-start | bytes 3145732
  502.7 1.1 copy-start.2
  502.7 2.6 copy-start.4
  509.5 3.1 copy-start.8
  509.5 3.1 copy-start.16
  512.6 2.2 copy-start.9
  512.6 2.8 copy-start.10
  517.0 204.9 %all-gather.13.cloned.1.call-start = ((), (), s32[]{:S(2)}) async-start(), calls=%async_computation.5 | async-start | bytes 17825792 | tf_op jit(solution)/shard_map/all_gather | solution.py:11
  521.9 3.3 copy-start.15
  525.3 5.5 copy-start.6
  525.3 2.6 copy-start.3
  533.0 5.8 copy-start.5
  733.6 24.3 %copy-start.13 = (bf16[256,2048]{1,0:T(8,128)(2,1)S(1)}, bf16[256,2048]{1,0:T(8,128)(2,1)}, u32[]{:S(2)}) copy-start(bf16[256,2048]{1,0:T(8,128)(2,1)} %param.12) | copy-start | bytes 3145732
  761.9 6.4 copy-start.1
Sparse Core Ops, SparseCore 0:
  10.8 273.9 all-gather.8
  288.1 189.7 all-gather.10
  480.2 10.2 reduce-scatter.1
  517.2 8.9 all-gather.6
  529.1 192.7 all-gather.12
where the time goes:
time: 776 us; the launch traced here: 775 us
  waiting for transfers between devices  611 us (79%)
  matrix products  64.7 us (8%)
  other arithmetic  52.1 us (7%)
  local copies, waits for them, and re-layouts  31.8 us (4%)
  between operations  14.1 us (2%)
    all_gather x2, waiting for transfers between devices, entering(): pieces = lax.all_gather(value, axis)  341 us
    all_gather x1, waiting for transfers between devices, local(): weight_all = lax.all_gather(out_weight, 'ctx', axis=0, tiled=True)  269 us
    select_n x30, other arithmetic, lap(): return jnp.where(position < mine, longer, running)  48.3 us
  transfers between devices with their start and end apart: 5, of which 3 were waited for; matrix products, arithmetic and copies ran while one was open for 12% of the time, Pallas kernels for 0%

commit v1 on v0

--- a/solution.py
+++ b/solution.py
@@ -1,9 +1,25 @@
+import math
+
 import jax
 import jax.numpy as jnp
 from jax import lax
+from jax.experimental import pallas as pl
+from jax.experimental.pallas import tpu as pltpu
 from jax.sharding import PartitionSpec as P
 
 DH = 128
+F32 = jnp.float32
+BF16 = jnp.bfloat16
+PLANE = 4
+PLANES = 4
+CHUNKS = ((0, 1), (2, 3))
+QUAD = 4
+PAIR = 2
+MIB = 1024 * 1024
+LIGHT = pl.CostEstimate(flops=1, bytes_accessed=1, transcendentals=0)
+NT = (((1,), (1,)), ((), ()))
+TN = (((0,), (0,)), ((), ()))
+NN = (((1,), (0,)), ((), ()))
 
 
 def entering(value, axis, join, neutral, backward):
@@ -80,6 +96,412 @@
     return (mixed, grad_queries, grad_keys, grad_values)
 
 
+def mm(a, b, dims):
+    return lax.dot_general(a, b, dims, preferred_element_type=F32)
+
+
+def two_terms(value):
+    high = value.astype(BF16)
+    return high, (value - high.astype(F32)).astype(BF16)
+
+
+def lower_mask(rows):
+    row_ids = lax.broadcasted_iota(jnp.int32, (rows, rows), 0)
+    col_ids = lax.broadcasted_iota(jnp.int32, (rows, rows), 1)
+    return row_ids >= col_ids
+
+
+def span(h):
+    return slice(h * DH, (h + 1) * DH)
+
+
+def states_kernel(pos, k_ref, v_ref, out_ref):
+    for h in range(QUAD):
+        out_ref[h] = mm(k_ref[:, span(h)], v_ref[:, span(h)], TN)
+
+
+def forward_kernel(pos, q_ref, k_ref, v_ref, gain_ref, prefix_ref, heads_ref, attn_ref):
+    mask = lower_mask(q_ref.shape[0])
+    for h in range(QUAD):
+        cols = span(h)
+        q = q_ref[:, cols]
+        scores = jnp.where(mask, mm(q, k_ref[:, cols], NT), 0.0)
+        high, low = two_terms(scores)
+        top, rest = two_terms(prefix_ref[h])
+        v = v_ref[:, cols]
+        attn = mm(high, v, NN) + mm(low, v, NN) + mm(q, top, NN) + mm(q, rest, NN)
+        rnorm = lax.rsqrt(jnp.mean(attn * attn, axis=-1, keepdims=True) + 1e-06)
+        attn_ref[:, cols] = attn
+        heads_ref[:, cols] = (attn * rnorm * gain_ref[:, cols]).astype(BF16)
+
+
+def norm_kernel(pos, q_ref, gain_ref, attn_ref, mine_ref, one_ref, two_ref, three_ref, *refs):
+    g_ref, own_ref = refs[-2:]
+    for h in range(PAIR):
+        cols = span(h)
+        attn = attn_ref[:, cols]
+        rnorm = lax.rsqrt(jnp.mean(attn * attn, axis=-1, keepdims=True) + 1e-06)
+        normed = attn * rnorm
+        grads = mine_ref[:, cols]
+        for ref in (one_ref, two_ref, three_ref):
+            grads = grads + ref[:, cols].astype(F32)
+        scaled = grads * gain_ref[:, cols]
+        shared = jnp.mean(scaled * normed, axis=-1, keepdims=True)
+        g = rnorm * (scaled - normed * shared)
+        g_ref[:, cols] = g
+        high, low = two_terms(g)
+        q = q_ref[:, cols]
+        own_ref[h] = mm(q, high, TN) + mm(q, low, TN)
+
+
+def inner_kernel(pos, q_ref, k_ref, v_ref, g_ref, first_ref, second_ref, *refs):
+    gq_ref, gk_ref, gv_ref = refs[-3:]
+    mask = lower_mask(q_ref.shape[0])
+    for h in range(PAIR):
+        cols = span(h)
+        q, k, v = q_ref[:, cols], k_ref[:, cols], v_ref[:, cols]
+        high, low = two_terms(g_ref[:, cols])
+        top, rest = two_terms((first_ref, second_ref)[h][0])
+        weights = jnp.where(mask, mm(high, v, NT) + mm(low, v, NT), 0.0).astype(BF16)
+        scores = jnp.where(mask, mm(q, k, NT), 0.0).astype(BF16)
+        across = mm(high, top, NT) + mm(high, rest, NT) + mm(low, top, NT)
+        gq_ref[:, cols] = (across + mm(weights, k, NN)).astype(BF16)
+        gk_ref[:, cols] = mm(weights, q, TN)
+        gv_ref[:, cols] = mm(scores, high, TN)
+
+
+def outer_kernel(pos, k_ref, v_ref, gk_ref, gv_ref, first_ref, second_ref, *refs):
+    gk_out, gv_out = refs[-2:]
+    for h in range(PAIR):
+        cols = span(h)
+        top, rest = two_terms((first_ref, second_ref)[h][0])
+        v, k = v_ref[:, cols], k_ref[:, cols]
+        gk_out[:, cols] = (gk_ref[:, cols] + mm(v, top, NT) + mm(v, rest, NT)).astype(BF16)
+        gv_out[:, cols] = (gv_ref[:, cols] + mm(k, top, NN) + mm(k, rest, NN)).astype(BF16)
+
+
+def by_heads(kernel, pos, ins, outs, flops, chunk=None, onto=(), after=()):
+    rows = ins[0][0].shape[0]
+    count = QUAD if chunk is None else PAIR
+    width = count * DH
+    each = PLANE if chunk is None else len(chunk)
+    steps = PLANE if chunk is None else 2 * each
+
+    def pair_of(s):
+        return s if chunk is None else (s // each) * PLANE + chunk[0] + s % each
+
+    def held(head, share, pos):
+        return (((head // share) ^ pos[0]) * share + head % share, 0, 0)
+
+    one = (1, DH, DH)
+    specs = {
+        "cols": pl.BlockSpec((rows, width), lambda s, pos: (0, pair_of(s))),
+        "row": pl.BlockSpec((1, width), lambda s, pos: (0, pair_of(s))),
+        "chunk": pl.BlockSpec((rows, width), lambda s, pos: (0, s)),
+        "own": pl.BlockSpec((count, DH, DH), lambda s, pos: (s, 0, 0)),
+        "xor": pl.BlockSpec((count, DH, DH), lambda s, pos: (s ^ pos[0], 0, 0)),
+        "prefix0": pl.BlockSpec(one, lambda s, pos: held(pair_of(s) * PAIR, QUAD, pos)),
+        "prefix1": pl.BlockSpec(one, lambda s, pos: held(pair_of(s) * PAIR + 1, QUAD, pos)),
+        "later0": pl.BlockSpec(one, lambda s, pos: held(s * PAIR, each, pos)),
+        "later1": pl.BlockSpec(one, lambda s, pos: held(s * PAIR + 1, each, pos)),
+    }
+    moved = sum(math.prod(shape) * jnp.dtype(dtype).itemsize for shape, dtype, _ in outs)
+    moved += sum(a.size * a.dtype.itemsize for a, _ in ins)
+    aliases = {1 + len(ins) + n: at for n, (_, at) in enumerate(onto)}
+    unread = [a for a, _ in onto] + list(after)
+    return pl.pallas_call(
+        kernel,
+        grid_spec=pltpu.PrefetchScalarGridSpec(
+            num_scalar_prefetch=1,
+            grid=(steps,),
+            in_specs=[specs[kind] for _, kind in ins] + [pl.BlockSpec(memory_space=pl.ANY)] * len(unread),
+            out_specs=[specs[kind] for _, _, kind in outs],
+        ),
+        out_shape=[jax.ShapeDtypeStruct(shape, dtype) for shape, dtype, _ in outs],
+        input_output_aliases=aliases,
+        compiler_params=pltpu.CompilerParams(vmem_limit_bytes=24 * MIB),
+        cost_estimate=LIGHT,
+    )(pos, *[a for a, _ in ins], *unread)
+
+
+def others_kernel(pos, cot_ref, w_ref, *refs):
+    out_ref = refs[-1]
+    for t in range(PLANE):
+        out_ref[t] = mm(cot_ref[t], w_ref[0], NT).astype(BF16)
+
+
+def mine_kernel(pos, cot_ref, w_ref, other_ref, *refs):
+    own_ref, sent = refs[-4], refs[-3:]
+    for t in range(PLANE):
+        total = mm(cot_ref[t], w_ref[0], NT) + other_ref[t].astype(F32)
+        if t == 0:
+            own_ref[...] = total
+        else:
+            sent[t - 1][...] = total.astype(BF16)
+
+
+def partial_grads(pos, cot, weights, taken=None, after=()):
+    planes, rows, width = weights.shape
+    blocks, tokens, _ = cot.shape
+    each = planes // 2
+    whole = (blocks, tokens, each * rows)
+    block = pl.BlockSpec((blocks, tokens, rows), lambda i, pos: (0, 0, i))
+    flat = pl.BlockSpec((tokens, rows), lambda i, pos: (0, i))
+
+    def plane_of(i, pos):
+        return ((1 - pos[2] if taken is None else pos[2]) * each + i, 0, 0)
+
+    in_specs = [pl.BlockSpec(cot.shape, lambda i, pos: (0, 0, 0)), pl.BlockSpec((1, rows, width), plane_of)]
+    if taken is None:
+        kernel, out_specs, out_shape, given = others_kernel, block, jax.ShapeDtypeStruct(whole, BF16), ()
+    else:
+        kernel, given = mine_kernel, (taken,)
+        in_specs.append(block)
+        out_specs = [flat] * blocks
+        out_shape = [jax.ShapeDtypeStruct(whole[1:], F32)] + [jax.ShapeDtypeStruct(whole[1:], BF16)] * (blocks - 1)
+    in_specs += [pl.BlockSpec(memory_space=pl.ANY)] * len(after)
+    return pl.pallas_call(
+        kernel,
+        grid_spec=pltpu.PrefetchScalarGridSpec(
+            num_scalar_prefetch=1, grid=(each,), in_specs=in_specs, out_specs=out_specs
+        ),
+        out_shape=out_shape,
+        compiler_params=pltpu.CompilerParams(vmem_limit_bytes=40 * MIB),
+        cost_estimate=LIGHT,
+    )(pos, cot, weights, *given, *after)
+
+
+def place_kernel(pos, *refs):
+    pieces, outs = refs[:PLANE], refs[PLANE:]
+    rows = pieces[0].shape[0]
+    for k, piece in enumerate(pieces):
+        j = pos[0] ^ k
+        for chunk, out in zip(CHUNKS, outs, strict=True):
+
+            def store(chunk=chunk, out=out, piece=piece, j=j):
+                within = jnp.clip(j - chunk[0], 0, len(chunk) - 1)
+                out[pl.ds(pl.multiple_of(within * rows, rows), rows)] = piece[...]
+
+            pl.when((j >= chunk[0]) & (j <= chunk[-1]))(store)
+
+
+def place_chunks(pos, pieces):
+    rows, width = pieces[0].shape
+    whole = pl.BlockSpec(memory_space=pltpu.VMEM)
+    return pl.pallas_call(
+        place_kernel,
+        in_specs=[pl.BlockSpec(memory_space=pltpu.SMEM)] + [whole] * len(pieces),
+        out_specs=[whole] * len(CHUNKS),
+        out_shape=[jax.ShapeDtypeStruct((len(chunk) * rows, width), BF16) for chunk in CHUNKS],
+        compiler_params=pltpu.CompilerParams(vmem_limit_bytes=16 * MIB),
+        cost_estimate=LIGHT,
+    )(pos, *pieces)
+
+
+def mixed_kernel(pos, *refs):
+    groups, weights = (refs[0:5], refs[5:10]), refs[10:12]
+    outs, held, sems = refs[-6:-2], refs[-2], refs[-1]
+    tokens, width = refs[0].shape
+    copies = []
+    for group, core in zip(groups, (pos[2], 1 - pos[2]), strict=True):
+        columns = pl.ds(pl.multiple_of(core * width, width), width)
+        for n, ref in enumerate(group):
+            if n < PLANE - 1:
+                target = held.at[n, :, columns]
+            else:
+                count = tokens // 2
+                target = held.at[PLANE - 1, pl.ds((n - PLANE + 1) * count, count), columns]
+            copy = pltpu.make_async_copy(ref, target, sems.at[len(copies)])
+            copy.start()
+            copies.append(copy)
+    for copy in copies:
+        copy.wait()
+    planes, rows = weights[0].shape[0], [ref.shape[1] for ref in weights]
+    for t in range(PLANE):
+
+        def add(i, total, t=t):
+            start = 0
+            for ref, count in zip(weights, rows, strict=True):
+                at = pl.multiple_of(i * sum(rows) + start, math.gcd(*rows))
+                total = total + mm(held[t, :, pl.ds(at, count)], ref[i], NN)
+                start += count
+            return total
+
+        outs[t][...] = lax.fori_loop(0, planes, add, jnp.zeros(outs[t].shape, F32)).astype(BF16)
+
+
+def mixed_blocks(pos, x_own, x_other, weights, after):
+    tokens, depth = x_own[0].shape
+    width = weights[0].shape[2]
+    given = list(x_own) + list(x_other)
+    whole = pl.BlockSpec(memory_space=pltpu.VMEM)
+    return pl.pallas_call(
+        mixed_kernel,
+        in_specs=[pl.BlockSpec(memory_space=pltpu.SMEM)]
+        + [pl.BlockSpec(memory_space=pl.ANY)] * len(given)
+        + [whole] * len(weights)
+        + [pl.BlockSpec(memory_space=pl.ANY)] * len(after),
+        out_specs=[whole] * PLANE,
+        out_shape=[jax.ShapeDtypeStruct((tokens, width), BF16)] * PLANE,
+        scratch_shapes=[
+            pltpu.VMEM((PLANE, tokens, 2 * depth), BF16),
+            pltpu.SemaphoreType.DMA((len(given),)),
+        ],
+        compiler_params=pltpu.CompilerParams(vmem_limit_bytes=40 * MIB),
+        cost_estimate=LIGHT,
+    )(pos, *given, *weights, *after)
+
+
+def plane_swap(value, k):
+    return lax.ppermute(value, "ctx", [(i, i ^ k) for i in range(PLANE * PLANES)])
+
+
+def core_swap(value):
+    return lax.ppermute(value, "tp", [(0, 1), (1, 0)])
+
+
+def z_shift(value, by):
+    count = PLANE * PLANES
+    pairs = [(i, i + by * PLANE) for i in range(count) if 0 <= i + by * PLANE < count]
+    return lax.ppermute(value, "ctx", pairs)
+
+
+def z_gather(value):
+    lines = [[z * PLANE + j for z in range(PLANES)] for j in range(PLANE)]
+    return lax.all_gather(value, "ctx", axis_index_groups=lines)
+
+
+def add_kernel(*refs):
+    refs[-1][...] = refs[0][...] + refs[1][...]
+
+
+def add_after(one, two, after):
+    whole = pl.BlockSpec(memory_space=pltpu.VMEM)
+    return pl.pallas_call(
+        add_kernel,
+        in_specs=[whole, whole] + [pl.BlockSpec(memory_space=pl.ANY)] * len(after),
+        out_specs=whole,
+        out_shape=jax.ShapeDtypeStruct(one.shape, one.dtype),
+    )(one, two, *after)
+
+
+def plane_parts(own, p):
+    count = own.shape[0] // PLANE
+    parts = [lax.dynamic_slice_in_dim(own, (p ^ k) * count, count, 0) for k in range(PLANE)]
+    parts = [parts[0]] + [plane_swap(parts[k], k) for k in range(1, PLANE)]
+    return parts, parts[0] + parts[1] + parts[2] + parts[3]
+
+
+def plane_sums(total, backward, after=()):
+    sign = -1 if backward else 1
+    near = z_shift(total, sign)
+    return near + z_shift(add_after(total, near, after) if after else total + near, 2 * sign)
+
+
+def plane_returns(parts, entering, p, backward):
+    given = []
+    for t in range(PLANE):
+        value = entering
+        for k in range(PLANE):
+            if k != t:
+                ahead = (p ^ k) > (p ^ t) if backward else (p ^ k) < (p ^ t)
+                value = value + jnp.where(ahead, parts[k], 0.0)
+        given.append(value)
+    back = [given[0]] + [plane_swap(given[k], k) for k in range(1, PLANE)]
+    return jnp.concatenate(back, axis=0)
+
+
+def plane_local(queries, keys, values, gain, out_weight, cotangent):
+    rows, columns = queries.shape
+    heads = columns // DH
+    at = lax.axis_index("ctx")
+    p, z = at % PLANE, at // PLANE
+    pos = jnp.stack([p, z, lax.axis_index("tp")]).astype(jnp.int32)
+    wide = out_weight.shape[1] // PLANE
+
+    def quarters(array):
+        cut = [lax.dynamic_slice_in_dim(array, (p ^ k) * wide, wide, 1) for k in range(PLANE)]
+        return [cut[0]] + [plane_swap(cut[k], k) for k in range(1, PLANE)]
+
+    lined = place_chunks(pos, quarters(out_weight))
+    weights = [z_gather(chunk) for chunk in lined]
+    cot_pieces = quarters(cotangent)
+
+    (own_state,) = by_heads(
+        states_kernel, pos, [(keys, "cols"), (values, "cols")], [((heads, DH, DH), F32, "own")], 2 * rows * columns * DH
+    )
+    parts, total = plane_parts(own_state, p)
+    prefix = plane_returns(parts, plane_sums(total, False, cot_pieces[1:]), p, False)
+    gain_row = gain.reshape(1, columns)
+    heads_out, attn = by_heads(
+        forward_kernel,
+        pos,
+        [(queries, "cols"), (keys, "cols"), (values, "cols"), (gain_row, "row"), (prefix, "xor")],
+        [((rows, columns), BF16, "cols"), ((rows, columns), F32, "cols")],
+        2 * rows * columns * (3 * rows + 2 * DH),
+    )
+    x_one, x_two = plane_swap(heads_out, 1), plane_swap(heads_out, 2)
+    x_three = plane_swap(x_one[: rows // 2], 2), plane_swap(x_two[rows // 2 :], 1)
+    x_own = [heads_out, x_one, x_two, *x_three]
+    x_other = [core_swap(x) for x in x_own]
+    cot = jnp.stack(cot_pieces)
+
+    grad_q = grad_k = grad_v = None
+    before_others, before_mine = (heads_out,), (x_one, x_two)
+    waiting = [(), (*x_three, *x_other)]
+    states = []
+    for n, (chunk, weight) in enumerate(zip(CHUNKS, weights, strict=True)):
+        last = n == len(CHUNKS) - 1
+        count = 2 * PAIR * len(chunk)
+        part = (rows, count * DH)
+        other = core_swap(partial_grads(pos, cot, weight, after=before_others))
+        mine, *sent = partial_grads(pos, cot, weight, other, (*before_mine, *waiting[n]))
+        blocks = mixed_blocks(pos, x_own, x_other, weights, (sent[0],)) if last else ()
+        taken = [plane_swap(sent[k - 1], k) for k in range(1, PLANE)]
+        g, own_grad = by_heads(
+            norm_kernel,
+            pos,
+            [(queries, "cols"), (gain_row, "row"), (attn, "cols"), (mine, "chunk")]
+            + [(value, "chunk") for value in taken],
+            [(part, F32, "chunk"), ((count, DH, DH), F32, "own")],
+            0,
+            chunk,
+            after=blocks[:1],
+        )
+        parts, total = plane_parts(own_grad, p)
+        before_others, before_mine = (own_grad,), (total,)
+        states.append((part, g, parts, total))
+    for chunk, (part, g, parts, total) in zip(CHUNKS, states, strict=True):
+        later = plane_returns(parts, plane_sums(total, True), p, True)
+        grad_q, inner_k, inner_v = by_heads(
+            inner_kernel,
+            pos,
+            [(queries, "cols"), (keys, "cols"), (values, "cols"), (g, "chunk"), (prefix, "prefix0"), (prefix, "prefix1")],
+            [((rows, columns), BF16, "cols"), (part, F32, "chunk"), (part, F32, "chunk")],
+            0,
+            chunk,
+            [] if grad_q is None else [(grad_q, 0)],
+        )
+        grad_k, grad_v = by_heads(
+            outer_kernel,
+            pos,
+            [(keys, "cols"), (values, "cols"), (inner_k, "chunk"), (inner_v, "chunk"), (later, "later0"), (later, "later1")],
+            [((rows, columns), BF16, "cols"), ((rows, columns), BF16, "cols")],
+            0,
+            chunk,
+            [] if grad_k is None else [(grad_k, 0), (grad_v, 1)],
+        )
+    mixed = jnp.zeros((rows, PLANE * wide), BF16)
+    for k in range(PLANE):
+        block = blocks[0] if k == 0 else plane_swap(blocks[k], k)
+        mixed = lax.dynamic_update_slice_in_dim(mixed, block, (p ^ k) * wide, 1)
+    return mixed, grad_q, grad_k, grad_v
+
+
+def planes_fit(mesh):
+    return mesh.shape["ctx"] == PLANE * PLANES and mesh.shape["tp"] == 2
+
+
 def solution(mesh):
     placed = (
         P("ctx", "tp"),
@@ -90,7 +512,7 @@
         P("ctx", "tp"),
     )
     return jax.shard_map(
-        local,
+        plane_local if planes_fit(mesh) else local,
         mesh=mesh,
         in_specs=placed,
         out_specs=(P("ctx", "tp"), P("ctx", "tp"), P("ctx", "tp"), P("ctx", "tp")),

time: 776 us -> 331 us (0.43)
  waiting for transfers between devices: 611 us -> 158 us
  starting transfers between devices: 0.38 us -> 66.3 us
  Pallas kernels: 0 us -> 65.4 us
  matrix products: 64.7 us -> 0 us
  other arithmetic: 52.1 us -> 5.56 us
  local copies, waits for them, and re-layouts: 31.8 us -> 20.5 us
    all_gather x4 -> x2, waiting for transfers between devices: 610 us -> 4.08 us  [z_gather(): return lax.all_gather(value, 'ctx', axis_index_groups=lines)]
    ppermute x0 -> x50, waiting for transfers between devices: none -> 154 us  [the longest x37 116 us: plane_swap(): lax.ppermute(value, 'ctx', [(i, i ^ k) for i in range(PLANE * PLANES)])]
    ppermute x0 -> x50, starting transfers between devices: none -> 66.2 us  [the longest x37 45.5 us: plane_swap(): lax.ppermute(value, 'ctx', [(i, i ^ k) for i in range(PLANE * PLANES)])]
    pallas_call x0 -> x15, Pallas kernels: none -> 65.4 us  [the longest x8 31.5 us: by_heads(): pl.pallas_call(kernel, grid_spec=pltpu.PrefetchScalarGridSpec(num_scalar_...]
    dot_general x14 -> x0, matrix products: 64.7 us -> none  [the longest x1 13.6 us: local(): lax.dot_general(cotangent, weight_all, (((1,), (1,)), ((), ())), preferre...]
    select_n x30 -> x0, other arithmetic: 48.3 us -> none  [lap(): return jnp.where(position < mine, longer, running)]
    rev x1 -> x0, local copies, waits for them, and re-layouts: 11.6 us -> none  [entering(): pieces = pieces[::-1]]
  transfers between devices with their start and end apart: 5 -> 52, of which waited for: 3 -> 27; matrix products, arithmetic and copies ran while one was open for 12% -> 4% of each run, Pallas kernels for 0% -> 16%
where the time goes in v1:
time: 331 us
  waiting for transfers between devices  158 us (48%)
  starting transfers between devices  66.3 us (20%)
  Pallas kernels  65.4 us (20%)
  local copies, waits for them, and re-layouts  20.5 us (6%)
  between operations  14.8 us (4%)
  other arithmetic  5.56 us (2%)
    ppermute x37, waiting for transfers between devices, plane_swap(): lax.ppermute(value, 'ctx', [(i, i ^ k) for i in range(PLANE * PLANES)])  116 us
    ppermute x37, starting transfers between devices, plane_swap(): lax.ppermute(value, 'ctx', [(i, i ^ k) for i in range(PLANE * PLANES)])  45.5 us
    ppermute x6, waiting for transfers between devices, z_shift(): return lax.ppermute(value, 'ctx', pairs)  36.7 us
    pallas_call x8, Pallas kernels, by_heads(): pl.pallas_call(kernel, grid_spec=pltpu.PrefetchScalarGridSpec(num_scalar_...  31.5 us
    ppermute x6, starting transfers between devices, z_shift(): return lax.ppermute(value, 'ctx', pairs)  20.1 us
    pallas_call x1, Pallas kernels, mixed_blocks(): pl.pallas_call(mixed_kernel, in_specs=[pl.BlockSpec(memory_space=pltpu.SM...  16.6 us
    pallas_call x4, Pallas kernels, partial_grads(): pl.pallas_call(kernel, grid_spec=pltpu.PrefetchScalarGridSpec(num_scalar_...  14.4 us
    unnamed x66, local copies, waits for them, and re-layouts  11.7 us
  transfers between devices with their start and end apart: 52, of which 27 were waited for; matrix products, arithmetic and copies ran while one was open for 4% of the time, Pallas kernels for 16%

profile of v1, /device:TPU:0, one launch (start us, length us, event | category | flops | bytes accessed | tf_op | source)
XLA Modules:
  0.0 330.8 jit_solution(13547371085239370997)
XLA Ops:
  7.3 2.4 constant_dynamic-slice_fusion.6
  9.7 2.9 collective-permute-start.20
  12.6 1.5 collective-permute-start.21
  14.2 8.5 %collective-permute-done.20.refs_1_ = bf16[256,768]{1,0:T(8,128)(2,1)S(1)} collective-permute-done((bf16[256,768]{1,0:T(8,128)(2,1)}, bf16[256,768]{1,0:T(8,128)(2,1)S(1)}, u32[]{:S(2)}, u32[]{:S(2)}) %collective-permute-start.20) | collective-permute-done | bytes 393248 | tf_op jit(solution)/shard_map/ppermute | solution.py:356
  22.7 9.1 %collective-permute-done.21.refs_2_ = bf16[256,768]{1,0:T(8,128)(2,1)S(1)} collective-permute-done((bf16[256,768]{1,0:T(8,128)(2,1)}, bf16[256,768]{1,0:T(8,128)(2,1)S(1)}, u32[]{:S(2)}, u32[]{:S(2)}) %collective-permute-start.21) | collective-permute-done | bytes 393248 | tf_op jit(solution)/shard_map/ppermute | solution.py:356
  34.9 1.8 shard_map.93
  39.8 1.4 collective-permute-start.2
  44.5 2.7 collective-permute-done
  47.2 1.5 collective-permute-start.6
  48.7 4.9 %collective-permute-done.1 = f32[4,128,128]{2,1,0:T(8,128)S(1)} collective-permute-done((f32[4,128,128]{2,1,0:T(8,128)}, f32[4,128,128]{2,1,0:T(8,128)S(1)}, u32[]{:S(2)}, u32[]{:S(2)}) %collective-permute-start.1) | collective-permute-done | bytes 262176 | tf_op jit(solution)/shard_map/ppermute | solution.py:356
  53.9 4.2 %collective-permute-start.3 = (f32[4,128,128]{2,1,0:T(8,128)S(1)}, f32[4,128,128]{2,1,0:T(8,128)}, u32[]{:S(2)}, u32[]{:S(2)}) collective-permute-start(f32[4,128,128]{2,1,0:T(8,128)S(1)} %add_add_fusion.refs_0_), channel_id=1, source_target_pairs={{0,8},{2,10},{4,12},{6,14},{8,16},{10,18},{12,20},{14,22},{16,24},... | collective-permute-start | bytes 786440 | tf_op jit(solution)/shard_map/ppermute | solution.py:366
  58.1 3.2 collective-permute-done.4.refs_2_
  61.3 7.4 %collective-permute-done.5.refs_3_ = bf16[256,768]{1,0:T(8,128)(2,1)S(1)} collective-permute-done((bf16[256,768]{1,0:T(8,128)(2,1)}, bf16[256,768]{1,0:T(8,128)(2,1)S(1)}, u32[]{:S(2)}, u32[]{:S(2)}) %collective-permute-start.5) | collective-permute-done | bytes 393248 | tf_op jit(solution)/shard_map/ppermute | solution.py:356
  69.6 1.8 shard_map.94
  71.4 10.6 %collective-permute-start.7 = (f32[4,128,128]{2,1,0:T(8,128)}, f32[4,128,128]{2,1,0:T(8,128)S(1)}, u32[]{:S(2)}, u32[]{:S(2)}) collective-permute-start(f32[4,128,128]{2,1,0:T(8,128)} %shard_map.94), channel_id=1, source_target_pairs={{0,16},{2,18},{4,20},{6,22},{8,24},{10,26},{12,28},{14,30},{1,17},... | collective-permute-start | bytes 786440 | tf_op jit(solution)/shard_map/ppermute | solution.py:366
  82.1 9.7 %collective-permute-done.7 = f32[4,128,128]{2,1,0:T(8,128)S(1)} collective-permute-done((f32[4,128,128]{2,1,0:T(8,128)}, f32[4,128,128]{2,1,0:T(8,128)S(1)}, u32[]{:S(2)}, u32[]{:S(2)}) %collective-permute-start.7) | collective-permute-done | bytes 262176 | tf_op jit(solution)/shard_map/ppermute | solution.py:366
  92.9 2.5 collective-permute-start.10
  96.8 3.6 %collective-permute-done.10 = f32[4,128,128]{2,1,0:T(8,128)S(1)} collective-permute-done((f32[4,128,128]{2,1,0:T(8,128)S(1)}, f32[4,128,128]{2,1,0:T(8,128)S(1)}, u32[]{:S(2)}, u32[]{:S(2)}) %collective-permute-start.10) | collective-permute-done | bytes 262176 | tf_op jit(solution)/shard_map/ppermute | solution.py:356
  100.3 2.8 collective-permute-done.8
  103.3 6.4 %shard_map.95 = (bf16[256,2048]{1,0:T(8,128)(2,1)}, f32[256,2048]{1,0:T(8,128)S(1)}) custom-call(s32[3]{0:T(128)S(1)} %pad_add_fusion.pos, bf16[256,2048]{1,0:T(8,128)(2,1)S(1)} %copy-done.9, bf16[256,2048]{1,0:T(8,128)(2,1)S(1)} %copy-done.1, bf16[256,2048]{1,0:T(8,128)(2,1)S(1)} %copy-done.4, f32[1,2048]{1,0:T(1,128)S(1)} %bitcast.17, ...), custom_call_target="tpu_custom_call" | custom-call | flops 1 | bytes 1 | tf_op jit(solution)/shard_map/pallas_call | solution.py:212
  111.1 1.9 copy-done.6
  113.0 2.7 shard_map.97
  115.9 1.6 collective-permute-start.11
  117.4 1.4 collective-permute-start.12
  118.9 22.9 %collective-permute-done.11.refs_0_.refs_1_ = bf16[256,2048]{1,0:T(8,128)(2,1)} collective-permute-done((bf16[256,2048]{1,0:T(8,128)(2,1)}, bf16[256,2048]{1,0:T(8,128)(2,1)}, u32[]{:S(2)}, u32[]{:S(2)}) %collective-permute-start.11) | collective-permute-done | bytes 1048608 | tf_op jit(solution)/shard_map/ppermute | solution.py:356
  143.0 2.9 shard_map.98
  146.5 1.4 collective-permute-start.25
  147.9 1.6 collective-permute-start.26
  149.5 11.4 %collective-permute-done.24.one_ref = bf16[256,1024]{1,0:T(8,128)(2,1)S(1)} collective-permute-done((bf16[256,1024]{1,0:T(8,128)(2,1)S(1)}, bf16[256,1024]{1,0:T(8,128)(2,1)S(1)}, u32[]{:S(2)}, u32[]{:S(2)}) %collective-permute-start.24) | collective-permute-done | bytes 524320 | tf_op jit(solution)/shard_map/ppermute | solution.py:356
  160.9 8.8 %collective-permute-done.25.two_ref = bf16[256,1024]{1,0:T(8,128)(2,1)S(1)} collective-permute-done((bf16[256,1024]{1,0:T(8,128)(2,1)S(1)}, bf16[256,1024]{1,0:T(8,128)(2,1)S(1)}, u32[]{:S(2)}, u32[]{:S(2)}) %collective-permute-start.25) | collective-permute-done | bytes 524320 | tf_op jit(solution)/shard_map/ppermute | solution.py:356
  169.7 1.6 collective-permute-done.26.three_ref
  171.3 3.1 shard_map.99
  175.3 4.1 %all-gather.7.cloned.1.call-done = bf16[2048,768]{1,0:T(8,128)(2,1)} async-done(((bf16[512,768]{1,0:T(8,128)(2,1)}), bf16[2048,768]{1,0:T(8,128)(2,1)}) %all-gather.7.cloned.1.call-update) | async-done | bytes 3145744 | tf_op jit(solution)/shard_map/all_gather | solution.py:371
  179.4 1.9 copy-done.8
  181.3 3.6 %shard_map.100 = bf16[4,256,1024]{2,1,0:T(8,128)(2,1)} custom-call(s32[3]{0:T(128)S(1)} %pad_add_fusion.pos, bf16[4,256,768]{2,1,0:T(8,128)(2,1)S(1)} %pad_maximum_fusion.cot_ref, bf16[4,512,768]{2,1,0:T(8,128)(2,1)S(1)} %bitcast.16, f32[8,128,128]{2,1,0:T(8,128)S(1)} %get-tuple-element.42.refs_0_), custom_call_target="tpu_custom_call" | custom-call | flops 1 | bytes 1 | tf_op jit(solution)/shard_map/pallas_call | solution.py:263
  184.9 1.9 slice.8
  186.8 1.5 collective-permute-start.13
  188.3 1.9 slice.9
  190.2 1.5 collective-permute-start.14
  192.2 9.3 %collective-permute-done.13.refs_1_.refs_3_ = bf16[128,2048]{1,0:T(8,128)(2,1)} collective-permute-done((bf16[128,2048]{1,0:T(8,128)(2,1)}, bf16[128,2048]{1,0:T(8,128)(2,1)}, u32[]{:S(2)}, u32[]{:S(2)}) %collective-permute-start.13) | collective-permute-done | bytes 524320 | tf_op jit(solution)/shard_map/ppermute | solution.py:356
  201.5 1.5 collective-permute-start.28
  202.9 2.2 collective-permute-done.14.refs_2_.refs_4_
  205.1 2.1 collective-permute-done.28
  207.2 1.7 collective-permute-start.30
  210.1 3.1 collective-permute-done.30
  215.5 5.1 %shard_map.101 = (f32[256,1024]{1,0:T(8,128)S(1)}, bf16[256,1024]{1,0:T(8,128)(2,1)}, bf16[256,1024]{1,0:T(8,128)(2,1)}, bf16[256,1024]{1,0:T(8,128)(2,1)}) custom-call(s32[3]{0:T(128)S(1)} %pad_add_fusion.pos, bf16[4,256,768]{2,1,0:T(8,128)(2,1)S(1)} %pad_maximum_fusion.cot_ref, bf16[4,512,768]{2,1,0:T(8,128)(2,1)} %bitcast.14, ...), custom_call_target="tpu_custom_call" | custom-call | flops 1 | bytes 1 | tf_op jit(solution)/shard_map/pallas_call | solution.py:263
  221.5 1.5 collective-permute-start.34
  226.3 15.2 %collective-permute-done.45 = f32[2,128,128]{2,1,0:T(8,128)S(1)} collective-permute-done((f32[2,128,128]{2,1,0:T(8,128)S(1)}, f32[2,128,128]{2,1,0:T(8,128)S(1)}, u32[]{:S(2)}, u32[]{:S(2)}) %collective-permute-start.45) | collective-permute-done | bytes 131104 | tf_op jit(solution)/shard_map/ppermute | solution.py:366
  242.2 1.5 collective-permute-start.46
  243.7 8.5 %collective-permute-done.46 = f32[2,128,128]{2,1,0:T(8,128)} collective-permute-done((f32[2,128,128]{2,1,0:T(8,128)}, f32[2,128,128]{2,1,0:T(8,128)}, u32[]{:S(2)}, u32[]{:S(2)}) %collective-permute-start.46) | collective-permute-done | bytes 131104 | tf_op jit(solution)/shard_map/ppermute | solution.py:366
  253.3 1.9 copy-done.7
  255.2 16.6 %shard_map.102 = (bf16[256,768]{1,0:T(8,128)(2,1)S(1)}, bf16[256,768]{1,0:T(8,128)(2,1)S(1)}, bf16[256,768]{1,0:T(8,128)(2,1)S(1)}, bf16[256,768]{1,0:T(8,128)(2,1)S(1)}) custom-call(s32[3]{0:T(128)S(1)} %pad_add_fusion.pos, bf16[256,2048]{1,0:T(8,128)(2,1)} %get-tuple-element.34.refs_0_, bf16[256,2048]{1,0:T(8,128)(2,1)} %collective-permute-done.11.refs_0_.refs_1_, ...), custom_call_target="tpu_custom_call" | custom-call | flops 1 | bytes 1 | tf_op jit(solution)/shard_map/pallas_call | solution.py:338
  271.9 3.1 shard_map.103
  275.1 1.5 collective-permute-start.37
  279.6 1.5 collective-permute-start.47
  283.2 2.4 collective-permute-done.38
  287.6 5.3 %shard_map.104 = (bf16[256,2048]{1,0:T(8,128)(2,1)}, f32[256,1024]{1,0:T(8,128)S(1)}, f32[256,1024]{1,0:T(8,128)S(1)}) custom-call(s32[3]{0:T(128)S(1)} %pad_add_fusion.pos, bf16[256,2048]{1,0:T(8,128)(2,1)S(1)} %copy-done.11, bf16[256,2048]{1,0:T(8,128)(2,1)S(1)} %copy-done.2, bf16[256,2048]{1,0:T(8,128)(2,1)S(1)} %copy-done.5, f32[256,1024]{1,0:T(8,128)S(1)} %copy-done.16, ...), custom_call_target="tpu_custom_call" | custom-call | flops 1 | bytes 1 | tf_op jit(solution)/shard_map/pallas_call | solution.py:212
  293.0 3.2 shard_map.106
  297.9 2.7 collective-permute-start.33
  300.7 3.2 collective-permute-done.41
  304.0 1.5 collective-permute-start.42
  307.6 7.6 %collective-permute-done.32 = bf16[256,768]{1,0:T(8,128)(2,1)S(1)} collective-permute-done((bf16[256,768]{1,0:T(8,128)(2,1)S(1)}, bf16[256,768]{1,0:T(8,128)(2,1)S(1)}, u32[]{:S(2)}, u32[]{:S(2)}) %collective-permute-start.32) | collective-permute-done | bytes 393248 | tf_op jit(solution)/shard_map/ppermute | solution.py:356
  315.4 5.4 %shard_map.105 = (bf16[256,2048]{1,0:T(8,128)(2,1)}, f32[256,1024]{1,0:T(8,128)S(1)}, f32[256,1024]{1,0:T(8,128)S(1)}) custom-call(s32[3]{0:T(128)S(1)} %pad_add_fusion.pos, bf16[256,2048]{1,0:T(8,128)(2,1)S(1)} %copy-done.11, bf16[256,2048]{1,0:T(8,128)(2,1)S(1)} %copy-done.2, bf16[256,2048]{1,0:T(8,128)(2,1)S(1)} %copy-done.5, ...), custom_call_target="tpu_custom_call", output_to_operand_aliasing={{0}: (7, {})} | custom-call | flops 1 | bytes 1 | tf_op jit(solution)/shard_map/pallas_call | solution.py:212
  320.8 3.1 shard_map.107
  (151 shorter events, 38.7 us)
Async XLA Ops:
  7.2 103.9 %all-gather.5.cloned.1.call-start = ((), (), s32[]{:S(2)}) async-start(), calls=%async_computation | async-start | bytes 3932160 | tf_op jit(solution)/shard_map/all_gather | solution.py:371
  9.7 25.2 %copy-start = (bf16[256,2048]{1,0:T(8,128)(2,1)S(1)}, bf16[256,2048]{1,0:T(8,128)(2,1)}, u32[]{:S(2)}) copy-start(bf16[256,2048]{1,0:T(8,128)(2,1)} %k_ref.11) | copy-start | bytes 3145732
  9.7 25.2 %copy-start.3 = (bf16[256,2048]{1,0:T(8,128)(2,1)S(1)}, bf16[256,2048]{1,0:T(8,128)(2,1)}, u32[]{:S(2)}) copy-start(bf16[256,2048]{1,0:T(8,128)(2,1)} %v_ref.11) | copy-start | bytes 3145732
  9.7 13.1 %collective-permute-start.20 = (bf16[256,768]{1,0:T(8,128)(2,1)}, bf16[256,768]{1,0:T(8,128)(2,1)S(1)}, u32[]{:S(2)}, u32[]{:S(2)}) collective-permute-start(bf16[256,768]{1,0:T(8,128)(2,1)} %get-tuple-element.75), channel_id=1, source_target_pairs={{0,2},{2,0},{4,6},{6,4},{8,10},{10,8},{12,14},{14,12},{16,18},{18,... | collective-permute-start | bytes 1179656 | tf_op jit(solution)/shard_map/ppermute | solution.py:356
  12.6 19.2 %collective-permute-start.21 = (bf16[256,768]{1,0:T(8,128)(2,1)}, bf16[256,768]{1,0:T(8,128)(2,1)S(1)}, u32[]{:S(2)}, u32[]{:S(2)}) collective-permute-start(bf16[256,768]{1,0:T(8,128)(2,1)} %get-tuple-element.77), channel_id=1, source_target_pairs={{0,4},{2,6},{4,0},{6,2},{8,12},{10,14},{12,8},{14,10},{16,20},{18,... | collective-permute-start | bytes 1179656 | tf_op jit(solution)/shard_map/ppermute | solution.py:356
  14.1 17.7 %collective-permute-start.22 = (bf16[256,768]{1,0:T(8,128)(2,1)}, bf16[256,768]{1,0:T(8,128)(2,1)}, u32[]{:S(2)}, u32[]{:S(2)}) collective-permute-start(bf16[256,768]{1,0:T(8,128)(2,1)} %get-tuple-element.74), channel_id=1, source_target_pairs={{0,6},{2,4},{4,2},{6,0},{8,14},{10,12},{12,10},{14,8},{16,22},{18,... | collective-permute-start | bytes 1179656 | tf_op jit(solution)/shard_map/ppermute | solution.py:356
  34.8 144.6 %all-gather.7.cloned.1.call-start = ((), (), s32[]{:S(2)}) async-start(), calls=%async_computation.1 | async-start | bytes 3932160 | tf_op jit(solution)/shard_map/all_gather | solution.py:371
  37.8 9.5 %collective-permute-start = (f32[4,128,128]{2,1,0:T(8,128)}, f32[4,128,128]{2,1,0:T(8,128)S(1)}, u32[]{:S(2)}, u32[]{:S(2)}) collective-permute-start(f32[4,128,128]{2,1,0:T(8,128)} %get-tuple-element.83), channel_id=1, source_target_pairs={{0,2},{2,0},{4,6},{6,4},{8,10},{10,8},{12,14},{14,12},{16,18},{18,... | collective-permute-start | bytes 786440 | tf_op jit(solution)/shard_map/ppermute | solution.py:356
  39.1 14.5 %collective-permute-start.1 = (f32[4,128,128]{2,1,0:T(8,128)}, f32[4,128,128]{2,1,0:T(8,128)S(1)}, u32[]{:S(2)}, u32[]{:S(2)}) collective-permute-start(f32[4,128,128]{2,1,0:T(8,128)} %get-tuple-element.82), channel_id=1, source_target_pairs={{0,4},{2,6},{4,0},{6,2},{8,12},{10,14},{12,8},{14,10},{16,20},{18,... | collective-permute-start | bytes 786440 | tf_op jit(solution)/shard_map/ppermute | solution.py:356
  39.8 14.0 %collective-permute-start.2 = (f32[4,128,128]{2,1,0:T(8,128)}, f32[4,128,128]{2,1,0:T(8,128)S(1)}, u32[]{:S(2)}, u32[]{:S(2)}) collective-permute-start(f32[4,128,128]{2,1,0:T(8,128)} %get-tuple-element.81), channel_id=1, source_target_pairs={{0,6},{2,4},{4,2},{6,0},{8,14},{10,12},{12,10},{14,8},{16,22},{18,... | collective-permute-start | bytes 786440 | tf_op jit(solution)/shard_map/ppermute | solution.py:356
  42.5 18.8 %collective-permute-start.4 = (bf16[256,768]{1,0:T(8,128)(2,1)}, bf16[256,768]{1,0:T(8,128)(2,1)S(1)}, u32[]{:S(2)}, u32[]{:S(2)}) collective-permute-start(bf16[256,768]{1,0:T(8,128)(2,1)} %get-tuple-element.72), channel_id=1, source_target_pairs={{0,2},{2,0},{4,6},{6,4},{8,10},{10,8},{12,14},{14,12},{16,18},{18,... | collective-permute-start | bytes 1179656 | tf_op jit(solution)/shard_map/ppermute | solution.py:356
  43.8 24.9 %collective-permute-start.5 = (bf16[256,768]{1,0:T(8,128)(2,1)}, bf16[256,768]{1,0:T(8,128)(2,1)S(1)}, u32[]{:S(2)}, u32[]{:S(2)}) collective-permute-start(bf16[256,768]{1,0:T(8,128)(2,1)} %get-tuple-element.71), channel_id=1, source_target_pairs={{0,4},{2,6},{4,0},{6,2},{8,12},{10,14},{12,8},{14,10},{16,20},{18,... | collective-permute-start | bytes 1179656 | tf_op jit(solution)/shard_map/ppermute | solution.py:356
  47.2 21.5 %collective-permute-start.6 = (bf16[256,768]{1,0:T(8,128)(2,1)}, bf16[256,768]{1,0:T(8,128)(2,1)S(1)}, u32[]{:S(2)}, u32[]{:S(2)}) collective-permute-start(bf16[256,768]{1,0:T(8,128)(2,1)} %get-tuple-element.73), channel_id=1, source_target_pairs={{0,6},{2,4},{4,2},{6,0},{8,14},{10,12},{12,10},{14,8},{16,22},{18,... | collective-permute-start | bytes 1179656 | tf_op jit(solution)/shard_map/ppermute | solution.py:356
  53.8 14.8 %copy-start.31 = (f32[4,128,128]{2,1,0:T(8,128)}, f32[4,128,128]{2,1,0:T(8,128)S(1)}, u32[]{:S(2)}) copy-start(f32[4,128,128]{2,1,0:T(8,128)S(1)} %add_add_fusion.refs_0_) | copy-start | bytes 786436
  53.9 14.8 %collective-permute-start.3 = (f32[4,128,128]{2,1,0:T(8,128)S(1)}, f32[4,128,128]{2,1,0:T(8,128)}, u32[]{:S(2)}, u32[]{:S(2)}) collective-permute-start(f32[4,128,128]{2,1,0:T(8,128)S(1)} %add_add_fusion.refs_0_), channel_id=1, source_target_pairs={{0,8},{2,10},{4,12},{6,14},{8,16},{10,18},{12,20},{14,22},{16,24},... | collective-permute-start | bytes 786440 | tf_op jit(solution)/shard_map/ppermute | solution.py:366
  71.4 20.4 %collective-permute-start.7 = (f32[4,128,128]{2,1,0:T(8,128)}, f32[4,128,128]{2,1,0:T(8,128)S(1)}, u32[]{:S(2)}, u32[]{:S(2)}) collective-permute-start(f32[4,128,128]{2,1,0:T(8,128)} %shard_map.94), channel_id=1, source_target_pairs={{0,16},{2,18},{4,20},{6,22},{8,24},{10,26},{12,28},{14,30},{1,17},... | collective-permute-start | bytes 786440 | tf_op jit(solution)/shard_map/ppermute | solution.py:366
  82.0 14.5 %copy-start.24 = (bf16[1,256,768]{2,1,0:T(8,128)(2,1)S(1)}, bf16[1,256,768]{2,1,0:T(8,128)(2,1)}, u32[]{:S(2)}) copy-start(bf16[1,256,768]{2,1,0:T(8,128)(2,1)} %get-tuple-element.70) | copy-start | bytes 1179652
  82.0 14.5 %copy-start.26 = (bf16[256,768]{1,0:T(8,128)(2,1)S(1)}, bf16[256,768]{1,0:T(8,128)(2,1)}, u32[]{:S(2)}) copy-start(bf16[256,768]{1,0:T(8,128)(2,1)} %copy-done.25) | copy-start | bytes 1179652
  82.0 14.5 %copy-start.28 = (bf16[256,768]{1,0:T(8,128)(2,1)S(1)}, bf16[256,768]{1,0:T(8,128)(2,1)}, u32[]{:S(2)}) copy-start(bf16[256,768]{1,0:T(8,128)(2,1)} %copy-done.27) | copy-start | bytes 1179652
  92.9 7.4 %collective-permute-start.10 = (f32[4,128,128]{2,1,0:T(8,128)S(1)}, f32[4,128,128]{2,1,0:T(8,128)S(1)}, u32[]{:S(2)}, u32[]{:S(2)}) collective-permute-start(f32[4,128,128]{2,1,0:T(8,128)S(1)} %get-tuple-element.79), channel_id=1, source_target_pairs={{0,6},{2,4},{4,2},{6,0},{8,14},{10,12},{12,10},{14,8},{16,22},{18,... | collective-permute-start | bytes 786440 | tf_op jit(solution)/shard_map/ppermute | solution.py:356
  95.5 7.7 %collective-permute-start.8 = (f32[4,128,128]{2,1,0:T(8,128)S(1)}, f32[4,128,128]{2,1,0:T(8,128)S(1)}, u32[]{:S(2)}, u32[]{:S(2)}) collective-permute-start(f32[4,128,128]{2,1,0:T(8,128)S(1)} %get-tuple-element.78), channel_id=1, source_target_pairs={{0,2},{2,0},{4,6},{6,4},{8,10},{10,8},{12,14},{14,12},{16,18},{18,... | collective-permute-start | bytes 786440 | tf_op jit(solution)/shard_map/ppermute | solution.py:356
  96.0 7.2 %collective-permute-start.9 = (f32[4,128,128]{2,1,0:T(8,128)S(1)}, f32[4,128,128]{2,1,0:T(8,128)S(1)}, u32[]{:S(2)}, u32[]{:S(2)}) collective-permute-start(f32[4,128,128]{2,1,0:T(8,128)S(1)} %get-tuple-element.80), channel_id=1, source_target_pairs={{0,4},{2,6},{4,0},{6,2},{8,12},{10,14},{12,8},{14,10},{16,20},{18,... | collective-permute-start | bytes 786440 | tf_op jit(solution)/shard_map/ppermute | solution.py:356
  115.7 55.5 %copy-start.10 = (bf16[256,2048]{1,0:T(8,128)(2,1)S(1)}, bf16[256,2048]{1,0:T(8,128)(2,1)}, u32[]{:S(2)}) copy-start(bf16[256,2048]{1,0:T(8,128)(2,1)} %q_ref.9) | copy-start | bytes 3145732
  115.8 55.5 %copy-start.13 = (f32[256,2048]{1,0:T(8,128)S(1)}, f32[256,2048]{1,0:T(8,128)}, u32[]{:S(2)}) copy-start(f32[256,2048]{1,0:T(8,128)} %copy-done.12) | copy-start | bytes 6291460
  115.8 27.2 %collective-permute-start.23 = (bf16[4,256,1024]{2,1,0:T(8,128)(2,1)S(1)}, bf16[4,256,1024]{2,1,0:T(8,128)(2,1)S(1)}, u32[]{:S(2)}, u32[]{:S(2)}) collective-permute-start(bf16[4,256,1024]{2,1,0:T(8,128)(2,1)S(1)} %shard_map.97), channel_id=1, source_target_pairs={{0,1},{1,0},{2,3},{3,2},{4,5},{5,4},{6,7},{7,6},{8,9},{9,8},{10,11... | collective-permute-start | bytes 6291464 | tf_op jit(solution)/shard_map/ppermute | solution.py:360
  115.9 25.9 %collective-permute-start.11 = (bf16[256,2048]{1,0:T(8,128)(2,1)}, bf16[256,2048]{1,0:T(8,128)(2,1)}, u32[]{:S(2)}, u32[]{:S(2)}) collective-permute-start(bf16[256,2048]{1,0:T(8,128)(2,1)} %get-tuple-element.34.refs_0_), channel_id=1, source_target_pairs={{0,2},{2,0},{4,6},{6,4},{8,10},{10,8},{12,14},{14,12},{16,18},{18,... | collective-permute-start | bytes 3145736 | tf_op jit(solution)/shard_map/ppermute | solution.py:356
  117.4 25.5 %collective-permute-start.12 = (bf16[256,2048]{1,0:T(8,128)(2,1)}, bf16[256,2048]{1,0:T(8,128)(2,1)}, u32[]{:S(2)}, u32[]{:S(2)}) collective-permute-start(bf16[256,2048]{1,0:T(8,128)(2,1)} %get-tuple-element.34.refs_0_), channel_id=1, source_target_pairs={{0,4},{2,6},{4,0},{6,2},{8,12},{10,14},{12,8},{14,10},{16,20},{18,... | collective-permute-start | bytes 3145736 | tf_op jit(solution)/shard_map/ppermute | solution.py:356
  145.9 14.9 %collective-permute-start.24 = (bf16[256,1024]{1,0:T(8,128)(2,1)S(1)}, bf16[256,1024]{1,0:T(8,128)(2,1)S(1)}, u32[]{:S(2)}, u32[]{:S(2)}) collective-permute-start(bf16[256,1024]{1,0:T(8,128)(2,1)S(1)} %get-tuple-element.39), channel_id=1, source_target_pairs={{0,2},{2,0},{4,6},{6,4},{8,10},{10,8},{12,14},{14,12},{16,18},{18,... | collective-permute-start | bytes 1572872 | tf_op jit(solution)/shard_map/ppermute | solution.py:356
  146.5 23.2 %collective-permute-start.25 = (bf16[256,1024]{1,0:T(8,128)(2,1)S(1)}, bf16[256,1024]{1,0:T(8,128)(2,1)S(1)}, u32[]{:S(2)}, u32[]{:S(2)}) collective-permute-start(bf16[256,1024]{1,0:T(8,128)(2,1)S(1)} %get-tuple-element.40), channel_id=1, source_target_pairs={{0,4},{2,6},{4,0},{6,2},{8,12},{10,14},{12,8},{14,10},{16,20},{18,... | collective-permute-start | bytes 1572872 | tf_op jit(solution)/shard_map/ppermute | solution.py:356
  147.9 23.3 %collective-permute-start.26 = (bf16[256,1024]{1,0:T(8,128)(2,1)S(1)}, bf16[256,1024]{1,0:T(8,128)(2,1)S(1)}, u32[]{:S(2)}, u32[]{:S(2)}) collective-permute-start(bf16[256,1024]{1,0:T(8,128)(2,1)S(1)} %get-tuple-element.41), channel_id=1, source_target_pairs={{0,6},{2,4},{4,2},{6,0},{8,14},{10,12},{12,10},{14,8},{16,22},{18,... | collective-permute-start | bytes 1572872 | tf_op jit(solution)/shard_map/ppermute | solution.py:356
  149.5 42.1 %collective-permute-start.15 = (bf16[256,2048]{1,0:T(8,128)(2,1)}, bf16[256,2048]{1,0:T(8,128)(2,1)}, u32[]{:S(2)}, u32[]{:S(2)}) collective-permute-start(bf16[256,2048]{1,0:T(8,128)(2,1)} %get-tuple-element.34.refs_0_), channel_id=1, source_target_pairs={{0,1},{1,0},{2,3},{3,2},{4,5},{5,4},{6,7},{7,6},{8,9},{9,8},{10,11... | collective-permute-start | bytes 3145736 | tf_op jit(solution)/shard_map/ppermute | solution.py:360
  184.9 30.5 %collective-permute-start.27 = (bf16[4,256,1024]{2,1,0:T(8,128)(2,1)}, bf16[4,256,1024]{2,1,0:T(8,128)(2,1)}, u32[]{:S(2)}, u32[]{:S(2)}) collective-permute-start(bf16[4,256,1024]{2,1,0:T(8,128)(2,1)} %shard_map.100), channel_id=1, source_target_pairs={{0,1},{1,0},{2,3},{3,2},{4,5},{5,4},{6,7},{7,6},{8,9},{9,8},{10,11... | collective-permute-start | bytes 6291464 | tf_op jit(solution)/shard_map/ppermute | solution.py:360
  186.8 14.7 %collective-permute-start.13 = (bf16[128,2048]{1,0:T(8,128)(2,1)}, bf16[128,2048]{1,0:T(8,128)(2,1)}, u32[]{:S(2)}, u32[]{:S(2)}) collective-permute-start(bf16[128,2048]{1,0:T(8,128)(2,1)} %slice.8), channel_id=1, source_target_pairs={{0,4},{2,6},{4,0},{6,2},{8,12},{10,14},{12,8},{14,10},{16,20},{18,... | collective-permute-start | bytes 1572872 | tf_op jit(solution)/shard_map/ppermute | solution.py:356
  190.2 15.0 %collective-permute-start.14 = (bf16[128,2048]{1,0:T(8,128)(2,1)}, bf16[128,2048]{1,0:T(8,128)(2,1)}, u32[]{:S(2)}, u32[]{:S(2)}) collective-permute-start(bf16[128,2048]{1,0:T(8,128)(2,1)} %slice.9), channel_id=1, source_target_pairs={{0,2},{2,0},{4,6},{6,4},{8,10},{10,8},{12,14},{14,12},{16,18},{18,... | collective-permute-start | bytes 1572872 | tf_op jit(solution)/shard_map/ppermute | solution.py:356
  191.6 22.5 %collective-permute-start.16 = (bf16[256,2048]{1,0:T(8,128)(2,1)}, bf16[256,2048]{1,0:T(8,128)(2,1)}, u32[]{:S(2)}, u32[]{:S(2)}) collective-permute-start(bf16[256,2048]{1,0:T(8,128)(2,1)} %collective-permute-done.11.refs_0_.refs_1_), channel_id=1, source_target_pairs={{0,1},{1,0},{2,3},{3,2},{4,5},{5,4},{6,7},{7,6},{8,9},{9,8},{10,11... | collective-permute-start | bytes 3145736 | tf_op jit(solution)/shard_map/ppermute | solution.py:360
  191.6 22.5 %collective-permute-start.17 = (bf16[256,2048]{1,0:T(8,128)(2,1)}, bf16[256,2048]{1,0:T(8,128)(2,1)}, u32[]{:S(2)}, u32[]{:S(2)}) collective-permute-start(bf16[256,2048]{1,0:T(8,128)(2,1)} %collective-permute-done.12.refs_1_.refs_2_), channel_id=1, source_target_pairs={{0,1},{1,0},{2,3},{3,2},{4,5},{5,4},{6,7},{7,6},{8,9},{9,8},{10,11... | collective-permute-start | bytes 3145736 | tf_op jit(solution)/shard_map/ppermute | solution.py:360
  201.5 5.8 %collective-permute-start.28 = (f32[2,128,128]{2,1,0:T(8,128)S(1)}, f32[2,128,128]{2,1,0:T(8,128)S(1)}, u32[]{:S(2)}, u32[]{:S(2)}) collective-permute-start(f32[2,128,128]{2,1,0:T(8,128)S(1)} %get-tuple-element.93), channel_id=1, source_target_pairs={{0,2},{2,0},{4,6},{6,4},{8,10},{10,8},{12,14},{14,12},{16,18},{18,... | collective-permute-start | bytes 393224 | tf_op jit(solution)/shard_map/ppermute | solution.py:356
  205.1 5.0 %collective-permute-start.29 = (f32[2,128,128]{2,1,0:T(8,128)S(1)}, f32[2,128,128]{2,1,0:T(8,128)S(1)}, u32[]{:S(2)}, u32[]{:S(2)}) collective-permute-start(f32[2,128,128]{2,1,0:T(8,128)S(1)} %get-tuple-element.95), channel_id=1, source_target_pairs={{0,4},{2,6},{4,0},{6,2},{8,12},{10,14},{12,8},{14,10},{16,20},{18,... | collective-permute-start | bytes 393224 | tf_op jit(solution)/shard_map/ppermute | solution.py:356
  207.2 6.0 %collective-permute-start.30 = (f32[2,128,128]{2,1,0:T(8,128)S(1)}, f32[2,128,128]{2,1,0:T(8,128)}, u32[]{:S(2)}, u32[]{:S(2)}) collective-permute-start(f32[2,128,128]{2,1,0:T(8,128)S(1)} %get-tuple-element.94), channel_id=1, source_target_pairs={{0,6},{2,4},{4,2},{6,0},{8,14},{10,12},{12,10},{14,8},{16,22},{18,... | collective-permute-start | bytes 393224 | tf_op jit(solution)/shard_map/ppermute | solution.py:356
  210.1 4.1 %collective-permute-start.18 = (bf16[128,2048]{1,0:T(8,128)(2,1)}, bf16[128,2048]{1,0:T(8,128)(2,1)}, u32[]{:S(2)}, u32[]{:S(2)}) collective-permute-start(bf16[128,2048]{1,0:T(8,128)(2,1)} %collective-permute-done.13.refs_1_.refs_3_), channel_id=1, source_target_pairs={{0,1},{1,0},{2,3},{3,2},{4,5},{5,4},{6,7},{7,6},{8,9},{9,8},{10,11... | collective-permute-start | bytes 1572872 | tf_op jit(solution)/shard_map/ppermute | solution.py:360
  213.2 2.3 collective-permute-start.19
  221.5 50.4 %collective-permute-start.34 = (bf16[256,1024]{1,0:T(8,128)(2,1)}, bf16[256,1024]{1,0:T(8,128)(2,1)S(1)}, u32[]{:S(2)}, u32[]{:S(2)}) collective-permute-start(bf16[256,1024]{1,0:T(8,128)(2,1)} %get-tuple-element.43.refs_12_), channel_id=1, source_target_pairs={{0,2},{2,0},{4,6},{6,4},{8,10},{10,8},{12,14},{14,12},{16,18},{18,... | collective-permute-start | bytes 1572872 | tf_op jit(solution)/shard_map/ppermute | solution.py:356
  223.0 48.9 %collective-permute-start.35 = (bf16[256,1024]{1,0:T(8,128)(2,1)}, bf16[256,1024]{1,0:T(8,128)(2,1)S(1)}, u32[]{:S(2)}, u32[]{:S(2)}) collective-permute-start(bf16[256,1024]{1,0:T(8,128)(2,1)} %get-tuple-element.49), channel_id=1, source_target_pairs={{0,4},{2,6},{4,0},{6,2},{8,12},{10,14},{12,8},{14,10},{16,20},{18,... | collective-permute-start | bytes 1572872 | tf_op jit(solution)/shard_map/ppermute | solution.py:356
  223.8 48.1 %collective-permute-start.36 = (bf16[256,1024]{1,0:T(8,128)(2,1)}, bf16[256,1024]{1,0:T(8,128)(2,1)S(1)}, u32[]{:S(2)}, u32[]{:S(2)}) collective-permute-start(bf16[256,1024]{1,0:T(8,128)(2,1)} %get-tuple-element.50), channel_id=1, source_target_pairs={{0,6},{2,4},{4,2},{6,0},{8,14},{10,12},{12,10},{14,8},{16,22},{18,... | collective-permute-start | bytes 1572872 | tf_op jit(solution)/shard_map/ppermute | solution.py:356
  225.0 16.5 %collective-permute-start.45 = (f32[2,128,128]{2,1,0:T(8,128)S(1)}, f32[2,128,128]{2,1,0:T(8,128)S(1)}, u32[]{:S(2)}, u32[]{:S(2)}) collective-permute-start(f32[2,128,128]{2,1,0:T(8,128)S(1)} %add_add_fusion.2.refs_0_), channel_id=1, source_target_pairs={{8,0},{10,2},{12,4},{14,6},{16,8},{18,10},{20,12},{22,14},{24,16},... | collective-permute-start | bytes 393224 | tf_op jit(solution)/shard_map/ppermute | solution.py:366
  242.2 10.0 %collective-permute-start.46 = (f32[2,128,128]{2,1,0:T(8,128)}, f32[2,128,128]{2,1,0:T(8,128)}, u32[]{:S(2)}, u32[]{:S(2)}) collective-permute-start(f32[2,128,128]{2,1,0:T(8,128)} %add.252), channel_id=1, source_target_pairs={{16,0},{18,2},{20,4},{22,6},{24,8},{26,10},{28,12},{30,14},{17,1},... | collective-permute-start | bytes 393224 | tf_op jit(solution)/shard_map/ppermute | solution.py:366
  255.2 16.7 %copy-start.11 = (bf16[256,2048]{1,0:T(8,128)(2,1)S(1)}, bf16[256,2048]{1,0:T(8,128)(2,1)}, u32[]{:S(2)}) copy-start(bf16[256,2048]{1,0:T(8,128)(2,1)} %q_ref.9) | copy-start | bytes 3145732
  255.2 16.7 %copy-start.14 = (f32[256,2048]{1,0:T(8,128)S(1)}, f32[256,2048]{1,0:T(8,128)}, u32[]{:S(2)}) copy-start(f32[256,2048]{1,0:T(8,128)} %copy-done.12) | copy-start | bytes 6291460
  255.2 16.7 %copy-start.18 = (f32[256,1024]{1,0:T(8,128)S(1)}, f32[256,1024]{1,0:T(8,128)}, u32[]{:S(2)}) copy-start(f32[256,1024]{1,0:T(8,128)} %copy-done.17) | copy-start | bytes 3145732
  271.9 15.6 %copy-start.16 = (f32[256,1024]{1,0:T(8,128)S(1)}, f32[256,1024]{1,0:T(8,128)}, u32[]{:S(2)}) copy-start(f32[256,1024]{1,0:T(8,128)} %copy-done.15) | copy-start | bytes 3145732
  275.1 6.8 %collective-permute-start.37 = (f32[2,128,128]{2,1,0:T(8,128)S(1)}, f32[2,128,128]{2,1,0:T(8,128)S(1)}, u32[]{:S(2)}, u32[]{:S(2)}) collective-permute-start(f32[2,128,128]{2,1,0:T(8,128)S(1)} %get-tuple-element.92), channel_id=1, source_target_pairs={{0,2},{2,0},{4,6},{6,4},{8,10},{10,8},{12,14},{14,12},{16,18},{18,... | collective-permute-start | bytes 393224 | tf_op jit(solution)/shard_map/ppermute | solution.py:356
  276.6 9.0 %collective-permute-start.38 = (f32[2,128,128]{2,1,0:T(8,128)S(1)}, f32[2,128,128]{2,1,0:T(8,128)S(1)}, u32[]{:S(2)}, u32[]{:S(2)}) collective-permute-start(f32[2,128,128]{2,1,0:T(8,128)S(1)} %get-tuple-element.91), channel_id=1, source_target_pairs={{0,4},{2,6},{4,0},{6,2},{8,12},{10,14},{12,8},{14,10},{16,20},{18,... | collective-permute-start | bytes 393224 | tf_op jit(solution)/shard_map/ppermute | solution.py:356
  277.3 8.9 %collective-permute-start.39 = (f32[2,128,128]{2,1,0:T(8,128)S(1)}, f32[2,128,128]{2,1,0:T(8,128)S(1)}, u32[]{:S(2)}, u32[]{:S(2)}) collective-permute-start(f32[2,128,128]{2,1,0:T(8,128)S(1)} %get-tuple-element.90), channel_id=1, source_target_pairs={{0,6},{2,4},{4,2},{6,0},{8,14},{10,12},{12,10},{14,8},{16,22},{18,... | collective-permute-start | bytes 393224 | tf_op jit(solution)/shard_map/ppermute | solution.py:356
  279.6 13.3 %collective-permute-start.47 = (f32[2,128,128]{2,1,0:T(8,128)S(1)}, f32[2,128,128]{2,1,0:T(8,128)S(1)}, u32[]{:S(2)}, u32[]{:S(2)}) collective-permute-start(f32[2,128,128]{2,1,0:T(8,128)S(1)} %get-tuple-element.84), channel_id=1, source_target_pairs={{0,2},{2,0},{4,6},{6,4},{8,10},{10,8},{12,14},{14,12},{16,18},{18,... | collective-permute-start | bytes 393224 | tf_op jit(solution)/shard_map/ppermute | solution.py:356
  281.1 11.8 %collective-permute-start.48 = (f32[2,128,128]{2,1,0:T(8,128)S(1)}, f32[2,128,128]{2,1,0:T(8,128)S(1)}, u32[]{:S(2)}, u32[]{:S(2)}) collective-permute-start(f32[2,128,128]{2,1,0:T(8,128)S(1)} %get-tuple-element.86), channel_id=1, source_target_pairs={{0,4},{2,6},{4,0},{6,2},{8,12},{10,14},{12,8},{14,10},{16,20},{18,... | collective-permute-start | bytes 393224 | tf_op jit(solution)/shard_map/ppermute | solution.py:356
  281.9 11.0 %collective-permute-start.49 = (f32[2,128,128]{2,1,0:T(8,128)S(1)}, f32[2,128,128]{2,1,0:T(8,128)S(1)}, u32[]{:S(2)}, u32[]{:S(2)}) collective-permute-start(f32[2,128,128]{2,1,0:T(8,128)S(1)} %get-tuple-element.85), channel_id=1, source_target_pairs={{0,6},{2,4},{4,2},{6,0},{8,14},{10,12},{12,10},{14,8},{16,22},{18,... | collective-permute-start | bytes 393224 | tf_op jit(solution)/shard_map/ppermute | solution.py:356
  285.6 15.0 %collective-permute-start.31 = (bf16[256,768]{1,0:T(8,128)(2,1)S(1)}, bf16[256,768]{1,0:T(8,128)(2,1)S(1)}, u32[]{:S(2)}, u32[]{:S(2)}) collective-permute-start(bf16[256,768]{1,0:T(8,128)(2,1)S(1)} %get-tuple-element.45), channel_id=1, source_target_pairs={{0,2},{2,0},{4,6},{6,4},{8,10},{10,8},{12,14},{14,12},{16,18},{18,... | collective-permute-start | bytes 1179656 | tf_op jit(solution)/shard_map/ppermute | solution.py:356
  286.2 9.9 %collective-permute-start.40 = (f32[2,128,128]{2,1,0:T(8,128)S(1)}, f32[2,128,128]{2,1,0:T(8,128)S(1)}, u32[]{:S(2)}, u32[]{:S(2)}) collective-permute-start(f32[2,128,128]{2,1,0:T(8,128)S(1)} %add_add_fusion.1), channel_id=1, source_target_pairs={{8,0},{10,2},{12,4},{14,6},{16,8},{18,10},{20,12},{22,14},{24,16},... | collective-permute-start | bytes 393224 | tf_op jit(solution)/shard_map/ppermute | solution.py:366
  296.1 7.8 %collective-permute-start.41 = (f32[2,128,128]{2,1,0:T(8,128)S(1)}, f32[2,128,128]{2,1,0:T(8,128)S(1)}, u32[]{:S(2)}, u32[]{:S(2)}) collective-permute-start(f32[2,128,128]{2,1,0:T(8,128)S(1)} %add.238), channel_id=1, source_target_pairs={{16,0},{18,2},{20,4},{22,6},{24,8},{26,10},{28,12},{30,14},{17,1},... | collective-permute-start | bytes 393224 | tf_op jit(solution)/shard_map/ppermute | solution.py:366
  297.7 17.6 %collective-permute-start.32 = (bf16[256,768]{1,0:T(8,128)(2,1)S(1)}, bf16[256,768]{1,0:T(8,128)(2,1)S(1)}, u32[]{:S(2)}, u32[]{:S(2)}) collective-permute-start(bf16[256,768]{1,0:T(8,128)(2,1)S(1)} %get-tuple-element.46), channel_id=1, source_target_pairs={{0,4},{2,6},{4,0},{6,2},{8,12},{10,14},{12,8},{14,10},{16,20},{18,... | collective-permute-start | bytes 1179656 | tf_op jit(solution)/shard_map/ppermute | solution.py:356
  297.9 17.4 %collective-permute-start.33 = (bf16[256,768]{1,0:T(8,128)(2,1)S(1)}, bf16[256,768]{1,0:T(8,128)(2,1)S(1)}, u32[]{:S(2)}, u32[]{:S(2)}) collective-permute-start(bf16[256,768]{1,0:T(8,128)(2,1)S(1)} %get-tuple-element.47), channel_id=1, source_target_pairs={{0,6},{2,4},{4,2},{6,0},{8,14},{10,12},{12,10},{14,8},{16,22},{18,... | collective-permute-start | bytes 1179656 | tf_op jit(solution)/shard_map/ppermute | solution.py:356
  304.0 16.7 %collective-permute-start.42 = (f32[2,128,128]{2,1,0:T(8,128)S(1)}, f32[2,128,128]{2,1,0:T(8,128)S(1)}, u32[]{:S(2)}, u32[]{:S(2)}) collective-permute-start(f32[2,128,128]{2,1,0:T(8,128)S(1)} %get-tuple-element.87), channel_id=1, source_target_pairs={{0,2},{2,0},{4,6},{6,4},{8,10},{10,8},{12,14},{14,12},{16,18},{18,... | collective-permute-start | bytes 393224 | tf_op jit(solution)/shard_map/ppermute | solution.py:356
  305.5 15.2 %collective-permute-start.43 = (f32[2,128,128]{2,1,0:T(8,128)S(1)}, f32[2,128,128]{2,1,0:T(8,128)S(1)}, u32[]{:S(2)}, u32[]{:S(2)}) collective-permute-start(f32[2,128,128]{2,1,0:T(8,128)S(1)} %get-tuple-element.89), channel_id=1, source_target_pairs={{0,4},{2,6},{4,0},{6,2},{8,12},{10,14},{12,8},{14,10},{16,20},{18,... | collective-permute-start | bytes 393224 | tf_op jit(solution)/shard_map/ppermute | solution.py:356
  306.3 14.5 %collective-permute-start.44 = (f32[2,128,128]{2,1,0:T(8,128)S(1)}, f32[2,128,128]{2,1,0:T(8,128)S(1)}, u32[]{:S(2)}, u32[]{:S(2)}) collective-permute-start(f32[2,128,128]{2,1,0:T(8,128)S(1)} %get-tuple-element.88), channel_id=1, source_target_pairs={{0,6},{2,4},{4,2},{6,0},{8,14},{10,12},{12,10},{14,8},{16,22},{18,... | collective-permute-start | bytes 393224 | tf_op jit(solution)/shard_map/ppermute | solution.py:356
  (21 other events, 96.6 us)
Sparse Core Ops, SparseCore 0:
  34.9 70.9 all-gather.4
  108.1 71.2 all-gather.6

commit v2 on v1

--- a/solution.py
+++ b/solution.py
@@ -1,3 +1,4 @@
+import functools
 import math
 
 import jax
@@ -115,9 +116,29 @@
     return slice(h * DH, (h + 1) * DH)
 
 
-def states_kernel(pos, k_ref, v_ref, out_ref):
-    for h in range(QUAD):
-        out_ref[h] = mm(k_ref[:, span(h)], v_ref[:, span(h)], TN)
+def prepare_kernel(pos, k_ref, v_ref, w_ref, *outs):
+    states, pieces = outs[:PLANE], outs[PLANE:]
+    width = pieces[0].shape[1]
+    for n in range(PLANE):
+        j = pos[0] ^ n
+        pieces[n][...] = w_ref[:, pl.ds(pl.multiple_of(j * width, DH), width)]
+        for h in range(QUAD):
+            cols = pl.ds(pl.multiple_of((j * QUAD + h) * DH, DH), DH)
+            states[n][h] = mm(k_ref[:, cols], v_ref[:, cols], TN)
+
+
+def prepare(pos, keys, values, out_weight):
+    whole = pl.BlockSpec(memory_space=pltpu.VMEM)
+    piece = (out_weight.shape[0], out_weight.shape[1] // PLANE)
+    out = pl.pallas_call(
+        prepare_kernel,
+        in_specs=[pl.BlockSpec(memory_space=pltpu.SMEM)] + [whole] * 3,
+        out_specs=[whole] * (2 * PLANE),
+        out_shape=[jax.ShapeDtypeStruct((QUAD, DH, DH), F32)] * PLANE + [jax.ShapeDtypeStruct(piece, BF16)] * PLANE,
+        compiler_params=pltpu.CompilerParams(vmem_limit_bytes=56 * MIB),
+        cost_estimate=LIGHT,
+    )(pos, keys, values, out_weight)
+    return out[:PLANE], out[PLANE:]
 
 
 def forward_kernel(pos, q_ref, k_ref, v_ref, gain_ref, prefix_ref, heads_ref, attn_ref):
@@ -170,11 +191,11 @@
         gv_ref[:, cols] = mm(scores, high, TN)
 
 
-def outer_kernel(pos, k_ref, v_ref, gk_ref, gv_ref, first_ref, second_ref, *refs):
+def outer_kernel(pos, k_ref, v_ref, gk_ref, gv_ref, later_ref, *refs):
     gk_out, gv_out = refs[-2:]
     for h in range(PAIR):
         cols = span(h)
-        top, rest = two_terms((first_ref, second_ref)[h][0])
+        top, rest = two_terms(later_ref[h])
         v, k = v_ref[:, cols], k_ref[:, cols]
         gk_out[:, cols] = (gk_ref[:, cols] + mm(v, top, NT) + mm(v, rest, NT)).astype(BF16)
         gv_out[:, cols] = (gv_ref[:, cols] + mm(k, top, NN) + mm(k, rest, NN)).astype(BF16)
@@ -202,8 +223,9 @@
         "xor": pl.BlockSpec((count, DH, DH), lambda s, pos: (s ^ pos[0], 0, 0)),
         "prefix0": pl.BlockSpec(one, lambda s, pos: held(pair_of(s) * PAIR, QUAD, pos)),
         "prefix1": pl.BlockSpec(one, lambda s, pos: held(pair_of(s) * PAIR + 1, QUAD, pos)),
-        "later0": pl.BlockSpec(one, lambda s, pos: held(s * PAIR, each, pos)),
-        "later1": pl.BlockSpec(one, lambda s, pos: held(s * PAIR + 1, each, pos)),
+        "later": pl.BlockSpec(
+            (PAIR, DH, DH), lambda s, pos: ((((s // 4) * 2 + s % 2) ^ pos[0]) * len(CHUNKS) + s % 4 // 2, 0, 0)
+        ),
     }
     moved = sum(math.prod(shape) * jnp.dtype(dtype).itemsize for shape, dtype, _ in outs)
     moved += sum(a.size * a.dtype.itemsize for a, _ in ins)
@@ -219,7 +241,7 @@
         ),
         out_shape=[jax.ShapeDtypeStruct(shape, dtype) for shape, dtype, _ in outs],
         input_output_aliases=aliases,
-        compiler_params=pltpu.CompilerParams(vmem_limit_bytes=24 * MIB),
+        compiler_params=pltpu.CompilerParams(vmem_limit_bytes=56 * MIB),
         cost_estimate=LIGHT,
     )(pos, *[a for a, _ in ins], *unread)
 
@@ -266,7 +288,7 @@
             num_scalar_prefetch=1, grid=(each,), in_specs=in_specs, out_specs=out_specs
         ),
         out_shape=out_shape,
-        compiler_params=pltpu.CompilerParams(vmem_limit_bytes=40 * MIB),
+        compiler_params=pltpu.CompilerParams(vmem_limit_bytes=56 * MIB),
         cost_estimate=LIGHT,
     )(pos, cot, weights, *given, *after)
 
@@ -293,63 +315,62 @@
         in_specs=[pl.BlockSpec(memory_space=pltpu.SMEM)] + [whole] * len(pieces),
         out_specs=[whole] * len(CHUNKS),
         out_shape=[jax.ShapeDtypeStruct((len(chunk) * rows, width), BF16) for chunk in CHUNKS],
-        compiler_params=pltpu.CompilerParams(vmem_limit_bytes=16 * MIB),
+        compiler_params=pltpu.CompilerParams(vmem_limit_bytes=56 * MIB),
         cost_estimate=LIGHT,
     )(pos, *pieces)
 
 
 def mixed_kernel(pos, *refs):
-    groups, weights = (refs[0:5], refs[5:10]), refs[10:12]
-    outs, held, sems = refs[-6:-2], refs[-2], refs[-1]
+    groups, weights = (refs[0:5], refs[5:10]), refs[10 : 10 + len(CHUNKS)]
+    outs, (held, stacked, x_sems, w_sems) = refs[-8:-4], refs[-4:]
     tokens, width = refs[0].shape
-    copies = []
+    planes, depth = weights[0].shape[0], sum(ref.shape[1] for ref in weights)
+    loads = []
+    for i in range(planes):
+        start = i * depth
+        for ref in weights:
+            target = stacked.at[pl.ds(start, ref.shape[1])]
+            loads.append(pltpu.make_async_copy(ref.at[i], target, w_sems.at[len(loads)]))
+            start += ref.shape[1]
+    blocks = [[] for _ in range(PLANE)]
+    count = 0
     for group, core in zip(groups, (pos[2], 1 - pos[2]), strict=True):
         columns = pl.ds(pl.multiple_of(core * width, width), width)
         for n, ref in enumerate(group):
-            if n < PLANE - 1:
-                target = held.at[n, :, columns]
-            else:
-                count = tokens // 2
-                target = held.at[PLANE - 1, pl.ds((n - PLANE + 1) * count, count), columns]
-            copy = pltpu.make_async_copy(ref, target, sems.at[len(copies)])
-            copy.start()
-            copies.append(copy)
-    for copy in copies:
+            target = held.at[min(n, PLANE - 1), :, columns]
+            if n >= PLANE - 1:
+                part = tokens // 2
+                target = held.at[PLANE - 1, pl.ds((n - PLANE + 1) * part, part), columns]
+            blocks[min(n, PLANE - 1)].append(pltpu.make_async_copy(ref, target, x_sems.at[count]))
+            count += 1
+    for copy in blocks[0] + loads + blocks[1] + blocks[2] + blocks[3]:
+        copy.start()
+    for copy in loads:
         copy.wait()
-    planes, rows = weights[0].shape[0], [ref.shape[1] for ref in weights]
     for t in range(PLANE):
-
-        def add(i, total, t=t):
-            start = 0
-            for ref, count in zip(weights, rows, strict=True):
-                at = pl.multiple_of(i * sum(rows) + start, math.gcd(*rows))
-                total = total + mm(held[t, :, pl.ds(at, count)], ref[i], NN)
-                start += count
-            return total
-
-        outs[t][...] = lax.fori_loop(0, planes, add, jnp.zeros(outs[t].shape, F32)).astype(BF16)
+        for copy in blocks[t]:
+            copy.wait()
+        outs[t][...] = mm(held[t], stacked[...], NN).astype(BF16)
 
 
 def mixed_blocks(pos, x_own, x_other, weights, after):
     tokens, depth = x_own[0].shape
     width = weights[0].shape[2]
-    given = list(x_own) + list(x_other)
-    whole = pl.BlockSpec(memory_space=pltpu.VMEM)
+    given = [*x_own, *x_other, *weights, *after]
     return pl.pallas_call(
         mixed_kernel,
-        in_specs=[pl.BlockSpec(memory_space=pltpu.SMEM)]
-        + [pl.BlockSpec(memory_space=pl.ANY)] * len(given)
-        + [whole] * len(weights)
-        + [pl.BlockSpec(memory_space=pl.ANY)] * len(after),
-        out_specs=[whole] * PLANE,
+        in_specs=[pl.BlockSpec(memory_space=pltpu.SMEM)] + [pl.BlockSpec(memory_space=pl.ANY)] * len(given),
+        out_specs=[pl.BlockSpec(memory_space=pltpu.VMEM)] * PLANE,
         out_shape=[jax.ShapeDtypeStruct((tokens, width), BF16)] * PLANE,
         scratch_shapes=[
             pltpu.VMEM((PLANE, tokens, 2 * depth), BF16),
-            pltpu.SemaphoreType.DMA((len(given),)),
+            pltpu.VMEM((2 * depth, width), BF16),
+            pltpu.SemaphoreType.DMA((2 * len(x_own),)),
+            pltpu.SemaphoreType.DMA((PLANES * len(weights),)),
         ],
-        compiler_params=pltpu.CompilerParams(vmem_limit_bytes=40 * MIB),
-        cost_estimate=LIGHT,
-    )(pos, *given, *weights, *after)
+        compiler_params=pltpu.CompilerParams(vmem_limit_bytes=56 * MIB),
+        cost_estimate=LIGHT,
+    )(pos, *given)
 
 
 def plane_swap(value, k):
@@ -371,31 +392,58 @@
     return lax.all_gather(value, "ctx", axis_index_groups=lines)
 
 
-def add_kernel(*refs):
-    refs[-1][...] = refs[0][...] + refs[1][...]
-
-
-def add_after(one, two, after):
+def add_kernel(count, *refs):
+    total = refs[0][...]
+    for ref in refs[1:count]:
+        total = total + ref[...]
+    refs[-1][...] = total
+
+
+def add_after(values, after):
     whole = pl.BlockSpec(memory_space=pltpu.VMEM)
     return pl.pallas_call(
-        add_kernel,
-        in_specs=[whole, whole] + [pl.BlockSpec(memory_space=pl.ANY)] * len(after),
+        functools.partial(add_kernel, len(values)),
+        in_specs=[whole] * len(values) + [pl.BlockSpec(memory_space=pl.ANY)] * len(after),
         out_specs=whole,
-        out_shape=jax.ShapeDtypeStruct(one.shape, one.dtype),
-    )(one, two, *after)
-
-
-def plane_parts(own, p):
-    count = own.shape[0] // PLANE
-    parts = [lax.dynamic_slice_in_dim(own, (p ^ k) * count, count, 0) for k in range(PLANE)]
-    parts = [parts[0]] + [plane_swap(parts[k], k) for k in range(1, PLANE)]
-    return parts, parts[0] + parts[1] + parts[2] + parts[3]
+        out_shape=jax.ShapeDtypeStruct(values[0].shape, values[0].dtype),
+        compiler_params=pltpu.CompilerParams(vmem_limit_bytes=56 * MIB),
+        cost_estimate=LIGHT,
+    )(*values, *after)
+
+
+def plane_swaps(parts):
+    return [parts[0]] + [plane_swap(parts[k], k) for k in range(1, PLANE)]
+
+
+def parts_kernel(pos, *refs):
+    owns, outs = refs[: len(CHUNKS)], refs[-PLANE:]
+    for k in range(PLANE):
+        start = 0
+        for own in owns:
+            count = own.shape[0] // PLANE
+            outs[k][start : start + count] = own[pl.ds((pos[0] ^ k) * count, count)]
+            start += count
+
+
+def plane_parts(owns, pos, after):
+    whole = pl.BlockSpec(memory_space=pltpu.VMEM)
+    part = (sum(own.shape[0] for own in owns) // PLANE, *owns[0].shape[1:])
+    parts = pl.pallas_call(
+        parts_kernel,
+        in_specs=[pl.BlockSpec(memory_space=pltpu.SMEM)] + [whole] * len(owns),
+        out_specs=[whole] * PLANE,
+        out_shape=[jax.ShapeDtypeStruct(part, owns[0].dtype)] * PLANE,
+        compiler_params=pltpu.CompilerParams(vmem_limit_bytes=56 * MIB),
+        cost_estimate=LIGHT,
+    )(pos, *owns)
+    parts = plane_swaps(parts)
+    return parts, add_after(parts, after)
 
 
 def plane_sums(total, backward, after=()):
     sign = -1 if backward else 1
-    near = z_shift(total, sign)
-    return near + z_shift(add_after(total, near, after) if after else total + near, 2 * sign)
+    near = z_shift(total.astype(BF16), sign).astype(F32)
+    return near + z_shift(add_after([total, near], after).astype(BF16), 2 * sign).astype(F32)
 
 
 def plane_returns(parts, entering, p, backward):
@@ -407,31 +455,23 @@
                 ahead = (p ^ k) > (p ^ t) if backward else (p ^ k) < (p ^ t)
                 value = value + jnp.where(ahead, parts[k], 0.0)
         given.append(value)
-    back = [given[0]] + [plane_swap(given[k], k) for k in range(1, PLANE)]
-    return jnp.concatenate(back, axis=0)
+    return jnp.concatenate(plane_swaps(given), axis=0)
 
 
 def plane_local(queries, keys, values, gain, out_weight, cotangent):
     rows, columns = queries.shape
-    heads = columns // DH
     at = lax.axis_index("ctx")
     p, z = at % PLANE, at // PLANE
     pos = jnp.stack([p, z, lax.axis_index("tp")]).astype(jnp.int32)
     wide = out_weight.shape[1] // PLANE
 
-    def quarters(array):
-        cut = [lax.dynamic_slice_in_dim(array, (p ^ k) * wide, wide, 1) for k in range(PLANE)]
-        return [cut[0]] + [plane_swap(cut[k], k) for k in range(1, PLANE)]
-
-    lined = place_chunks(pos, quarters(out_weight))
-    weights = [z_gather(chunk) for chunk in lined]
-    cot_pieces = quarters(cotangent)
-
-    (own_state,) = by_heads(
-        states_kernel, pos, [(keys, "cols"), (values, "cols")], [((heads, DH, DH), F32, "own")], 2 * rows * columns * DH
-    )
-    parts, total = plane_parts(own_state, p)
+    states, pieces = prepare(pos, keys, values, out_weight)
+    parts = plane_swaps(states)
+    total = add_after(parts, ())
+    weights = [z_gather(chunk) for chunk in place_chunks(pos, plane_swaps(pieces))]
+    cot_pieces = plane_swaps([lax.dynamic_slice_in_dim(cotangent, (p ^ k) * wide, wide, 1) for k in range(PLANE)])
     prefix = plane_returns(parts, plane_sums(total, False, cot_pieces[1:]), p, False)
+    cot = jnp.stack(cot_pieces)
     gain_row = gain.reshape(1, columns)
     heads_out, attn = by_heads(
         forward_kernel,
@@ -444,53 +484,57 @@
     x_three = plane_swap(x_one[: rows // 2], 2), plane_swap(x_two[rows // 2 :], 1)
     x_own = [heads_out, x_one, x_two, *x_three]
     x_other = [core_swap(x) for x in x_own]
-    cot = jnp.stack(cot_pieces)
-
-    grad_q = grad_k = grad_v = None
-    before_others, before_mine = (heads_out,), (x_one, x_two)
-    waiting = [(), (*x_three, *x_other)]
-    states = []
+
+    before_others, before_norm = (heads_out,), ()
+    before_mine = (x_one, x_two)
+    owns, inners = [], []
     for n, (chunk, weight) in enumerate(zip(CHUNKS, weights, strict=True)):
         last = n == len(CHUNKS) - 1
         count = 2 * PAIR * len(chunk)
-        part = (rows, count * DH)
-        other = core_swap(partial_grads(pos, cot, weight, after=before_others))
-        mine, *sent = partial_grads(pos, cot, weight, other, (*before_mine, *waiting[n]))
-        blocks = mixed_blocks(pos, x_own, x_other, weights, (sent[0],)) if last else ()
-        taken = [plane_swap(sent[k - 1], k) for k in range(1, PLANE)]
+        if n == 0:
+            other = core_swap(partial_grads(pos, cot, weight, after=before_others))
+            mine, *sent = partial_grads(pos, cot, weight, other, before_mine)
+        else:
+            mine, *sent = partial_grads(pos, cot, weight, core_swap(theirs), before_mine)
+        if last:
+            blocks = mixed_blocks(pos, x_own, x_other, weights, (sent[0],))
+            before_norm = (blocks[0], inners[0])
+        taken = plane_swaps([None, *sent])[1:]
+        if not last:
+            theirs = partial_grads(pos, cot, weights[n + 1], after=(*taken, *x_three))
+            before_norm = (theirs,)
         g, own_grad = by_heads(
             norm_kernel,
             pos,
             [(queries, "cols"), (gain_row, "row"), (attn, "cols"), (mine, "chunk")]
             + [(value, "chunk") for value in taken],
-            [(part, F32, "chunk"), ((count, DH, DH), F32, "own")],
+            [((rows, count * DH), F32, "chunk"), ((count, DH, DH), F32, "own")],
             0,
             chunk,
-            after=blocks[:1],
+            after=before_norm,
         )
-        parts, total = plane_parts(own_grad, p)
-        before_others, before_mine = (own_grad,), (total,)
-        states.append((part, g, parts, total))
-    for chunk, (part, g, parts, total) in zip(CHUNKS, states, strict=True):
-        later = plane_returns(parts, plane_sums(total, True), p, True)
-        grad_q, inner_k, inner_v = by_heads(
+        before_mine = (own_grad,)
+        owns.append(own_grad)
+        inners = by_heads(
             inner_kernel,
             pos,
             [(queries, "cols"), (keys, "cols"), (values, "cols"), (g, "chunk"), (prefix, "prefix0"), (prefix, "prefix1")],
-            [((rows, columns), BF16, "cols"), (part, F32, "chunk"), (part, F32, "chunk")],
+            [((rows, columns), BF16, "cols"), ((rows, columns), F32, "cols"), ((rows, columns), F32, "cols")],
             0,
             chunk,
-            [] if grad_q is None else [(grad_q, 0)],
+            list(zip(inners, range(3), strict=False)),
         )
-        grad_k, grad_v = by_heads(
-            outer_kernel,
-            pos,
-            [(keys, "cols"), (values, "cols"), (inner_k, "chunk"), (inner_v, "chunk"), (later, "later0"), (later, "later1")],
-            [((rows, columns), BF16, "cols"), ((rows, columns), BF16, "cols")],
-            0,
-            chunk,
-            [] if grad_k is None else [(grad_k, 0), (grad_v, 1)],
-        )
+    grad_q, inner_k, inner_v = inners
+    parts, total = plane_parts(owns, pos, ())
+    later = plane_returns(parts, plane_sums(total, True, (grad_q,)), p, True)
+    grad_k, grad_v = by_heads(
+        outer_kernel,
+        pos,
+        [(keys, "cols"), (values, "cols"), (inner_k, "cols"), (inner_v, "cols"), (later, "later")],
+        [((rows, columns), BF16, "cols"), ((rows, columns), BF16, "cols")],
+        0,
+        (0, 1, 2, 3),
+    )
     mixed = jnp.zeros((rows, PLANE * wide), BF16)
     for k in range(PLANE):
         block = blocks[0] if k == 0 else plane_swap(blocks[k], k)

time: 331 us -> 317 us (0.958); the launches traced: 331 us -> 312 us
  Pallas kernels: 65.4 us -> 96 us
  waiting for transfers between devices: 158 us -> 130 us
  starting transfers between devices: 66.3 us -> 51.6 us
  local copies, waits for them, and re-layouts: 20.5 us -> 9.78 us
  other arithmetic: 5.56 us -> 10.2 us
    ppermute x37 -> x31, waiting for transfers between devices: 116 us -> 86.9 us  [plane_swap(): lax.ppermute(value, 'ctx', [(i, i ^ k) for i in range(PLANE * PLANES)])]
    ppermute x6 -> x4, waiting for transfers between devices: 36.7 us -> 19.6 us  [z_shift(): return lax.ppermute(value, 'ctx', pairs)]
    all_gather x2, waiting for transfers between devices: 4.08 us -> 20 us  [z_gather(): return lax.all_gather(value, 'ctx', axis_index_groups=lines)]
    pallas_call x1 -> x6, Pallas kernels: 1.77 us -> 13.9 us  [the longest x4 7.49 us: add_after(): pl.pallas_call(functools.partial(add_kernel, len(values)), in_specs=[whol...]
    pallas_call x8 -> x6, Pallas kernels: 31.5 us -> 40.9 us  [by_heads(): pl.pallas_call(kernel, grid_spec=pltpu.PrefetchScalarGridSpec(num_scalar_...]
    pallas_call x4, Pallas kernels: 14.4 us -> 22.3 us  [partial_grads(): pl.pallas_call(kernel, grid_spec=pltpu.PrefetchScalarGridSpec(num_scalar_...]
    ppermute x37 -> x31, starting transfers between devices: 45.5 us -> 37.8 us  [plane_swap(): lax.ppermute(value, 'ctx', [(i, i ^ k) for i in range(PLANE * PLANES)])]
    ppermute x6 -> x4, starting transfers between devices: 20.1 us -> 12.6 us  [z_shift(): return lax.ppermute(value, 'ctx', pairs)]
  transfers between devices with their start and end apart: 52 -> 44, of which waited for: 27 -> 25; matrix products, arithmetic and copies ran while one was open for 4% -> 2% of each run, Pallas kernels for 16% -> 20%
where the time goes in v2:
time: 317 us; the launch traced here: 312 us
  waiting for transfers between devices  130 us (41%)
  Pallas kernels  96 us (30%)
  starting transfers between devices  51.6 us (16%)
  between operations  14.5 us (5%)
  other arithmetic  10.2 us (3%)
  local copies, waits for them, and re-layouts  9.78 us (3%)
    ppermute x31, waiting for transfers between devices, plane_swap(): lax.ppermute(value, 'ctx', [(i, i ^ k) for i in range(PLANE * PLANES)])  86.9 us
    pallas_call x6, Pallas kernels, by_heads(): pl.pallas_call(kernel, grid_spec=pltpu.PrefetchScalarGridSpec(num_scalar_...  40.9 us
    ppermute x31, starting transfers between devices, plane_swap(): lax.ppermute(value, 'ctx', [(i, i ^ k) for i in range(PLANE * PLANES)])  37.8 us
    pallas_call x4, Pallas kernels, partial_grads(): pl.pallas_call(kernel, grid_spec=pltpu.PrefetchScalarGridSpec(num_scalar_...  22.3 us
    all_gather x2, waiting for transfers between devices, z_gather(): return lax.all_gather(value, 'ctx', axis_index_groups=lines)  20 us
    ppermute x4, waiting for transfers between devices, z_shift(): return lax.ppermute(value, 'ctx', pairs)  19.6 us
    pallas_call x1, Pallas kernels, mixed_blocks(): pl.pallas_call(mixed_kernel, in_specs=[pl.BlockSpec(memory_space=pltpu.SM...  15.9 us
    ppermute x4, starting transfers between devices, z_shift(): return lax.ppermute(value, 'ctx', pairs)  12.6 us
  transfers between devices with their start and end apart: 44, of which 25 were waited for; matrix products, arithmetic and copies ran while one was open for 2% of the time, Pallas kernels for 20%

profile of v2, /device:TPU:0, one launch (start us, length us, event | category | flops | bytes accessed | tf_op | source)
XLA Modules:
  0.0 312.1 jit_solution(1546495028169350294)
XLA Ops:
  7.8 4.2 %shard_map.93 = (f32[4,128,128]{2,1,0:T(8,128)}, f32[4,128,128]{2,1,0:T(8,128)}, f32[4,128,128]{2,1,0:T(8,128)}, f32[4,128,128]{2,1,0:T(8,128)}, bf16[256,768]{1...) custom-call(s32[3]{0:T(128)} %pad_add_fusion.pos, ...), custom_call_target="tpu_custom_call" | custom-call | flops 1 | bytes 1 | tf_op jit(solution)/shard_map/pallas_call | solution.py:133
  12.0 2.9 collective-permute-start.20
  14.9 1.5 collective-permute-start.21
  16.5 8.6 %collective-permute-done.20.refs_1_ = bf16[256,768]{1,0:T(8,128)(2,1)S(1)} collective-permute-done((bf16[256,768]{1,0:T(8,128)(2,1)}, bf16[256,768]{1,0:T(8,128)(2,1)S(1)}, u32[]{:S(2)}, u32[]{:S(2)}) %collective-permute-start.20) | collective-permute-done | bytes 393248 | tf_op jit(solution)/shard_map/ppermute | solution.py:377
  25.1 9.1 %collective-permute-done.21.refs_2_ = bf16[256,768]{1,0:T(8,128)(2,1)S(1)} collective-permute-done((bf16[256,768]{1,0:T(8,128)(2,1)}, bf16[256,768]{1,0:T(8,128)(2,1)S(1)}, u32[]{:S(2)}, u32[]{:S(2)}) %collective-permute-start.21) | collective-permute-done | bytes 393248 | tf_op jit(solution)/shard_map/ppermute | solution.py:377
  35.0 2.8 shard_map.97
  38.7 1.2 collective-permute-start
  40.8 1.4 collective-permute-start.2
  42.4 1.6 collective-permute-start.5
  44.5 3.5 %collective-permute-done.refs_1_ = f32[4,128,128]{2,1,0:T(8,128)S(1)} collective-permute-done((f32[4,128,128]{2,1,0:T(8,128)S(1)}, f32[4,128,128]{2,1,0:T(8,128)S(1)}, u32[]{:S(2)}, u32[]{:S(2)}) %collective-permute-start) | collective-permute-done | bytes 262176 | tf_op jit(solution)/shard_map/ppermute | solution.py:377
  48.0 1.5 collective-permute-start.6
  49.5 4.3 %collective-permute-done.1.refs_2_ = f32[4,128,128]{2,1,0:T(8,128)S(1)} collective-permute-done((f32[4,128,128]{2,1,0:T(8,128)S(1)}, f32[4,128,128]{2,1,0:T(8,128)S(1)}, u32[]{:S(2)}, u32[]{:S(2)}) %collective-permute-start.1) | collective-permute-done | bytes 262176 | tf_op jit(solution)/shard_map/ppermute | solution.py:377
  55.3 2.0 shard_map.94.refs_0_
  58.3 3.5 %collective-permute-start.3 = (bf16[4,128,128]{2,1,0:T(8,128)(2,1)S(1)}, bf16[4,128,128]{2,1,0:T(8,128)(2,1)S(1)}, u32[]{:S(2)}, u32[]{:S(2)}) collective-permute-start(bf16[4,128,128]{2,1,0:T(8,128)(2,1)S(1)} %convert_element_type.24), channel_id=1, source_target_pairs={{0,8},{2,10},{4,12},{6,14},{8,16},{10,18},{12,20},{14,22},{16,24},... | collective-permute-start | bytes 393224 | tf_op jit(solution)/shard_map/ppermute | solution.py:387
  61.8 5.2 %collective-permute-done.3 = bf16[4,128,128]{2,1,0:T(8,128)(2,1)S(1)} collective-permute-done((bf16[4,128,128]{2,1,0:T(8,128)(2,1)S(1)}, bf16[4,128,128]{2,1,0:T(8,128)(2,1)S(1)}, u32[]{:S(2)}, u32[]{:S(2)}) %collective-permute-start.3) | collective-permute-done | bytes 131104 | tf_op jit(solution)/shard_map/ppermute | solution.py:387
  67.8 1.4 collective-permute-done.5.refs_3_
  70.8 1.8 shard_map.95
  73.7 6.5 %collective-permute-start.7 = (bf16[4,128,128]{2,1,0:T(8,128)(2,1)S(1)}, bf16[4,128,128]{2,1,0:T(8,128)(2,1)S(1)}, u32[]{:S(2)}, u32[]{:S(2)}) collective-permute-start(bf16[4,128,128]{2,1,0:T(8,128)(2,1)S(1)} %convert_element_type.26), channel_id=1, source_target_pairs={{0,16},{2,18},{4,20},{6,22},{8,24},{10,26},{12,28},{14,30},{1,17},... | collective-permute-start | bytes 393224 | tf_op jit(solution)/shard_map/ppermute | solution.py:387
  80.2 5.2 %collective-permute-done.7 = bf16[4,128,128]{2,1,0:T(8,128)(2,1)S(1)} collective-permute-done((bf16[4,128,128]{2,1,0:T(8,128)(2,1)S(1)}, bf16[4,128,128]{2,1,0:T(8,128)(2,1)S(1)}, u32[]{:S(2)}, u32[]{:S(2)}) %collective-permute-start.7) | collective-permute-done | bytes 131104 | tf_op jit(solution)/shard_map/ppermute | solution.py:387
  85.7 2.7 collective-permute-start.10
  89.3 1.3 pad_maximum_fusion.cot_ref
  90.6 2.5 collective-permute-done.10
  93.2 2.7 collective-permute-done.9
  97.2 7.8 %shard_map.96 = (bf16[256,2048]{1,0:T(8,128)(2,1)}, f32[256,2048]{1,0:T(8,128)}) custom-call(s32[3]{0:T(128)} %pad_add_fusion.pos, bf16[256,2048]{1,0:T(8,128)(2,1)} %q_ref.9, bf16[256,2048]{1,0:T(8,128)(2,1)} %k_ref.9, bf16[256,2048]{1,0:T(8,128)(2,1)} %v_ref.9, f32[1,2048]{1,0:T(1,128)} %bitcast.20, ...), custom_call_target="tpu_custom_call" | custom-call | flops 1 | bytes 1 | tf_op jit(solution)/shard_map/pallas_call | solution.py:234
  105.0 5.5 %shard_map.98 = bf16[4,256,1024]{2,1,0:T(8,128)(2,1)} custom-call(s32[3]{0:T(128)} %pad_add_fusion.pos, bf16[4,256,768]{2,1,0:T(8,128)(2,1)} %pad_maximum_fusion.cot_ref, bf16[4,512,768]{2,1,0:T(8,128)(2,1)} %bitcast.11, bf16[256,2048]{1,0:T(8,128)(2,1)} %get-tuple-element.48.refs_0_), custom_call_target="tpu_custom_call" | custom-call | flops 1 | bytes 1 | tf_op jit(solution)/shard_map/pallas_call | solution.py:285
  110.5 1.5 collective-permute-start.12
  112.9 23.2 %collective-permute-done.12.refs_1_.refs_2_ = bf16[256,2048]{1,0:T(8,128)(2,1)S(1)} collective-permute-done((bf16[256,2048]{1,0:T(8,128)(2,1)S(1)}, bf16[256,2048]{1,0:T(8,128)(2,1)S(1)}, u32[]{:S(2)}, u32[]{:S(2)}) %collective-permute-start.12) | collective-permute-done | bytes 1048608 | tf_op jit(solution)/shard_map/ppermute | solution.py:377
  136.2 1.5 collective-permute-start.14
  139.5 1.4 copy-done.5
  140.9 5.6 %shard_map.99 = (f32[256,1024]{1,0:T(8,128)}, bf16[256,1024]{1,0:T(8,128)(2,1)}, bf16[256,1024]{1,0:T(8,128)(2,1)}, bf16[256,1024]{1,0:T(8,128)(2,1)}) custom-call(s32[3]{0:T(128)} %pad_add_fusion.pos, bf16[4,256,768]{2,1,0:T(8,128)(2,1)} %pad_maximum_fusion.cot_ref, bf16[4,512,768]{2,1,0:T(8,128)(2,1)} %bitcast.12, bf16[4,256,1024]{2,1,0:T(8,128)(2,1)} %copy-done.5, ...), custom_call_target="tpu_custom_call" | custom-call | flops 1 | bytes 1 | tf_op jit(solution)/shard_map/pallas_call | solution.py:285
  146.5 1.2 collective-permute-start.24
  148.3 1.7 collective-permute-start.26
  151.1 2.6 collective-permute-done.13.refs_3_
  153.7 20.0 %all-gather.7.cloned.1.call-done = bf16[2048,768]{1,0:T(8,128)(2,1)} async-done(((bf16[512,768]{1,0:T(8,128)(2,1)}), bf16[2048,768]{1,0:T(8,128)(2,1)}) %all-gather.7.cloned.1.call-update) | async-done | bytes 3145744 | tf_op jit(solution)/shard_map/all_gather | solution.py:392
  175.4 5.5 %shard_map.100.refs_0_ = bf16[4,256,1024]{2,1,0:T(8,128)(2,1)} custom-call(s32[3]{0:T(128)} %pad_add_fusion.pos, bf16[4,256,768]{2,1,0:T(8,128)(2,1)} %pad_maximum_fusion.cot_ref, bf16[4,512,768]{2,1,0:T(8,128)(2,1)} %bitcast.14, bf16[256,1024]{1,0:T(8,128)(2,1)} %copy-done.9, bf16[256,1024]{1,0:T(8,128)(2,1)} %copy-done.10, ...), custom_call_target="tpu_custom_call" | custom-call | flops 1 | bytes 1 | tf_op jit(solution)/shard_map/pallas_call | solution.py:285
  182.0 5.6 %shard_map.101 = (f32[256,1024]{1,0:T(8,128)}, f32[8,128,128]{2,1,0:T(8,128)}) custom-call(s32[3]{0:T(128)} %pad_add_fusion.pos, bf16[256,2048]{1,0:T(8,128)(2,1)} %q_ref.9, f32[1,2048]{1,0:T(1,128)} %bitcast.21, f32[256,2048]{1,0:T(8,128)} %get-tuple-element.58.attn_ref, f32[256,1024]{1,0:T(8,128)} %get-tuple-element.59.mine_ref, ...), custom_call_target="tpu_custom_call" | custom-call | flops 1 | bytes 1 | tf_op jit(solution)/shard_map/pallas_call | solution.py:234
  187.6 2.9 collective-permute-done.27.other_ref
  190.6 1.2 copy-done.11
  191.8 5.7 %shard_map.102 = (f32[256,1024]{1,0:T(8,128)}, bf16[256,1024]{1,0:T(8,128)(2,1)}, bf16[256,1024]{1,0:T(8,128)(2,1)}, bf16[256,1024]{1,0:T(8,128)(2,1)}) custom-call(s32[3]{0:T(128)} %pad_add_fusion.pos, bf16[4,256,768]{2,1,0:T(8,128)(2,1)} %pad_maximum_fusion.cot_ref, bf16[4,512,768]{2,1,0:T(8,128)(2,1)} %bitcast.15, bf16[4,256,1024]{2,1,0:T(8,128)(2,1)} %copy-done.11, ...), custom_call_target="tpu_custom_call" | custom-call | flops 1 | bytes 1 | tf_op jit(solution)/shard_map/pallas_call | solution.py:285
  198.4 1.3 collective-permute-start.33
  199.7 1.3 collective-permute-start.31
  201.1 6.8 %shard_map.104 = (bf16[256,2048]{1,0:T(8,128)(2,1)}, f32[256,2048]{1,0:T(8,128)}, f32[256,2048]{1,0:T(8,128)}) custom-call(s32[3]{0:T(128)} %pad_add_fusion.pos, bf16[256,2048]{1,0:T(8,128)(2,1)} %q_ref.9, bf16[256,2048]{1,0:T(8,128)(2,1)} %k_ref.9, bf16[256,2048]{1,0:T(8,128)(2,1)} %v_ref.9, f32[256,1024]{1,0:T(8,128)} %get-tuple-element.69.g_ref, ...), custom_call_target="tpu_custom_call" | custom-call | flops 1 | bytes 1 | tf_op jit(solution)/shard_map/pallas_call | solution.py:234
  207.9 15.9 %shard_map.103 = (bf16[256,768]{1,0:T(8,128)(2,1)}, bf16[256,768]{1,0:T(8,128)(2,1)}, bf16[256,768]{1,0:T(8,128)(2,1)}, bf16[256,768]{1,0:T(8,128)(2,1)}) custom-call(s32[3]{0:T(128)} %pad_add_fusion.pos, bf16[256,2048]{1,0:T(8,128)(2,1)} %get-tuple-element.48.refs_0_, bf16[256,2048]{1,0:T(8,128)(2,1)} %copy-done.2, bf16[256,2048]{1,0:T(8,128)(2,1)} %copy-done, ...), custom_call_target="tpu_custom_call" | custom-call | flops 1 | bytes 1 | tf_op jit(solution)/shard_map/pallas_call | solution.py:360
  225.0 5.5 %shard_map.105 = (f32[256,1024]{1,0:T(8,128)}, f32[8,128,128]{2,1,0:T(8,128)}) custom-call(s32[3]{0:T(128)} %pad_add_fusion.pos, bf16[256,2048]{1,0:T(8,128)(2,1)} %q_ref.9, f32[1,2048]{1,0:T(1,128)} %bitcast.22, f32[256,2048]{1,0:T(8,128)} %get-tuple-element.58.attn_ref, f32[256,1024]{1,0:T(8,128)} %get-tuple-element.66.mine_ref, ...), custom_call_target="tpu_custom_call" | custom-call | flops 1 | bytes 1 | tf_op jit(solution)/shard_map/pallas_call | solution.py:234
  230.5 2.3 shard_map.107
  233.5 1.5 collective-permute-start.35
  235.0 1.3 collective-permute-start.36
  236.3 6.0 %collective-permute-done.34.refs_1_ = f32[4,128,128]{2,1,0:T(8,128)S(1)} collective-permute-done((f32[4,128,128]{2,1,0:T(8,128)}, f32[4,128,128]{2,1,0:T(8,128)S(1)}, u32[]{:S(2)}, u32[]{:S(2)}) %collective-permute-start.34) | collective-permute-done | bytes 262176 | tf_op jit(solution)/shard_map/ppermute | solution.py:377
  242.2 4.3 %collective-permute-done.35.refs_2_ = f32[4,128,128]{2,1,0:T(8,128)S(1)} collective-permute-done((f32[4,128,128]{2,1,0:T(8,128)}, f32[4,128,128]{2,1,0:T(8,128)S(1)}, u32[]{:S(2)}, u32[]{:S(2)}) %collective-permute-start.35) | collective-permute-done | bytes 262176 | tf_op jit(solution)/shard_map/ppermute | solution.py:377
  247.4 2.0 shard_map.108.refs_0_
  250.3 1.3 collective-permute-start.37
  251.6 6.8 %shard_map.106 = (bf16[256,2048]{1,0:T(8,128)(2,1)}, f32[256,2048]{1,0:T(8,128)}, f32[256,2048]{1,0:T(8,128)}) custom-call(s32[3]{0:T(128)} %pad_add_fusion.pos, bf16[256,2048]{1,0:T(8,128)(2,1)} %q_ref.9, bf16[256,2048]{1,0:T(8,128)(2,1)} %k_ref.9, bf16[256,2048]{1,0:T(8,128)(2,1)} %v_ref.9, ...), custom_call_target="tpu_custom_call", output_to_operand_aliasing={{0}: (7, {}), {1}: (8, {}), {2}: (9, {})} | custom-call | flops 1 | bytes 1 | tf_op jit(solution)/shard_map/pallas_call | solution.py:234
  258.5 3.3 %collective-permute-done.37 = bf16[4,128,128]{2,1,0:T(8,128)(2,1)S(1)} collective-permute-done((bf16[4,128,128]{2,1,0:T(8,128)(2,1)S(1)}, bf16[4,128,128]{2,1,0:T(8,128)(2,1)S(1)}, u32[]{:S(2)}, u32[]{:S(2)}) %collective-permute-start.37) | collective-permute-done | bytes 131104 | tf_op jit(solution)/shard_map/ppermute | solution.py:387
  262.5 1.8 shard_map.109
  265.4 1.3 collective-permute-start.38
  266.7 1.7 collective-permute-start.28
  269.1 1.1 collective-permute-start.30
  270.5 5.9 %collective-permute-done.38 = bf16[4,128,128]{2,1,0:T(8,128)(2,1)S(1)} collective-permute-done((bf16[4,128,128]{2,1,0:T(8,128)(2,1)S(1)}, bf16[4,128,128]{2,1,0:T(8,128)(2,1)S(1)}, u32[]{:S(2)}, u32[]{:S(2)}) %collective-permute-start.38) | collective-permute-done | bytes 131104 | tf_op jit(solution)/shard_map/ppermute | solution.py:387
  276.7 1.9 collective-permute-start.41
  278.5 1.3 collective-permute-start.40
  280.5 10.0 %collective-permute-done.29 = bf16[256,768]{1,0:T(8,128)(2,1)S(1)} collective-permute-done((bf16[256,768]{1,0:T(8,128)(2,1)S(1)}, bf16[256,768]{1,0:T(8,128)(2,1)S(1)}, u32[]{:S(2)}, u32[]{:S(2)}) %collective-permute-start.29) | collective-permute-done | bytes 393248 | tf_op jit(solution)/shard_map/ppermute | solution.py:377
  290.7 2.2 collective-permute-done.41
  292.9 2.9 collective-permute-done.40
  297.0 8.3 %shard_map.110 = (bf16[256,2048]{1,0:T(8,128)(2,1)}, bf16[256,2048]{1,0:T(8,128)(2,1)}) custom-call(s32[3]{0:T(128)} %pad_add_fusion.pos, bf16[256,2048]{1,0:T(8,128)(2,1)} %k_ref.9, bf16[256,2048]{1,0:T(8,128)(2,1)} %v_ref.9, f32[256,2048]{1,0:T(8,128)} %get-tuple-element.75.gk_ref, f32[256,2048]{1,0:T(8,128)} %get-tuple-element.76.gv_ref, ...), custom_call_target="tpu_custom_call" | custom-call | flops 1 | bytes 1 | tf_op jit(solution)/shard_map/pallas_call | solution.py:234
  (162 shorter events, 28.9 us)
Async XLA Ops:
  7.2 97.8 %all-gather.5.cloned.1.call-start = ((), (), s32[]{:S(2)}) async-start(), calls=%async_computation | async-start | bytes 3932160 | tf_op jit(solution)/shard_map/all_gather | solution.py:392
  12.0 13.1 %collective-permute-start.20 = (bf16[256,768]{1,0:T(8,128)(2,1)}, bf16[256,768]{1,0:T(8,128)(2,1)S(1)}, u32[]{:S(2)}, u32[]{:S(2)}) collective-permute-start(bf16[256,768]{1,0:T(8,128)(2,1)} %get-tuple-element.50), channel_id=1, source_target_pairs={{0,2},{2,0},{4,6},{6,4},{8,10},{10,8},{12,14},{14,12},{16,18},{18,... | collective-permute-start | bytes 1179656 | tf_op jit(solution)/shard_map/ppermute | solution.py:377
  14.9 19.2 %collective-permute-start.21 = (bf16[256,768]{1,0:T(8,128)(2,1)}, bf16[256,768]{1,0:T(8,128)(2,1)S(1)}, u32[]{:S(2)}, u32[]{:S(2)}) collective-permute-start(bf16[256,768]{1,0:T(8,128)(2,1)} %get-tuple-element.51), channel_id=1, source_target_pairs={{0,4},{2,6},{4,0},{6,2},{8,12},{10,14},{12,8},{14,10},{16,20},{18,... | collective-permute-start | bytes 1179656 | tf_op jit(solution)/shard_map/ppermute | solution.py:377
  16.5 17.7 %collective-permute-start.22 = (bf16[256,768]{1,0:T(8,128)(2,1)}, bf16[256,768]{1,0:T(8,128)(2,1)S(1)}, u32[]{:S(2)}, u32[]{:S(2)}) collective-permute-start(bf16[256,768]{1,0:T(8,128)(2,1)} %get-tuple-element.52), channel_id=1, source_target_pairs={{0,6},{2,4},{4,2},{6,0},{8,14},{10,12},{12,10},{14,8},{16,22},{18,... | collective-permute-start | bytes 1179656 | tf_op jit(solution)/shard_map/ppermute | solution.py:377
  25.1 9.1 %copy-start.40 = (bf16[256,768]{1,0:T(8,128)(2,1)}, bf16[256,768]{1,0:T(8,128)(2,1)S(1)}, u32[]{:S(2)}) copy-start(bf16[256,768]{1,0:T(8,128)(2,1)S(1)} %collective-permute-done.20.refs_1_) | copy-start | bytes 1179652
  37.9 135.7 %all-gather.7.cloned.1.call-start = ((), (), s32[]{:S(2)}) async-start(), calls=%async_computation.1 | async-start | bytes 3932160 | tf_op jit(solution)/shard_map/all_gather | solution.py:392
  38.7 9.3 %collective-permute-start = (f32[4,128,128]{2,1,0:T(8,128)S(1)}, f32[4,128,128]{2,1,0:T(8,128)S(1)}, u32[]{:S(2)}, u32[]{:S(2)}) collective-permute-start(f32[4,128,128]{2,1,0:T(8,128)S(1)} %copy-done.48), channel_id=1, source_target_pairs={{0,2},{2,0},{4,6},{6,4},{8,10},{10,8},{12,14},{14,12},{16,18},{18,... | collective-permute-start | bytes 786440 | tf_op jit(solution)/shard_map/ppermute | solution.py:377
  39.9 13.9 %collective-permute-start.1 = (f32[4,128,128]{2,1,0:T(8,128)S(1)}, f32[4,128,128]{2,1,0:T(8,128)S(1)}, u32[]{:S(2)}, u32[]{:S(2)}) collective-permute-start(f32[4,128,128]{2,1,0:T(8,128)S(1)} %copy-done.47), channel_id=1, source_target_pairs={{0,4},{2,6},{4,0},{6,2},{8,12},{10,14},{12,8},{14,10},{16,20},{18,... | collective-permute-start | bytes 786440 | tf_op jit(solution)/shard_map/ppermute | solution.py:377
  40.8 13.8 %collective-permute-start.2 = (f32[4,128,128]{2,1,0:T(8,128)S(1)}, f32[4,128,128]{2,1,0:T(8,128)S(1)}, u32[]{:S(2)}, u32[]{:S(2)}) collective-permute-start(f32[4,128,128]{2,1,0:T(8,128)S(1)} %copy-done.46), channel_id=1, source_target_pairs={{0,6},{2,4},{4,2},{6,0},{8,14},{10,12},{12,10},{14,8},{16,22},{18,... | collective-permute-start | bytes 786440 | tf_op jit(solution)/shard_map/ppermute | solution.py:377
  42.4 26.8 %collective-permute-start.5 = (bf16[256,768]{1,0:T(8,128)(2,1)S(1)}, bf16[256,768]{1,0:T(8,128)(2,1)S(1)}, u32[]{:S(2)}, u32[]{:S(2)}) collective-permute-start(bf16[256,768]{1,0:T(8,128)(2,1)S(1)} %get-tuple-element.85), channel_id=1, source_target_pairs={{0,4},{2,6},{4,0},{6,2},{8,12},{10,14},{12,8},{14,10},{16,20},{18,... | collective-permute-start | bytes 1179656 | tf_op jit(solution)/shard_map/ppermute | solution.py:377
  44.0 25.2 %collective-permute-start.4 = (bf16[256,768]{1,0:T(8,128)(2,1)S(1)}, bf16[256,768]{1,0:T(8,128)(2,1)S(1)}, u32[]{:S(2)}, u32[]{:S(2)}) collective-permute-start(bf16[256,768]{1,0:T(8,128)(2,1)S(1)} %get-tuple-element.86), channel_id=1, source_target_pairs={{0,2},{2,0},{4,6},{6,4},{8,10},{10,8},{12,14},{14,12},{16,18},{18,... | collective-permute-start | bytes 1179656 | tf_op jit(solution)/shard_map/ppermute | solution.py:377
  48.0 21.2 %collective-permute-start.6 = (bf16[256,768]{1,0:T(8,128)(2,1)S(1)}, bf16[256,768]{1,0:T(8,128)(2,1)S(1)}, u32[]{:S(2)}, u32[]{:S(2)}) collective-permute-start(bf16[256,768]{1,0:T(8,128)(2,1)S(1)} %get-tuple-element.87), channel_id=1, source_target_pairs={{0,6},{2,4},{4,2},{6,0},{8,14},{10,12},{12,10},{14,8},{16,22},{18,... | collective-permute-start | bytes 1179656 | tf_op jit(solution)/shard_map/ppermute | solution.py:377
  57.2 28.2 %copy-start.23 = (f32[4,128,128]{2,1,0:T(8,128)S(1)}, f32[4,128,128]{2,1,0:T(8,128)}, u32[]{:S(2)}) copy-start(f32[4,128,128]{2,1,0:T(8,128)} %get-tuple-element.44.refs_0_) | copy-start | bytes 786436
  57.2 28.2 %copy-start.25 = (f32[4,128,128]{2,1,0:T(8,128)S(1)}, f32[4,128,128]{2,1,0:T(8,128)}, u32[]{:S(2)}) copy-start(f32[4,128,128]{2,1,0:T(8,128)} %copy-done.24) | copy-start | bytes 786436
  57.3 28.2 %copy-start.27 = (f32[4,128,128]{2,1,0:T(8,128)S(1)}, f32[4,128,128]{2,1,0:T(8,128)}, u32[]{:S(2)}) copy-start(f32[4,128,128]{2,1,0:T(8,128)} %copy-done.26) | copy-start | bytes 786436
  57.3 28.2 %copy-start.29 = (f32[4,128,128]{2,1,0:T(8,128)S(1)}, f32[4,128,128]{2,1,0:T(8,128)}, u32[]{:S(2)}) copy-start(f32[4,128,128]{2,1,0:T(8,128)} %copy-done.28) | copy-start | bytes 786436
  58.3 8.7 %collective-permute-start.3 = (bf16[4,128,128]{2,1,0:T(8,128)(2,1)S(1)}, bf16[4,128,128]{2,1,0:T(8,128)(2,1)S(1)}, u32[]{:S(2)}, u32[]{:S(2)}) collective-permute-start(bf16[4,128,128]{2,1,0:T(8,128)(2,1)S(1)} %convert_element_type.24), channel_id=1, source_target_pairs={{0,8},{2,10},{4,12},{6,14},{8,16},{10,18},{12,20},{14,22},{16,24},... | collective-permute-start | bytes 393224 | tf_op jit(solution)/shard_map/ppermute | solution.py:387
  72.6 16.7 %copy-start.16 = (bf16[256,768]{1,0:T(8,128)(2,1)S(1)}, bf16[256,768]{1,0:T(8,128)(2,1)}, u32[]{:S(2)}) copy-start(bf16[256,768]{1,0:T(8,128)(2,1)} %copy-done.15) | copy-start | bytes 1179652
  72.6 16.7 %copy-start.18 = (bf16[256,768]{1,0:T(8,128)(2,1)S(1)}, bf16[256,768]{1,0:T(8,128)(2,1)}, u32[]{:S(2)}) copy-start(bf16[256,768]{1,0:T(8,128)(2,1)} %copy-done.17) | copy-start | bytes 1179652
  72.6 16.7 %copy-start.20 = (bf16[256,768]{1,0:T(8,128)(2,1)S(1)}, bf16[256,768]{1,0:T(8,128)(2,1)}, u32[]{:S(2)}) copy-start(bf16[256,768]{1,0:T(8,128)(2,1)} %copy-done.19) | copy-start | bytes 1179652
  73.7 11.8 %collective-permute-start.7 = (bf16[4,128,128]{2,1,0:T(8,128)(2,1)S(1)}, bf16[4,128,128]{2,1,0:T(8,128)(2,1)S(1)}, u32[]{:S(2)}, u32[]{:S(2)}) collective-permute-start(bf16[4,128,128]{2,1,0:T(8,128)(2,1)S(1)} %convert_element_type.26), channel_id=1, source_target_pairs={{0,16},{2,18},{4,20},{6,22},{8,24},{10,26},{12,28},{14,30},{1,17},... | collective-permute-start | bytes 393224 | tf_op jit(solution)/shard_map/ppermute | solution.py:387
  85.7 7.4 %collective-permute-start.10 = (f32[4,128,128]{2,1,0:T(8,128)S(1)}, f32[4,128,128]{2,1,0:T(8,128)S(1)}, u32[]{:S(2)}, u32[]{:S(2)}) collective-permute-start(f32[4,128,128]{2,1,0:T(8,128)S(1)} %get-tuple-element.93), channel_id=1, source_target_pairs={{0,6},{2,4},{4,2},{6,0},{8,14},{10,12},{12,10},{14,8},{16,22},{18,... | collective-permute-start | bytes 786440 | tf_op jit(solution)/shard_map/ppermute | solution.py:377
  88.4 7.5 %collective-permute-start.9 = (f32[4,128,128]{2,1,0:T(8,128)S(1)}, f32[4,128,128]{2,1,0:T(8,128)S(1)}, u32[]{:S(2)}, u32[]{:S(2)}) collective-permute-start(f32[4,128,128]{2,1,0:T(8,128)S(1)} %get-tuple-element.94), channel_id=1, source_target_pairs={{0,4},{2,6},{4,0},{6,2},{8,12},{10,14},{12,8},{14,10},{16,20},{18,... | collective-permute-start | bytes 786440 | tf_op jit(solution)/shard_map/ppermute | solution.py:377
  89.0 7.2 %collective-permute-start.8 = (f32[4,128,128]{2,1,0:T(8,128)S(1)}, f32[4,128,128]{2,1,0:T(8,128)S(1)}, u32[]{:S(2)}, u32[]{:S(2)}) collective-permute-start(f32[4,128,128]{2,1,0:T(8,128)S(1)} %get-tuple-element.95), channel_id=1, source_target_pairs={{0,2},{2,0},{4,6},{6,4},{8,10},{10,8},{12,14},{14,12},{16,18},{18,... | collective-permute-start | bytes 786440 | tf_op jit(solution)/shard_map/ppermute | solution.py:377
  110.5 28.9 %collective-permute-start.23 = (bf16[4,256,1024]{2,1,0:T(8,128)(2,1)}, bf16[4,256,1024]{2,1,0:T(8,128)(2,1)S(1)}, u32[]{:S(2)}, u32[]{:S(2)}) collective-permute-start(bf16[4,256,1024]{2,1,0:T(8,128)(2,1)} %shard_map.98), channel_id=1, source_target_pairs={{0,1},{1,0},{2,3},{3,2},{4,5},{5,4},{6,7},{7,6},{8,9},{9,8},{10,11... | collective-permute-start | bytes 6291464 | tf_op jit(solution)/shard_map/ppermute | solution.py:381
  110.5 25.6 %collective-permute-start.12 = (bf16[256,2048]{1,0:T(8,128)(2,1)S(1)}, bf16[256,2048]{1,0:T(8,128)(2,1)S(1)}, u32[]{:S(2)}, u32[]{:S(2)}) collective-permute-start(bf16[256,2048]{1,0:T(8,128)(2,1)S(1)} %copy-done.4), channel_id=1, source_target_pairs={{0,4},{2,6},{4,0},{6,2},{8,12},{10,14},{12,8},{14,10},{16,20},{18,... | collective-permute-start | bytes 3145736 | tf_op jit(solution)/shard_map/ppermute | solution.py:377
  112.0 25.7 %collective-permute-start.11 = (bf16[256,2048]{1,0:T(8,128)(2,1)S(1)}, bf16[256,2048]{1,0:T(8,128)(2,1)S(1)}, u32[]{:S(2)}, u32[]{:S(2)}) collective-permute-start(bf16[256,2048]{1,0:T(8,128)(2,1)S(1)} %copy-done.4), channel_id=1, source_target_pairs={{0,2},{2,0},{4,6},{6,4},{8,10},{10,8},{12,14},{14,12},{16,18},{18,... | collective-permute-start | bytes 3145736 | tf_op jit(solution)/shard_map/ppermute | solution.py:377
  136.2 14.9 %collective-permute-start.14 = (bf16[128,2048]{1,0:T(8,128)(2,1)S(1)}, bf16[128,2048]{1,0:T(8,128)(2,1)S(1)}, u32[]{:S(2)}, u32[]{:S(2)}) collective-permute-start(bf16[128,2048]{1,0:T(8,128)(2,1)S(1)} %slice.9), channel_id=1, source_target_pairs={{0,2},{2,0},{4,6},{6,4},{8,10},{10,8},{12,14},{14,12},{16,18},{18,... | collective-permute-start | bytes 1572872 | tf_op jit(solution)/shard_map/ppermute | solution.py:377
  138.6 15.1 %collective-permute-start.13 = (bf16[128,2048]{1,0:T(8,128)(2,1)}, bf16[128,2048]{1,0:T(8,128)(2,1)S(1)}, u32[]{:S(2)}, u32[]{:S(2)}) collective-permute-start(bf16[128,2048]{1,0:T(8,128)(2,1)} %slice.8), channel_id=1, source_target_pairs={{0,4},{2,6},{4,0},{6,2},{8,12},{10,14},{12,8},{14,10},{16,20},{18,... | collective-permute-start | bytes 1572872 | tf_op jit(solution)/shard_map/ppermute | solution.py:377
  146.5 27.2 %collective-permute-start.24 = (bf16[256,1024]{1,0:T(8,128)(2,1)}, bf16[256,1024]{1,0:T(8,128)(2,1)S(1)}, u32[]{:S(2)}, u32[]{:S(2)}) collective-permute-start(bf16[256,1024]{1,0:T(8,128)(2,1)} %get-tuple-element.55), channel_id=1, source_target_pairs={{0,2},{2,0},{4,6},{6,4},{8,10},{10,8},{12,14},{14,12},{16,18},{18,... | collective-permute-start | bytes 1572872 | tf_op jit(solution)/shard_map/ppermute | solution.py:377
  147.7 26.9 %collective-permute-start.25 = (bf16[256,1024]{1,0:T(8,128)(2,1)}, bf16[256,1024]{1,0:T(8,128)(2,1)S(1)}, u32[]{:S(2)}, u32[]{:S(2)}) collective-permute-start(bf16[256,1024]{1,0:T(8,128)(2,1)} %get-tuple-element.56), channel_id=1, source_target_pairs={{0,4},{2,6},{4,0},{6,2},{8,12},{10,14},{12,8},{14,10},{16,20},{18,... | collective-permute-start | bytes 1572872 | tf_op jit(solution)/shard_map/ppermute | solution.py:377
  148.3 26.3 %collective-permute-start.26 = (bf16[256,1024]{1,0:T(8,128)(2,1)}, bf16[256,1024]{1,0:T(8,128)(2,1)}, u32[]{:S(2)}, u32[]{:S(2)}) collective-permute-start(bf16[256,1024]{1,0:T(8,128)(2,1)} %get-tuple-element.57), channel_id=1, source_target_pairs={{0,6},{2,4},{4,2},{6,0},{8,14},{10,12},{12,10},{14,8},{16,22},{18,... | collective-permute-start | bytes 1572872 | tf_op jit(solution)/shard_map/ppermute | solution.py:377
  151.1 23.6 %copy-start.6 = (bf16[128,2048]{1,0:T(8,128)(2,1)}, bf16[128,2048]{1,0:T(8,128)(2,1)S(1)}, u32[]{:S(2)}) copy-start(bf16[128,2048]{1,0:T(8,128)(2,1)S(1)} %collective-permute-done.14.refs_4_) | copy-start | bytes 1572868
  153.7 20.9 %copy-start.7 = (bf16[128,2048]{1,0:T(8,128)(2,1)}, bf16[128,2048]{1,0:T(8,128)(2,1)S(1)}, u32[]{:S(2)}) copy-start(bf16[128,2048]{1,0:T(8,128)(2,1)S(1)} %collective-permute-done.13.refs_3_) | copy-start | bytes 1572868
  180.9 9.6 %collective-permute-start.27 = (bf16[4,256,1024]{2,1,0:T(8,128)(2,1)}, bf16[4,256,1024]{2,1,0:T(8,128)(2,1)S(1)}, u32[]{:S(2)}, u32[]{:S(2)}) collective-permute-start(bf16[4,256,1024]{2,1,0:T(8,128)(2,1)} %shard_map.100.refs_0_), channel_id=1, source_target_pairs={{0,1},{1,0},{2,3},{3,2},{4,5},{5,4},{6,7},{7,6},{8,9},{9,8},{10,11... | collective-permute-start | bytes 6291464 | tf_op jit(solution)/shard_map/ppermute | solution.py:381
  181.0 16.5 %collective-permute-start.15 = (bf16[256,2048]{1,0:T(8,128)(2,1)S(1)}, bf16[256,2048]{1,0:T(8,128)(2,1)S(1)}, u32[]{:S(2)}, u32[]{:S(2)}) collective-permute-start(bf16[256,2048]{1,0:T(8,128)(2,1)S(1)} %copy-done.4), channel_id=1, source_target_pairs={{0,1},{1,0},{2,3},{3,2},{4,5},{5,4},{6,7},{7,6},{8,9},{9,8},{10,11... | collective-permute-start | bytes 3145736 | tf_op jit(solution)/shard_map/ppermute | solution.py:381
  181.5 18.3 %collective-permute-start.17 = (bf16[256,2048]{1,0:T(8,128)(2,1)S(1)}, bf16[256,2048]{1,0:T(8,128)(2,1)S(1)}, u32[]{:S(2)}, u32[]{:S(2)}) collective-permute-start(bf16[256,2048]{1,0:T(8,128)(2,1)S(1)} %copy-done.1), channel_id=1, source_target_pairs={{0,1},{1,0},{2,3},{3,2},{4,5},{5,4},{6,7},{7,6},{8,9},{9,8},{10,11... | collective-permute-start | bytes 3145736 | tf_op jit(solution)/shard_map/ppermute | solution.py:381
  181.5 16.9 %collective-permute-start.19 = (bf16[128,2048]{1,0:T(8,128)(2,1)}, bf16[128,2048]{1,0:T(8,128)(2,1)}, u32[]{:S(2)}, u32[]{:S(2)}) collective-permute-start(bf16[128,2048]{1,0:T(8,128)(2,1)} %copy-done.6), channel_id=1, source_target_pairs={{0,1},{1,0},{2,3},{3,2},{4,5},{5,4},{6,7},{7,6},{8,9},{9,8},{10,11... | collective-permute-start | bytes 1572872 | tf_op jit(solution)/shard_map/ppermute | solution.py:381
  182.0 25.9 %collective-permute-start.16 = (bf16[256,2048]{1,0:T(8,128)(2,1)S(1)}, bf16[256,2048]{1,0:T(8,128)(2,1)}, u32[]{:S(2)}, u32[]{:S(2)}) collective-permute-start(bf16[256,2048]{1,0:T(8,128)(2,1)S(1)} %copy-done.3), channel_id=1, source_target_pairs={{0,1},{1,0},{2,3},{3,2},{4,5},{5,4},{6,7},{7,6},{8,9},{9,8},{10,11... | collective-permute-start | bytes 3145736 | tf_op jit(solution)/shard_map/ppermute | solution.py:381
  182.0 8.5 %copy-start.8 = (bf16[128,2048]{1,0:T(8,128)(2,1)S(1)}, bf16[128,2048]{1,0:T(8,128)(2,1)}, u32[]{:S(2)}) copy-start(bf16[128,2048]{1,0:T(8,128)(2,1)} %copy-done.7) | copy-start | bytes 1572868
  190.5 17.4 %collective-permute-start.18 = (bf16[128,2048]{1,0:T(8,128)(2,1)S(1)}, bf16[128,2048]{1,0:T(8,128)(2,1)}, u32[]{:S(2)}, u32[]{:S(2)}) collective-permute-start(bf16[128,2048]{1,0:T(8,128)(2,1)S(1)} %copy-done.8), channel_id=1, source_target_pairs={{0,1},{1,0},{2,3},{3,2},{4,5},{5,4},{6,7},{7,6},{8,9},{9,8},{10,11... | collective-permute-start | bytes 1572872 | tf_op jit(solution)/shard_map/ppermute | solution.py:381
  197.5 10.4 %copy-start.21 = (bf16[256,2048]{1,0:T(8,128)(2,1)}, bf16[256,2048]{1,0:T(8,128)(2,1)S(1)}, u32[]{:S(2)}) copy-start(bf16[256,2048]{1,0:T(8,128)(2,1)S(1)} %collective-permute-done.15.refs_5_) | copy-start | bytes 3145732
  197.5 26.4 %collective-permute-start.32 = (bf16[256,1024]{1,0:T(8,128)(2,1)}, bf16[256,1024]{1,0:T(8,128)(2,1)S(1)}, u32[]{:S(2)}, u32[]{:S(2)}) collective-permute-start(bf16[256,1024]{1,0:T(8,128)(2,1)} %get-tuple-element.67), channel_id=1, source_target_pairs={{0,4},{2,6},{4,0},{6,2},{8,12},{10,14},{12,8},{14,10},{16,20},{18,... | collective-permute-start | bytes 1572872 | tf_op jit(solution)/shard_map/ppermute | solution.py:377
  198.4 25.5 %collective-permute-start.33 = (bf16[256,1024]{1,0:T(8,128)(2,1)}, bf16[256,1024]{1,0:T(8,128)(2,1)S(1)}, u32[]{:S(2)}, u32[]{:S(2)}) collective-permute-start(bf16[256,1024]{1,0:T(8,128)(2,1)} %get-tuple-element.68), channel_id=1, source_target_pairs={{0,6},{2,4},{4,2},{6,0},{8,14},{10,12},{12,10},{14,8},{16,22},{18,... | collective-permute-start | bytes 1572872 | tf_op jit(solution)/shard_map/ppermute | solution.py:377
  199.7 24.5 %collective-permute-start.31 = (bf16[256,1024]{1,0:T(8,128)(2,1)}, bf16[256,1024]{1,0:T(8,128)(2,1)S(1)}, u32[]{:S(2)}, u32[]{:S(2)}) collective-permute-start(bf16[256,1024]{1,0:T(8,128)(2,1)} %get-tuple-element.61.refs_12_), channel_id=1, source_target_pairs={{0,2},{2,0},{4,6},{6,4},{8,10},{10,8},{12,14},{14,12},{16,18},{18,... | collective-permute-start | bytes 1572872 | tf_op jit(solution)/shard_map/ppermute | solution.py:377
  232.8 9.5 %collective-permute-start.34 = (f32[4,128,128]{2,1,0:T(8,128)}, f32[4,128,128]{2,1,0:T(8,128)S(1)}, u32[]{:S(2)}, u32[]{:S(2)}) collective-permute-start(f32[4,128,128]{2,1,0:T(8,128)} %get-tuple-element.79), channel_id=1, source_target_pairs={{0,2},{2,0},{4,6},{6,4},{8,10},{10,8},{12,14},{14,12},{16,18},{18,... | collective-permute-start | bytes 786440 | tf_op jit(solution)/shard_map/ppermute | solution.py:377
  233.5 13.1 %collective-permute-start.35 = (f32[4,128,128]{2,1,0:T(8,128)}, f32[4,128,128]{2,1,0:T(8,128)S(1)}, u32[]{:S(2)}, u32[]{:S(2)}) collective-permute-start(f32[4,128,128]{2,1,0:T(8,128)} %get-tuple-element.80), channel_id=1, source_target_pairs={{0,4},{2,6},{4,0},{6,2},{8,12},{10,14},{12,8},{14,10},{16,20},{18,... | collective-permute-start | bytes 786440 | tf_op jit(solution)/shard_map/ppermute | solution.py:377
  235.0 11.6 %collective-permute-start.36 = (f32[4,128,128]{2,1,0:T(8,128)}, f32[4,128,128]{2,1,0:T(8,128)S(1)}, u32[]{:S(2)}, u32[]{:S(2)}) collective-permute-start(f32[4,128,128]{2,1,0:T(8,128)} %get-tuple-element.81), channel_id=1, source_target_pairs={{0,6},{2,4},{4,2},{6,0},{8,14},{10,12},{12,10},{14,8},{16,22},{18,... | collective-permute-start | bytes 786440 | tf_op jit(solution)/shard_map/ppermute | solution.py:377
  250.3 11.4 %collective-permute-start.37 = (bf16[4,128,128]{2,1,0:T(8,128)(2,1)S(1)}, bf16[4,128,128]{2,1,0:T(8,128)(2,1)S(1)}, u32[]{:S(2)}, u32[]{:S(2)}) collective-permute-start(bf16[4,128,128]{2,1,0:T(8,128)(2,1)S(1)} %convert_element_type.28), channel_id=1, source_target_pairs={{8,0},{10,2},{12,4},{14,6},{16,8},{18,10},{20,12},{22,14},{24,16},... | collective-permute-start | bytes 393224 | tf_op jit(solution)/shard_map/ppermute | solution.py:387
  258.5 8.2 %copy-start.45 = (bf16[256,768]{1,0:T(8,128)(2,1)S(1)}, bf16[256,768]{1,0:T(8,128)(2,1)}, u32[]{:S(2)}) copy-start(bf16[256,768]{1,0:T(8,128)(2,1)} %get-tuple-element.63) | copy-start | bytes 1179652
  258.5 10.0 %copy-start.44 = (bf16[256,768]{1,0:T(8,128)(2,1)S(1)}, bf16[256,768]{1,0:T(8,128)(2,1)}, u32[]{:S(2)}) copy-start(bf16[256,768]{1,0:T(8,128)(2,1)} %get-tuple-element.64) | copy-start | bytes 1179652
  258.5 10.7 %copy-start.43 = (bf16[256,768]{1,0:T(8,128)(2,1)S(1)}, bf16[256,768]{1,0:T(8,128)(2,1)}, u32[]{:S(2)}) copy-start(bf16[256,768]{1,0:T(8,128)(2,1)} %get-tuple-element.65) | copy-start | bytes 1179652
  264.3 12.1 %copy-start.30 = (f32[4,128,128]{2,1,0:T(8,128)S(1)}, f32[4,128,128]{2,1,0:T(8,128)}, u32[]{:S(2)}) copy-start(f32[4,128,128]{2,1,0:T(8,128)} %get-tuple-element.78.refs_0_) | copy-start | bytes 786436
  264.3 12.1 %copy-start.32 = (f32[4,128,128]{2,1,0:T(8,128)S(1)}, f32[4,128,128]{2,1,0:T(8,128)}, u32[]{:S(2)}) copy-start(f32[4,128,128]{2,1,0:T(8,128)} %copy-done.31) | copy-start | bytes 786436
  264.3 12.1 %copy-start.34 = (f32[4,128,128]{2,1,0:T(8,128)S(1)}, f32[4,128,128]{2,1,0:T(8,128)}, u32[]{:S(2)}) copy-start(f32[4,128,128]{2,1,0:T(8,128)} %copy-done.33) | copy-start | bytes 786436
  264.3 12.1 %copy-start.36 = (f32[4,128,128]{2,1,0:T(8,128)S(1)}, f32[4,128,128]{2,1,0:T(8,128)}, u32[]{:S(2)}) copy-start(f32[4,128,128]{2,1,0:T(8,128)} %copy-done.35) | copy-start | bytes 786436
  265.4 11.0 %collective-permute-start.38 = (bf16[4,128,128]{2,1,0:T(8,128)(2,1)S(1)}, bf16[4,128,128]{2,1,0:T(8,128)(2,1)S(1)}, u32[]{:S(2)}, u32[]{:S(2)}) collective-permute-start(bf16[4,128,128]{2,1,0:T(8,128)(2,1)S(1)} %convert_element_type.30), channel_id=1, source_target_pairs={{16,0},{18,2},{20,4},{22,6},{24,8},{26,10},{28,12},{30,14},{17,1},... | collective-permute-start | bytes 393224 | tf_op jit(solution)/shard_map/ppermute | solution.py:387
  266.7 13.2 %collective-permute-start.28 = (bf16[256,768]{1,0:T(8,128)(2,1)S(1)}, bf16[256,768]{1,0:T(8,128)(2,1)S(1)}, u32[]{:S(2)}, u32[]{:S(2)}) collective-permute-start(bf16[256,768]{1,0:T(8,128)(2,1)S(1)} %copy-done.45), channel_id=1, source_target_pairs={{0,2},{2,0},{4,6},{6,4},{8,10},{10,8},{12,14},{14,12},{16,18},{18,... | collective-permute-start | bytes 1179656 | tf_op jit(solution)/shard_map/ppermute | solution.py:377
  268.4 22.1 %collective-permute-start.29 = (bf16[256,768]{1,0:T(8,128)(2,1)S(1)}, bf16[256,768]{1,0:T(8,128)(2,1)S(1)}, u32[]{:S(2)}, u32[]{:S(2)}) collective-permute-start(bf16[256,768]{1,0:T(8,128)(2,1)S(1)} %copy-done.44), channel_id=1, source_target_pairs={{0,4},{2,6},{4,0},{6,2},{8,12},{10,14},{12,8},{14,10},{16,20},{18,... | collective-permute-start | bytes 1179656 | tf_op jit(solution)/shard_map/ppermute | solution.py:377
  269.1 21.5 %collective-permute-start.30 = (bf16[256,768]{1,0:T(8,128)(2,1)S(1)}, bf16[256,768]{1,0:T(8,128)(2,1)S(1)}, u32[]{:S(2)}, u32[]{:S(2)}) collective-permute-start(bf16[256,768]{1,0:T(8,128)(2,1)S(1)} %copy-done.43), channel_id=1, source_target_pairs={{0,6},{2,4},{4,2},{6,0},{8,14},{10,12},{12,10},{14,8},{16,22},{18,... | collective-permute-start | bytes 1179656 | tf_op jit(solution)/shard_map/ppermute | solution.py:377
  276.7 16.3 %collective-permute-start.41 = (f32[4,128,128]{2,1,0:T(8,128)S(1)}, f32[4,128,128]{2,1,0:T(8,128)S(1)}, u32[]{:S(2)}, u32[]{:S(2)}) collective-permute-start(f32[4,128,128]{2,1,0:T(8,128)S(1)} %get-tuple-element.89), channel_id=1, source_target_pairs={{0,6},{2,4},{4,2},{6,0},{8,14},{10,12},{12,10},{14,8},{16,22},{18,... | collective-permute-start | bytes 786440 | tf_op jit(solution)/shard_map/ppermute | solution.py:377
  278.5 17.3 %collective-permute-start.40 = (f32[4,128,128]{2,1,0:T(8,128)S(1)}, f32[4,128,128]{2,1,0:T(8,128)S(1)}, u32[]{:S(2)}, u32[]{:S(2)}) collective-permute-start(f32[4,128,128]{2,1,0:T(8,128)S(1)} %get-tuple-element.90), channel_id=1, source_target_pairs={{0,4},{2,6},{4,0},{6,2},{8,12},{10,14},{12,8},{14,10},{16,20},{18,... | collective-permute-start | bytes 786440 | tf_op jit(solution)/shard_map/ppermute | solution.py:377
  279.9 16.0 %collective-permute-start.39 = (f32[4,128,128]{2,1,0:T(8,128)S(1)}, f32[4,128,128]{2,1,0:T(8,128)S(1)}, u32[]{:S(2)}, u32[]{:S(2)}) collective-permute-start(f32[4,128,128]{2,1,0:T(8,128)S(1)} %get-tuple-element.91), channel_id=1, source_target_pairs={{0,2},{2,0},{4,6},{6,4},{8,10},{10,8},{12,14},{14,12},{16,18},{18,... | collective-permute-start | bytes 786440 | tf_op jit(solution)/shard_map/ppermute | solution.py:377
  290.7 14.6 %copy-start.12 = (bf16[256,3072]{1,0:T(8,128)(2,1)}, bf16[256,3072]{1,0:T(8,128)(2,1)S(1)}, u32[]{:S(2)}) copy-start(bf16[256,3072]{1,0:T(8,128)(2,1)S(1)} %constant_dynamic-update-slice_fusion) | copy-start | bytes 4718596
  (29 other events, 85.8 us)
Sparse Core Ops, SparseCore 0:
  38.0 65.4 all-gather.4
  105.1 68.4 all-gather.6

commit v3 on v2

--- a/solution.py
+++ b/solution.py
@@ -116,29 +116,41 @@
     return slice(h * DH, (h + 1) * DH)
 
 
-def prepare_kernel(pos, k_ref, v_ref, w_ref, *outs):
-    states, pieces = outs[:PLANE], outs[PLANE:]
-    width = pieces[0].shape[1]
+def pieces_kernel(pos, w_ref, *outs):
+    width = outs[0].shape[1]
     for n in range(PLANE):
-        j = pos[0] ^ n
-        pieces[n][...] = w_ref[:, pl.ds(pl.multiple_of(j * width, DH), width)]
+        outs[n][...] = w_ref[:, pl.ds(pl.multiple_of((pos[0] ^ n) * width, DH), width)]
+
+
+def states_kernel(pos, k_ref, v_ref, *refs):
+    for n in range(PLANE):
         for h in range(QUAD):
-            cols = pl.ds(pl.multiple_of((j * QUAD + h) * DH, DH), DH)
-            states[n][h] = mm(k_ref[:, cols], v_ref[:, cols], TN)
+            cols = pl.ds(pl.multiple_of(((pos[0] ^ n) * QUAD + h) * DH, DH), DH)
+            refs[n - PLANE][h] = mm(k_ref[:, cols], v_ref[:, cols], TN)
 
 
 def prepare(pos, keys, values, out_weight):
     whole = pl.BlockSpec(memory_space=pltpu.VMEM)
+    place = pl.BlockSpec(memory_space=pltpu.SMEM)
     piece = (out_weight.shape[0], out_weight.shape[1] // PLANE)
-    out = pl.pallas_call(
-        prepare_kernel,
-        in_specs=[pl.BlockSpec(memory_space=pltpu.SMEM)] + [whole] * 3,
-        out_specs=[whole] * (2 * PLANE),
-        out_shape=[jax.ShapeDtypeStruct((QUAD, DH, DH), F32)] * PLANE + [jax.ShapeDtypeStruct(piece, BF16)] * PLANE,
-        compiler_params=pltpu.CompilerParams(vmem_limit_bytes=56 * MIB),
-        cost_estimate=LIGHT,
-    )(pos, keys, values, out_weight)
-    return out[:PLANE], out[PLANE:]
+    params = pltpu.CompilerParams(vmem_limit_bytes=56 * MIB)
+    pieces = pl.pallas_call(
+        pieces_kernel,
+        in_specs=[place, whole],
+        out_specs=[whole] * PLANE,
+        out_shape=[jax.ShapeDtypeStruct(piece, BF16)] * PLANE,
+        compiler_params=params,
+        cost_estimate=LIGHT,
+    )(pos, out_weight)
+    states = pl.pallas_call(
+        states_kernel,
+        in_specs=[place, whole, whole, pl.BlockSpec(memory_space=pl.ANY)],
+        out_specs=[whole] * PLANE,
+        out_shape=[jax.ShapeDtypeStruct((QUAD, DH, DH), F32)] * PLANE,
+        compiler_params=params,
+        cost_estimate=LIGHT,
+    )(pos, keys, values, pieces[0])
+    return states, pieces
 
 
 def forward_kernel(pos, q_ref, k_ref, v_ref, gain_ref, prefix_ref, heads_ref, attn_ref):
@@ -249,13 +261,13 @@
 def others_kernel(pos, cot_ref, w_ref, *refs):
     out_ref = refs[-1]
     for t in range(PLANE):
-        out_ref[t] = mm(cot_ref[t], w_ref[0], NT).astype(BF16)
+        out_ref[t] = mm(cot_ref[t], w_ref[0], NT)
 
 
 def mine_kernel(pos, cot_ref, w_ref, other_ref, *refs):
     own_ref, sent = refs[-4], refs[-3:]
     for t in range(PLANE):
-        total = mm(cot_ref[t], w_ref[0], NT) + other_ref[t].astype(F32)
+        total = mm(cot_ref[t], w_ref[0], NT) + other_ref[t]
         if t == 0:
             own_ref[...] = total
         else:
@@ -275,7 +287,7 @@
 
     in_specs = [pl.BlockSpec(cot.shape, lambda i, pos: (0, 0, 0)), pl.BlockSpec((1, rows, width), plane_of)]
     if taken is None:
-        kernel, out_specs, out_shape, given = others_kernel, block, jax.ShapeDtypeStruct(whole, BF16), ()
+        kernel, out_specs, out_shape, given = others_kernel, block, jax.ShapeDtypeStruct(whole, F32), ()
     else:
         kernel, given = mine_kernel, (taken,)
         in_specs.append(block)
@@ -294,7 +306,7 @@
 
 
 def place_kernel(pos, *refs):
-    pieces, outs = refs[:PLANE], refs[PLANE:]
+    pieces, outs = refs[:PLANE], refs[-len(CHUNKS) :]
     rows = pieces[0].shape[0]
     for k, piece in enumerate(pieces):
         j = pos[0] ^ k
@@ -307,17 +319,18 @@
             pl.when((j >= chunk[0]) & (j <= chunk[-1]))(store)
 
 
-def place_chunks(pos, pieces):
+def place_chunks(pos, pieces, after):
     rows, width = pieces[0].shape
     whole = pl.BlockSpec(memory_space=pltpu.VMEM)
     return pl.pallas_call(
         place_kernel,
-        in_specs=[pl.BlockSpec(memory_space=pltpu.SMEM)] + [whole] * len(pieces),
+        in_specs=[pl.BlockSpec(memory_space=pltpu.SMEM)] + [whole] * len(pieces)
+        + [pl.BlockSpec(memory_space=pl.ANY)] * len(after),
         out_specs=[whole] * len(CHUNKS),
         out_shape=[jax.ShapeDtypeStruct((len(chunk) * rows, width), BF16) for chunk in CHUNKS],
         compiler_params=pltpu.CompilerParams(vmem_limit_bytes=56 * MIB),
         cost_estimate=LIGHT,
-    )(pos, *pieces)
+    )(pos, *pieces, *after)
 
 
 def mixed_kernel(pos, *refs):
@@ -405,7 +418,7 @@
         functools.partial(add_kernel, len(values)),
         in_specs=[whole] * len(values) + [pl.BlockSpec(memory_space=pl.ANY)] * len(after),
         out_specs=whole,
-        out_shape=jax.ShapeDtypeStruct(values[0].shape, values[0].dtype),
+        out_shape=jax.ShapeDtypeStruct(values[0].shape, F32),
         compiler_params=pltpu.CompilerParams(vmem_limit_bytes=56 * MIB),
         cost_estimate=LIGHT,
     )(*values, *after)
@@ -442,19 +455,33 @@
 
 def plane_sums(total, backward, after=()):
     sign = -1 if backward else 1
-    near = z_shift(total.astype(BF16), sign).astype(F32)
-    return near + z_shift(add_after([total, near], after).astype(BF16), 2 * sign).astype(F32)
-
-
-def plane_returns(parts, entering, p, backward):
-    given = []
+    near = z_shift(total, sign)
+    return near, z_shift(add_after([total, near], after), 2 * sign)
+
+
+def returns_kernel(backward, pos, near_ref, far_ref, *refs):
+    parts, outs = refs[:PLANE], refs[PLANE:]
+    entering = near_ref[...] + far_ref[...]
     for t in range(PLANE):
         value = entering
         for k in range(PLANE):
             if k != t:
-                ahead = (p ^ k) > (p ^ t) if backward else (p ^ k) < (p ^ t)
-                value = value + jnp.where(ahead, parts[k], 0.0)
-        given.append(value)
+                here, there = pos[0] ^ k, pos[0] ^ t
+                ahead = here > there if backward else here < there
+                value = value + jnp.where(ahead, parts[k][...], 0.0)
+        outs[t][...] = value
+
+
+def plane_returns(pos, parts, sums, backward):
+    whole = pl.BlockSpec(memory_space=pltpu.VMEM)
+    given = pl.pallas_call(
+        functools.partial(returns_kernel, backward),
+        in_specs=[pl.BlockSpec(memory_space=pltpu.SMEM)] + [whole] * (2 + PLANE),
+        out_specs=[whole] * PLANE,
+        out_shape=[jax.ShapeDtypeStruct(parts[0].shape, F32)] * PLANE,
+        compiler_params=pltpu.CompilerParams(vmem_limit_bytes=56 * MIB),
+        cost_estimate=LIGHT,
+    )(pos, *sums, *parts)
     return jnp.concatenate(plane_swaps(given), axis=0)
 
 
@@ -468,9 +495,9 @@
     states, pieces = prepare(pos, keys, values, out_weight)
     parts = plane_swaps(states)
     total = add_after(parts, ())
-    weights = [z_gather(chunk) for chunk in place_chunks(pos, plane_swaps(pieces))]
+    weights = [z_gather(chunk) for chunk in place_chunks(pos, plane_swaps(pieces), (states[0],))]
     cot_pieces = plane_swaps([lax.dynamic_slice_in_dim(cotangent, (p ^ k) * wide, wide, 1) for k in range(PLANE)])
-    prefix = plane_returns(parts, plane_sums(total, False, cot_pieces[1:]), p, False)
+    prefix = plane_returns(pos, parts, plane_sums(total, False, cot_pieces[1:]), False)
     cot = jnp.stack(cot_pieces)
     gain_row = gain.reshape(1, columns)
     heads_out, attn = by_heads(
@@ -526,7 +553,7 @@
         )
     grad_q, inner_k, inner_v = inners
     parts, total = plane_parts(owns, pos, ())
-    later = plane_returns(parts, plane_sums(total, True, (grad_q,)), p, True)
+    later = plane_returns(pos, parts, plane_sums(total, True, (grad_q,)), True)
     grad_k, grad_v = by_heads(
         outer_kernel,
         pos,

time: 317 us -> 343 us (1.082); the launches traced: 312 us -> 342 us
  waiting for transfers between devices: 130 us -> 154 us
  Pallas kernels: 96 us -> 104 us
  other arithmetic: 10.2 us -> 2.97 us
  starting transfers between devices: 51.6 us -> 55.6 us
    all_gather x2, waiting for transfers between devices: 20 us -> 37.1 us  [z_gather(): return lax.all_gather(value, 'ctx', axis_index_groups=lines)]
    pallas_call x1 -> x4, Pallas kernels: 4.18 us -> 10.7 us  [the longest x2 4.89 us: plane_returns(): pl.pallas_call(functools.partial(returns_kernel, backward), in_specs=[pl....]
    ppermute x4, starting transfers between devices: 12.6 us -> 18.5 us  [z_shift(): return lax.ppermute(value, 'ctx', pairs)]
    convert_element_type x6 -> x0, other arithmetic: 5.6 us -> none  [the longest x4 3.47 us: plane_sums(): near = z_shift(total.astype(BF16), sign).astype(F32)]
    unnamed x98 -> x103, local copies, waits for them, and re-layouts: 8.34 us -> 9.96 us
  transfers between devices with their start and end apart: 44 -> 44, of which waited for: 25 -> 23; matrix products, arithmetic and copies ran while one was open for 2% -> 1% of each run, Pallas kernels for 20% -> 20%
where the time goes in v3:
time: 343 us; the launch traced here: 342 us
  waiting for transfers between devices  154 us (45%)
  Pallas kernels  104 us (30%)
  starting transfers between devices  55.6 us (16%)
  between operations  14.5 us (4%)
  local copies, waits for them, and re-layouts  10.6 us (3%)
    ppermute x31, waiting for transfers between devices, plane_swap(): lax.ppermute(value, 'ctx', [(i, i ^ k) for i in range(PLANE * PLANES)])  88.2 us
    pallas_call x6, Pallas kernels, by_heads(): pl.pallas_call(kernel, grid_spec=pltpu.PrefetchScalarGridSpec(num_scalar_...  41 us
    all_gather x2, waiting for transfers between devices, z_gather(): return lax.all_gather(value, 'ctx', axis_index_groups=lines)  37.1 us
    ppermute x31, starting transfers between devices, plane_swap(): lax.ppermute(value, 'ctx', [(i, i ^ k) for i in range(PLANE * PLANES)])  35.8 us
    pallas_call x4, Pallas kernels, partial_grads(): pl.pallas_call(kernel, grid_spec=pltpu.PrefetchScalarGridSpec(num_scalar_...  23.8 us
    ppermute x4, waiting for transfers between devices, z_shift(): return lax.ppermute(value, 'ctx', pairs)  23 us
    ppermute x4, starting transfers between devices, z_shift(): return lax.ppermute(value, 'ctx', pairs)  18.5 us
    pallas_call x1, Pallas kernels, mixed_blocks(): pl.pallas_call(mixed_kernel, in_specs=[pl.BlockSpec(memory_space=pltpu.SM...  15.9 us
  transfers between devices with their start and end apart: 44, of which 23 were waited for; matrix products, arithmetic and copies ran while one was open for 1% of the time, Pallas kernels for 20%

profile of v3, /device:TPU:0, one launch (start us, length us, event | category | flops | bytes accessed | tf_op | source)
XLA Modules:
  0.0 341.8 jit_solution(798327584171620730)
XLA Ops:
  7.8 2.7 shard_map.93
  10.4 2.9 collective-permute-start.20
  13.4 1.5 collective-permute-start.21
  14.9 3.2 shard_map.94
  18.1 5.4 %collective-permute-done.20.refs_1_ = bf16[256,768]{1,0:T(8,128)(2,1)S(1)} collective-permute-done((bf16[256,768]{1,0:T(8,128)(2,1)}, bf16[256,768]{1,0:T(8,128)(2,1)S(1)}, u32[]{:S(2)}, u32[]{:S(2)}) %collective-permute-start.20) | collective-permute-done | bytes 393248 | tf_op jit(solution)/shard_map/ppermute | solution.py:390
  23.5 9.1 %collective-permute-done.21.refs_2_ = bf16[256,768]{1,0:T(8,128)(2,1)S(1)} collective-permute-done((bf16[256,768]{1,0:T(8,128)(2,1)}, bf16[256,768]{1,0:T(8,128)(2,1)S(1)}, u32[]{:S(2)}, u32[]{:S(2)}) %collective-permute-start.21) | collective-permute-done | bytes 393248 | tf_op jit(solution)/shard_map/ppermute | solution.py:390
  33.5 2.7 shard_map.99
  36.2 1.2 collective-permute-start
  38.4 1.4 collective-permute-start.2
  42.1 3.5 %collective-permute-done.refs_1_ = f32[4,128,128]{2,1,0:T(8,128)S(1)} collective-permute-done((f32[4,128,128]{2,1,0:T(8,128)S(1)}, f32[4,128,128]{2,1,0:T(8,128)S(1)}, u32[]{:S(2)}, u32[]{:S(2)}) %collective-permute-start) | collective-permute-done | bytes 262176 | tf_op jit(solution)/shard_map/ppermute | solution.py:390
  45.5 1.5 collective-permute-start.6
  47.0 4.3 %collective-permute-done.1.refs_2_ = f32[4,128,128]{2,1,0:T(8,128)S(1)} collective-permute-done((f32[4,128,128]{2,1,0:T(8,128)S(1)}, f32[4,128,128]{2,1,0:T(8,128)S(1)}, u32[]{:S(2)}, u32[]{:S(2)}) %collective-permute-start.1) | collective-permute-done | bytes 262176 | tf_op jit(solution)/shard_map/ppermute | solution.py:390
  52.8 1.9 shard_map.95.refs_0_
  54.8 3.5 %collective-permute-start.3 = (f32[4,128,128]{2,1,0:T(8,128)}, f32[4,128,128]{2,1,0:T(8,128)S(1)}, u32[]{:S(2)}, u32[]{:S(2)}) collective-permute-start(f32[4,128,128]{2,1,0:T(8,128)} %shard_map.95.refs_0_), channel_id=1, source_target_pairs={{0,8},{2,10},{4,12},{6,14},{8,16},{10,18},{12,20},{14,22},{16,24},... | collective-permute-start | bytes 786440 | tf_op jit(solution)/shard_map/ppermute | solution.py:400
  58.3 1.3 collective-permute-done.4.refs_2_
  59.6 7.2 %collective-permute-done.5.refs_3_ = bf16[256,768]{1,0:T(8,128)(2,1)S(1)} collective-permute-done((bf16[256,768]{1,0:T(8,128)(2,1)S(1)}, bf16[256,768]{1,0:T(8,128)(2,1)S(1)}, u32[]{:S(2)}, u32[]{:S(2)}) %collective-permute-start.5) | collective-permute-done | bytes 393248 | tf_op jit(solution)/shard_map/ppermute | solution.py:390
  66.8 1.7 collective-permute-done.3.refs_1_.near_ref
  69.2 1.8 shard_map.96
  71.0 12.5 %collective-permute-start.7 = (f32[4,128,128]{2,1,0:T(8,128)}, f32[4,128,128]{2,1,0:T(8,128)S(1)}, u32[]{:S(2)}, u32[]{:S(2)}) collective-permute-start(f32[4,128,128]{2,1,0:T(8,128)} %shard_map.96), channel_id=1, source_target_pairs={{0,16},{2,18},{4,20},{6,22},{8,24},{10,26},{12,28},{14,30},{1,17},... | collective-permute-start | bytes 786440 | tf_op jit(solution)/shard_map/ppermute | solution.py:400
  83.5 9.8 %collective-permute-done.7.far_ref = f32[4,128,128]{2,1,0:T(8,128)S(1)} collective-permute-done((f32[4,128,128]{2,1,0:T(8,128)}, f32[4,128,128]{2,1,0:T(8,128)S(1)}, u32[]{:S(2)}, u32[]{:S(2)}) %collective-permute-start.7) | collective-permute-done | bytes 262176 | tf_op jit(solution)/shard_map/ppermute | solution.py:400
  94.0 2.5 shard_map.97
  96.4 1.7 collective-permute-start.8
  98.2 1.6 collective-permute-start.9
  99.8 1.3 pad_maximum_fusion.cot_ref
  101.3 1.7 collective-permute-done.8
  103.0 3.8 %collective-permute-done.9 = f32[4,128,128]{2,1,0:T(8,128)S(1)} collective-permute-done((f32[4,128,128]{2,1,0:T(8,128)}, f32[4,128,128]{2,1,0:T(8,128)S(1)}, u32[]{:S(2)}, u32[]{:S(2)}) %collective-permute-start.9) | collective-permute-done | bytes 262176 | tf_op jit(solution)/shard_map/ppermute | solution.py:390
  106.8 1.6 collective-permute-done.10
  109.4 7.8 %shard_map.98 = (bf16[256,2048]{1,0:T(8,128)(2,1)}, f32[256,2048]{1,0:T(8,128)}) custom-call(s32[3]{0:T(128)} %pad_add_fusion.pos, bf16[256,2048]{1,0:T(8,128)(2,1)} %q_ref.9, bf16[256,2048]{1,0:T(8,128)(2,1)} %k_ref.9, bf16[256,2048]{1,0:T(8,128)(2,1)} %v_ref.9, f32[1,2048]{1,0:T(1,128)} %bitcast.20, f32[16,128,128]{2,1,0:T(8,128)} %copy-done), custom_call_target="tpu_custom_call" | custom-call | flops 1 | bytes 1 | tf_op jit(solution)/shard_map/pallas_call | solution.py:246
  117.2 5.9 %shard_map.100 = f32[4,256,1024]{2,1,0:T(8,128)} custom-call(s32[3]{0:T(128)} %pad_add_fusion.pos, bf16[4,256,768]{2,1,0:T(8,128)(2,1)} %pad_maximum_fusion.cot_ref, bf16[4,512,768]{2,1,0:T(8,128)(2,1)} %bitcast.11, bf16[256,2048]{1,0:T(8,128)(2,1)} %get-tuple-element.61.refs_0_), custom_call_target="tpu_custom_call" | custom-call | flops 1 | bytes 1 | tf_op jit(solution)/shard_map/pallas_call | solution.py:297
  124.4 24.3 %collective-permute-done.11.refs_0_.refs_1_ = bf16[256,2048]{1,0:T(8,128)(2,1)S(1)} collective-permute-done((bf16[256,2048]{1,0:T(8,128)(2,1)S(1)}, bf16[256,2048]{1,0:T(8,128)(2,1)S(1)}, u32[]{:S(2)}, u32[]{:S(2)}) %collective-permute-start.11) | collective-permute-done | bytes 1048608 | tf_op jit(solution)/shard_map/ppermute | solution.py:390
  150.7 6.0 %shard_map.101 = (f32[256,1024]{1,0:T(8,128)}, bf16[256,1024]{1,0:T(8,128)(2,1)}, bf16[256,1024]{1,0:T(8,128)(2,1)}, bf16[256,1024]{1,0:T(8,128)(2,1)}) custom-call(s32[3]{0:T(128)} %pad_add_fusion.pos, bf16[4,256,768]{2,1,0:T(8,128)(2,1)} %pad_maximum_fusion.cot_ref, bf16[4,512,768]{2,1,0:T(8,128)(2,1)} %bitcast.12, ...), custom_call_target="tpu_custom_call" | custom-call | flops 1 | bytes 1 | tf_op jit(solution)/shard_map/pallas_call | solution.py:297
  156.6 1.2 collective-permute-start.24
  157.8 1.2 collective-permute-start.25
  160.1 3.6 %collective-permute-done.13.refs_3_ = bf16[128,2048]{1,0:T(8,128)(2,1)S(1)} collective-permute-done((bf16[128,2048]{1,0:T(8,128)(2,1)S(1)}, bf16[128,2048]{1,0:T(8,128)(2,1)S(1)}, u32[]{:S(2)}, u32[]{:S(2)}) %collective-permute-start.13) | collective-permute-done | bytes 524320 | tf_op jit(solution)/shard_map/ppermute | solution.py:390
  164.7 37.1 %all-gather.7.cloned.1.call-done = bf16[2048,768]{1,0:T(8,128)(2,1)} async-done(((bf16[512,768]{1,0:T(8,128)(2,1)}), bf16[2048,768]{1,0:T(8,128)(2,1)}) %all-gather.7.cloned.1.call-update) | async-done | bytes 3145744 | tf_op jit(solution)/shard_map/all_gather | solution.py:405
  202.7 5.9 %shard_map.102.refs_0_ = f32[4,256,1024]{2,1,0:T(8,128)} custom-call(s32[3]{0:T(128)} %pad_add_fusion.pos, bf16[4,256,768]{2,1,0:T(8,128)(2,1)} %pad_maximum_fusion.cot_ref, bf16[4,512,768]{2,1,0:T(8,128)(2,1)} %bitcast.14, bf16[256,1024]{1,0:T(8,128)(2,1)} %copy-done.9, bf16[256,1024]{1,0:T(8,128)(2,1)} %copy-done.10, ...), custom_call_target="tpu_custom_call" | custom-call | flops 1 | bytes 1 | tf_op jit(solution)/shard_map/pallas_call | solution.py:297
  209.7 5.6 %shard_map.103 = (f32[256,1024]{1,0:T(8,128)}, f32[8,128,128]{2,1,0:T(8,128)}) custom-call(s32[3]{0:T(128)} %pad_add_fusion.pos, bf16[256,2048]{1,0:T(8,128)(2,1)} %q_ref.9, f32[1,2048]{1,0:T(1,128)} %bitcast.21, f32[256,2048]{1,0:T(8,128)} %get-tuple-element.70.attn_ref, f32[256,1024]{1,0:T(8,128)} %get-tuple-element.71.mine_ref, ...), custom_call_target="tpu_custom_call" | custom-call | flops 1 | bytes 1 | tf_op jit(solution)/shard_map/pallas_call | solution.py:246
  215.4 6.0 %collective-permute-done.27.other_ref = f32[4,256,1024]{2,1,0:T(8,128)} collective-permute-done((f32[4,256,1024]{2,1,0:T(8,128)}, f32[4,256,1024]{2,1,0:T(8,128)}, u32[]{:S(2)}, u32[]{:S(2)}) %collective-permute-start.27) | collective-permute-done | bytes 4194336 | tf_op jit(solution)/shard_map/ppermute | solution.py:394
  221.5 6.0 %shard_map.104 = (f32[256,1024]{1,0:T(8,128)}, bf16[256,1024]{1,0:T(8,128)(2,1)}, bf16[256,1024]{1,0:T(8,128)(2,1)}, bf16[256,1024]{1,0:T(8,128)(2,1)}) custom-call(s32[3]{0:T(128)} %pad_add_fusion.pos, bf16[4,256,768]{2,1,0:T(8,128)(2,1)} %pad_maximum_fusion.cot_ref, bf16[4,512,768]{2,1,0:T(8,128)(2,1)} %bitcast.15, ...), custom_call_target="tpu_custom_call" | custom-call | flops 1 | bytes 1 | tf_op jit(solution)/shard_map/pallas_call | solution.py:297
  227.5 1.5 collective-permute-start.31
  229.1 1.5 collective-permute-start.32
  231.1 6.8 %shard_map.106 = (bf16[256,2048]{1,0:T(8,128)(2,1)}, f32[256,2048]{1,0:T(8,128)}, f32[256,2048]{1,0:T(8,128)}) custom-call(s32[3]{0:T(128)} %pad_add_fusion.pos, bf16[256,2048]{1,0:T(8,128)(2,1)} %q_ref.9, bf16[256,2048]{1,0:T(8,128)(2,1)} %k_ref.9, bf16[256,2048]{1,0:T(8,128)(2,1)} %v_ref.9, f32[256,1024]{1,0:T(8,128)} %get-tuple-element.81.g_ref, ...), custom_call_target="tpu_custom_call" | custom-call | flops 1 | bytes 1 | tf_op jit(solution)/shard_map/pallas_call | solution.py:246
  239.6 15.9 %shard_map.105 = (bf16[256,768]{1,0:T(8,128)(2,1)}, bf16[256,768]{1,0:T(8,128)(2,1)}, bf16[256,768]{1,0:T(8,128)(2,1)}, bf16[256,768]{1,0:T(8,128)(2,1)}) custom-call(s32[3]{0:T(128)} %pad_add_fusion.pos, bf16[256,2048]{1,0:T(8,128)(2,1)} %get-tuple-element.61.refs_0_, bf16[256,2048]{1,0:T(8,128)(2,1)} %copy-done.1, bf16[256,2048]{1,0:T(8,128)(2,1)} %copy-done.3, ...), custom_call_target="tpu_custom_call" | custom-call | flops 1 | bytes 1 | tf_op jit(solution)/shard_map/pallas_call | solution.py:373
  256.6 5.5 %shard_map.107 = (f32[256,1024]{1,0:T(8,128)}, f32[8,128,128]{2,1,0:T(8,128)}) custom-call(s32[3]{0:T(128)} %pad_add_fusion.pos, bf16[256,2048]{1,0:T(8,128)(2,1)} %q_ref.9, f32[1,2048]{1,0:T(1,128)} %bitcast.22, f32[256,2048]{1,0:T(8,128)} %get-tuple-element.70.attn_ref, f32[256,1024]{1,0:T(8,128)} %get-tuple-element.78.mine_ref, ...), custom_call_target="tpu_custom_call" | custom-call | flops 1 | bytes 1 | tf_op jit(solution)/shard_map/pallas_call | solution.py:246
  262.2 2.3 shard_map.109
  264.5 1.5 collective-permute-start.34
  266.0 1.5 collective-permute-start.35
  268.0 6.0 %collective-permute-done.34.refs_1_ = f32[4,128,128]{2,1,0:T(8,128)S(1)} collective-permute-done((f32[4,128,128]{2,1,0:T(8,128)}, f32[4,128,128]{2,1,0:T(8,128)S(1)}, u32[]{:S(2)}, u32[]{:S(2)}) %collective-permute-start.34) | collective-permute-done | bytes 262176 | tf_op jit(solution)/shard_map/ppermute | solution.py:390
  274.0 5.3 %collective-permute-done.35.refs_2_ = f32[4,128,128]{2,1,0:T(8,128)S(1)} collective-permute-done((f32[4,128,128]{2,1,0:T(8,128)}, f32[4,128,128]{2,1,0:T(8,128)S(1)}, u32[]{:S(2)}, u32[]{:S(2)}) %collective-permute-start.35) | collective-permute-done | bytes 262176 | tf_op jit(solution)/shard_map/ppermute | solution.py:390
  280.1 2.0 shard_map.110.refs_0_
  282.0 1.3 collective-permute-start.37
  283.3 1.2 collective-permute-start.28
  285.4 6.9 %shard_map.108 = (bf16[256,2048]{1,0:T(8,128)(2,1)}, f32[256,2048]{1,0:T(8,128)}, f32[256,2048]{1,0:T(8,128)}) custom-call(s32[3]{0:T(128)} %pad_add_fusion.pos, bf16[256,2048]{1,0:T(8,128)(2,1)} %q_ref.9, bf16[256,2048]{1,0:T(8,128)(2,1)} %k_ref.9, bf16[256,2048]{1,0:T(8,128)(2,1)} %v_ref.9, ...), custom_call_target="tpu_custom_call", output_to_operand_aliasing={{0}: (7, {}), {1}: (8, {}), {2}: (9, {})} | custom-call | flops 1 | bytes 1 | tf_op jit(solution)/shard_map/pallas_call | solution.py:246
  293.0 1.8 shard_map.111
  294.8 1.3 collective-permute-start.38
  296.1 1.5 collective-permute-start.30
  297.9 11.5 %collective-permute-done.38.far_ref = f32[4,128,128]{2,1,0:T(8,128)S(1)} collective-permute-done((f32[4,128,128]{2,1,0:T(8,128)}, f32[4,128,128]{2,1,0:T(8,128)S(1)}, u32[]{:S(2)}, u32[]{:S(2)}) %collective-permute-start.38) | collective-permute-done | bytes 262176 | tf_op jit(solution)/shard_map/ppermute | solution.py:400
  310.0 2.4 shard_map.112
  313.0 1.4 collective-permute-start.40
  314.5 1.5 collective-permute-start.41
  316.1 5.7 %collective-permute-done.39 = f32[4,128,128]{2,1,0:T(8,128)S(1)} collective-permute-done((f32[4,128,128]{2,1,0:T(8,128)}, f32[4,128,128]{2,1,0:T(8,128)S(1)}, u32[]{:S(2)}, u32[]{:S(2)}) %collective-permute-start.39) | collective-permute-done | bytes 262176 | tf_op jit(solution)/shard_map/ppermute | solution.py:390
  321.8 2.2 collective-permute-done.40
  324.0 1.5 collective-permute-done.41
  326.6 8.3 %shard_map.113 = (bf16[256,2048]{1,0:T(8,128)(2,1)}, bf16[256,2048]{1,0:T(8,128)(2,1)}) custom-call(s32[3]{0:T(128)} %pad_add_fusion.pos, bf16[256,2048]{1,0:T(8,128)(2,1)} %k_ref.9, bf16[256,2048]{1,0:T(8,128)(2,1)} %v_ref.9, f32[256,2048]{1,0:T(8,128)} %get-tuple-element.87.gk_ref, f32[256,2048]{1,0:T(8,128)} %get-tuple-element.88.gv_ref, ...), custom_call_target="tpu_custom_call" | custom-call | flops 1 | bytes 1 | tf_op jit(solution)/shard_map/pallas_call | solution.py:246
  (162 shorter events, 25.2 us)
Async XLA Ops:
  7.2 110.0 %all-gather.5.cloned.1.call-start = ((), (), s32[]{:S(2)}) async-start(), calls=%async_computation | async-start | bytes 3932160 | tf_op jit(solution)/shard_map/all_gather | solution.py:405
  10.4 13.1 %collective-permute-start.20 = (bf16[256,768]{1,0:T(8,128)(2,1)}, bf16[256,768]{1,0:T(8,128)(2,1)S(1)}, u32[]{:S(2)}, u32[]{:S(2)}) collective-permute-start(bf16[256,768]{1,0:T(8,128)(2,1)} %get-tuple-element.62), channel_id=1, source_target_pairs={{0,2},{2,0},{4,6},{6,4},{8,10},{10,8},{12,14},{14,12},{16,18},{18,... | collective-permute-start | bytes 1179656 | tf_op jit(solution)/shard_map/ppermute | solution.py:390
  13.4 19.2 %collective-permute-start.21 = (bf16[256,768]{1,0:T(8,128)(2,1)}, bf16[256,768]{1,0:T(8,128)(2,1)S(1)}, u32[]{:S(2)}, u32[]{:S(2)}) collective-permute-start(bf16[256,768]{1,0:T(8,128)(2,1)} %get-tuple-element.63), channel_id=1, source_target_pairs={{0,4},{2,6},{4,0},{6,2},{8,12},{10,14},{12,8},{14,10},{16,20},{18,... | collective-permute-start | bytes 1179656 | tf_op jit(solution)/shard_map/ppermute | solution.py:390
  14.9 17.7 %collective-permute-start.22 = (bf16[256,768]{1,0:T(8,128)(2,1)}, bf16[256,768]{1,0:T(8,128)(2,1)S(1)}, u32[]{:S(2)}, u32[]{:S(2)}) collective-permute-start(bf16[256,768]{1,0:T(8,128)(2,1)} %get-tuple-element.64), channel_id=1, source_target_pairs={{0,6},{2,4},{4,2},{6,0},{8,14},{10,12},{12,10},{14,8},{16,22},{18,... | collective-permute-start | bytes 1179656 | tf_op jit(solution)/shard_map/ppermute | solution.py:390
  18.1 18.1 %copy-start.48 = (f32[4,128,128]{2,1,0:T(8,128)S(1)}, f32[4,128,128]{2,1,0:T(8,128)}, u32[]{:S(2)}) copy-start(f32[4,128,128]{2,1,0:T(8,128)} %get-tuple-element.54) | copy-start | bytes 786436
  18.1 19.3 %copy-start.47 = (f32[4,128,128]{2,1,0:T(8,128)S(1)}, f32[4,128,128]{2,1,0:T(8,128)}, u32[]{:S(2)}) copy-start(f32[4,128,128]{2,1,0:T(8,128)} %get-tuple-element.55) | copy-start | bytes 786436
  18.1 20.3 %copy-start.46 = (f32[4,128,128]{2,1,0:T(8,128)S(1)}, f32[4,128,128]{2,1,0:T(8,128)}, u32[]{:S(2)}) copy-start(f32[4,128,128]{2,1,0:T(8,128)} %get-tuple-element.56) | copy-start | bytes 786436
  18.1 21.7 %copy-start.13 = (bf16[256,3072]{1,0:T(8,128)(2,1)S(1)}, bf16[256,3072]{1,0:T(8,128)(2,1)}, u32[]{:S(2)}) copy-start(bf16[256,3072]{1,0:T(8,128)(2,1)} %param.11) | copy-start | bytes 4718596
  23.5 9.1 %copy-start.36 = (bf16[256,768]{1,0:T(8,128)(2,1)}, bf16[256,768]{1,0:T(8,128)(2,1)S(1)}, u32[]{:S(2)}) copy-start(bf16[256,768]{1,0:T(8,128)(2,1)S(1)} %collective-permute-done.20.refs_1_) | copy-start | bytes 1179652
  36.2 165.5 %all-gather.7.cloned.1.call-start = ((), (), s32[]{:S(2)}) async-start(), calls=%async_computation.1 | async-start | bytes 3932160 | tf_op jit(solution)/shard_map/all_gather | solution.py:405
  36.2 9.3 %collective-permute-start = (f32[4,128,128]{2,1,0:T(8,128)S(1)}, f32[4,128,128]{2,1,0:T(8,128)S(1)}, u32[]{:S(2)}, u32[]{:S(2)}) collective-permute-start(f32[4,128,128]{2,1,0:T(8,128)S(1)} %copy-done.48), channel_id=1, source_target_pairs={{0,2},{2,0},{4,6},{6,4},{8,10},{10,8},{12,14},{14,12},{16,18},{18,... | collective-permute-start | bytes 786440 | tf_op jit(solution)/shard_map/ppermute | solution.py:390
  37.4 13.9 %collective-permute-start.1 = (f32[4,128,128]{2,1,0:T(8,128)S(1)}, f32[4,128,128]{2,1,0:T(8,128)S(1)}, u32[]{:S(2)}, u32[]{:S(2)}) collective-permute-start(f32[4,128,128]{2,1,0:T(8,128)S(1)} %copy-done.47), channel_id=1, source_target_pairs={{0,4},{2,6},{4,0},{6,2},{8,12},{10,14},{12,8},{14,10},{16,20},{18,... | collective-permute-start | bytes 786440 | tf_op jit(solution)/shard_map/ppermute | solution.py:390
  38.4 13.8 %collective-permute-start.2 = (f32[4,128,128]{2,1,0:T(8,128)S(1)}, f32[4,128,128]{2,1,0:T(8,128)S(1)}, u32[]{:S(2)}, u32[]{:S(2)}) collective-permute-start(f32[4,128,128]{2,1,0:T(8,128)S(1)} %copy-done.46), channel_id=1, source_target_pairs={{0,6},{2,4},{4,2},{6,0},{8,14},{10,12},{12,10},{14,8},{16,22},{18,... | collective-permute-start | bytes 786440 | tf_op jit(solution)/shard_map/ppermute | solution.py:390
  40.0 19.6 %collective-permute-start.4 = (bf16[256,768]{1,0:T(8,128)(2,1)S(1)}, bf16[256,768]{1,0:T(8,128)(2,1)S(1)}, u32[]{:S(2)}, u32[]{:S(2)}) collective-permute-start(bf16[256,768]{1,0:T(8,128)(2,1)S(1)} %get-tuple-element.102), channel_id=1, source_target_pairs={{0,2},{2,0},{4,6},{6,4},{8,10},{10,8},{12,14},{14,12},{16,18},{18,... | collective-permute-start | bytes 1179656 | tf_op jit(solution)/shard_map/ppermute | solution.py:390
  41.1 25.6 %collective-permute-start.5 = (bf16[256,768]{1,0:T(8,128)(2,1)S(1)}, bf16[256,768]{1,0:T(8,128)(2,1)S(1)}, u32[]{:S(2)}, u32[]{:S(2)}) collective-permute-start(bf16[256,768]{1,0:T(8,128)(2,1)S(1)} %get-tuple-element.101), channel_id=1, source_target_pairs={{0,4},{2,6},{4,0},{6,2},{8,12},{10,14},{12,8},{14,10},{16,20},{18,... | collective-permute-start | bytes 1179656 | tf_op jit(solution)/shard_map/ppermute | solution.py:390
  45.5 6.6 %copy-start.23 = (f32[4,128,128]{2,1,0:T(8,128)}, f32[4,128,128]{2,1,0:T(8,128)S(1)}, u32[]{:S(2)}) copy-start(f32[4,128,128]{2,1,0:T(8,128)S(1)} %collective-permute-done.refs_1_) | copy-start | bytes 786436
  45.5 21.2 %collective-permute-start.6 = (bf16[256,768]{1,0:T(8,128)(2,1)S(1)}, bf16[256,768]{1,0:T(8,128)(2,1)S(1)}, u32[]{:S(2)}, u32[]{:S(2)}) collective-permute-start(bf16[256,768]{1,0:T(8,128)(2,1)S(1)} %get-tuple-element.103), channel_id=1, source_target_pairs={{0,6},{2,4},{4,2},{6,0},{8,14},{10,12},{12,10},{14,8},{16,22},{18,... | collective-permute-start | bytes 1179656 | tf_op jit(solution)/shard_map/ppermute | solution.py:390
  54.8 13.7 %collective-permute-start.3 = (f32[4,128,128]{2,1,0:T(8,128)}, f32[4,128,128]{2,1,0:T(8,128)S(1)}, u32[]{:S(2)}, u32[]{:S(2)}) collective-permute-start(f32[4,128,128]{2,1,0:T(8,128)} %shard_map.95.refs_0_), channel_id=1, source_target_pairs={{0,8},{2,10},{4,12},{6,14},{8,16},{10,18},{12,20},{14,22},{16,24},... | collective-permute-start | bytes 786440 | tf_op jit(solution)/shard_map/ppermute | solution.py:400
  59.6 8.9 %copy-start.14 = (bf16[256,768]{1,0:T(8,128)(2,1)}, bf16[256,768]{1,0:T(8,128)(2,1)S(1)}, u32[]{:S(2)}) copy-start(bf16[256,768]{1,0:T(8,128)(2,1)S(1)} %collective-permute-done.4.refs_2_) | copy-start | bytes 1179652
  71.0 28.8 %copy-start.15 = (bf16[256,768]{1,0:T(8,128)(2,1)S(1)}, bf16[256,768]{1,0:T(8,128)(2,1)}, u32[]{:S(2)}) copy-start(bf16[256,768]{1,0:T(8,128)(2,1)} %copy-done.14) | copy-start | bytes 1179652
  71.0 28.8 %copy-start.17 = (bf16[256,768]{1,0:T(8,128)(2,1)S(1)}, bf16[256,768]{1,0:T(8,128)(2,1)}, u32[]{:S(2)}) copy-start(bf16[256,768]{1,0:T(8,128)(2,1)} %copy-done.16) | copy-start | bytes 1179652
  71.0 28.8 %copy-start.19 = (bf16[256,768]{1,0:T(8,128)(2,1)S(1)}, bf16[256,768]{1,0:T(8,128)(2,1)}, u32[]{:S(2)}) copy-start(bf16[256,768]{1,0:T(8,128)(2,1)} %copy-done.18) | copy-start | bytes 1179652
  71.0 22.2 %collective-permute-start.7 = (f32[4,128,128]{2,1,0:T(8,128)}, f32[4,128,128]{2,1,0:T(8,128)S(1)}, u32[]{:S(2)}, u32[]{:S(2)}) collective-permute-start(f32[4,128,128]{2,1,0:T(8,128)} %shard_map.96), channel_id=1, source_target_pairs={{0,16},{2,18},{4,20},{6,22},{8,24},{10,26},{12,28},{14,30},{1,17},... | collective-permute-start | bytes 786440 | tf_op jit(solution)/shard_map/ppermute | solution.py:400
  96.4 6.6 %collective-permute-start.8 = (f32[4,128,128]{2,1,0:T(8,128)}, f32[4,128,128]{2,1,0:T(8,128)S(1)}, u32[]{:S(2)}, u32[]{:S(2)}) collective-permute-start(f32[4,128,128]{2,1,0:T(8,128)} %get-tuple-element.58), channel_id=1, source_target_pairs={{0,2},{2,0},{4,6},{6,4},{8,10},{10,8},{12,14},{14,12},{16,18},{18,... | collective-permute-start | bytes 786440 | tf_op jit(solution)/shard_map/ppermute | solution.py:390
  98.2 8.7 %collective-permute-start.9 = (f32[4,128,128]{2,1,0:T(8,128)}, f32[4,128,128]{2,1,0:T(8,128)S(1)}, u32[]{:S(2)}, u32[]{:S(2)}) collective-permute-start(f32[4,128,128]{2,1,0:T(8,128)} %get-tuple-element.59), channel_id=1, source_target_pairs={{0,4},{2,6},{4,0},{6,2},{8,12},{10,14},{12,8},{14,10},{16,20},{18,... | collective-permute-start | bytes 786440 | tf_op jit(solution)/shard_map/ppermute | solution.py:390
  101.1 7.3 %collective-permute-start.10 = (f32[4,128,128]{2,1,0:T(8,128)S(1)}, f32[4,128,128]{2,1,0:T(8,128)S(1)}, u32[]{:S(2)}, u32[]{:S(2)}) collective-permute-start(f32[4,128,128]{2,1,0:T(8,128)S(1)} %copy-done.49), channel_id=1, source_target_pairs={{0,6},{2,4},{4,2},{6,0},{8,14},{10,12},{12,10},{14,8},{16,22},{18,... | collective-permute-start | bytes 786440 | tf_op jit(solution)/shard_map/ppermute | solution.py:390
  123.1 27.5 %collective-permute-start.23 = (f32[4,256,1024]{2,1,0:T(8,128)}, f32[4,256,1024]{2,1,0:T(8,128)}, u32[]{:S(2)}, u32[]{:S(2)}) collective-permute-start(f32[4,256,1024]{2,1,0:T(8,128)} %shard_map.100), channel_id=1, source_target_pairs={{0,1},{1,0},{2,3},{3,2},{4,5},{5,4},{6,7},{7,6},{8,9},{9,8},{10,11... | collective-permute-start | bytes 12582920 | tf_op jit(solution)/shard_map/ppermute | solution.py:394
  123.1 25.6 %collective-permute-start.11 = (bf16[256,2048]{1,0:T(8,128)(2,1)S(1)}, bf16[256,2048]{1,0:T(8,128)(2,1)S(1)}, u32[]{:S(2)}, u32[]{:S(2)}) collective-permute-start(bf16[256,2048]{1,0:T(8,128)(2,1)S(1)} %copy-done.5), channel_id=1, source_target_pairs={{0,2},{2,0},{4,6},{6,4},{8,10},{10,8},{12,14},{14,12},{16,18},{18,... | collective-permute-start | bytes 3145736 | tf_op jit(solution)/shard_map/ppermute | solution.py:390
  123.7 26.0 %collective-permute-start.12 = (bf16[256,2048]{1,0:T(8,128)(2,1)S(1)}, bf16[256,2048]{1,0:T(8,128)(2,1)S(1)}, u32[]{:S(2)}, u32[]{:S(2)}) collective-permute-start(bf16[256,2048]{1,0:T(8,128)(2,1)S(1)} %copy-done.5), channel_id=1, source_target_pairs={{0,4},{2,6},{4,0},{6,2},{8,12},{10,14},{12,8},{14,10},{16,20},{18,... | collective-permute-start | bytes 3145736 | tf_op jit(solution)/shard_map/ppermute | solution.py:390
  148.8 14.9 %collective-permute-start.13 = (bf16[128,2048]{1,0:T(8,128)(2,1)S(1)}, bf16[128,2048]{1,0:T(8,128)(2,1)S(1)}, u32[]{:S(2)}, u32[]{:S(2)}) collective-permute-start(bf16[128,2048]{1,0:T(8,128)(2,1)S(1)} %slice.8), channel_id=1, source_target_pairs={{0,4},{2,6},{4,0},{6,2},{8,12},{10,14},{12,8},{14,10},{16,20},{18,... | collective-permute-start | bytes 1572872 | tf_op jit(solution)/shard_map/ppermute | solution.py:390
  149.7 14.9 %collective-permute-start.14 = (bf16[128,2048]{1,0:T(8,128)(2,1)S(1)}, bf16[128,2048]{1,0:T(8,128)(2,1)S(1)}, u32[]{:S(2)}, u32[]{:S(2)}) collective-permute-start(bf16[128,2048]{1,0:T(8,128)(2,1)S(1)} %slice.9), channel_id=1, source_target_pairs={{0,2},{2,0},{4,6},{6,4},{8,10},{10,8},{12,14},{14,12},{16,18},{18,... | collective-permute-start | bytes 1572872 | tf_op jit(solution)/shard_map/ppermute | solution.py:390
  156.6 45.1 %collective-permute-start.24 = (bf16[256,1024]{1,0:T(8,128)(2,1)}, bf16[256,1024]{1,0:T(8,128)(2,1)S(1)}, u32[]{:S(2)}, u32[]{:S(2)}) collective-permute-start(bf16[256,1024]{1,0:T(8,128)(2,1)} %get-tuple-element.67), channel_id=1, source_target_pairs={{0,2},{2,0},{4,6},{6,4},{8,10},{10,8},{12,14},{14,12},{16,18},{18,... | collective-permute-start | bytes 1572872 | tf_op jit(solution)/shard_map/ppermute | solution.py:390
  157.8 43.9 %collective-permute-start.25 = (bf16[256,1024]{1,0:T(8,128)(2,1)}, bf16[256,1024]{1,0:T(8,128)(2,1)S(1)}, u32[]{:S(2)}, u32[]{:S(2)}) collective-permute-start(bf16[256,1024]{1,0:T(8,128)(2,1)} %get-tuple-element.68), channel_id=1, source_target_pairs={{0,4},{2,6},{4,0},{6,2},{8,12},{10,14},{12,8},{14,10},{16,20},{18,... | collective-permute-start | bytes 1572872 | tf_op jit(solution)/shard_map/ppermute | solution.py:390
  159.0 42.7 %collective-permute-start.26 = (bf16[256,1024]{1,0:T(8,128)(2,1)}, bf16[256,1024]{1,0:T(8,128)(2,1)}, u32[]{:S(2)}, u32[]{:S(2)}) collective-permute-start(bf16[256,1024]{1,0:T(8,128)(2,1)} %get-tuple-element.69), channel_id=1, source_target_pairs={{0,6},{2,4},{4,2},{6,0},{8,14},{10,12},{12,10},{14,8},{16,22},{18,... | collective-permute-start | bytes 1572872 | tf_op jit(solution)/shard_map/ppermute | solution.py:390
  163.7 38.0 %copy-start.6 = (bf16[128,2048]{1,0:T(8,128)(2,1)}, bf16[128,2048]{1,0:T(8,128)(2,1)S(1)}, u32[]{:S(2)}) copy-start(bf16[128,2048]{1,0:T(8,128)(2,1)S(1)} %collective-permute-done.13.refs_3_) | copy-start | bytes 1572868
  164.7 37.1 %copy-start.7 = (bf16[128,2048]{1,0:T(8,128)(2,1)}, bf16[128,2048]{1,0:T(8,128)(2,1)S(1)}, u32[]{:S(2)}) copy-start(bf16[128,2048]{1,0:T(8,128)(2,1)S(1)} %collective-permute-done.14.refs_4_) | copy-start | bytes 1572868
  208.6 12.8 %collective-permute-start.27 = (f32[4,256,1024]{2,1,0:T(8,128)}, f32[4,256,1024]{2,1,0:T(8,128)}, u32[]{:S(2)}, u32[]{:S(2)}) collective-permute-start(f32[4,256,1024]{2,1,0:T(8,128)} %shard_map.102.refs_0_), channel_id=1, source_target_pairs={{0,1},{1,0},{2,3},{3,2},{4,5},{5,4},{6,7},{7,6},{8,9},{9,8},{10,11... | collective-permute-start | bytes 12582920 | tf_op jit(solution)/shard_map/ppermute | solution.py:394
  208.6 18.9 %collective-permute-start.15 = (bf16[256,2048]{1,0:T(8,128)(2,1)S(1)}, bf16[256,2048]{1,0:T(8,128)(2,1)S(1)}, u32[]{:S(2)}, u32[]{:S(2)}) collective-permute-start(bf16[256,2048]{1,0:T(8,128)(2,1)S(1)} %copy-done.5), channel_id=1, source_target_pairs={{0,1},{1,0},{2,3},{3,2},{4,5},{5,4},{6,7},{7,6},{8,9},{9,8},{10,11... | collective-permute-start | bytes 3145736 | tf_op jit(solution)/shard_map/ppermute | solution.py:394
  209.1 19.9 %collective-permute-start.16 = (bf16[256,2048]{1,0:T(8,128)(2,1)S(1)}, bf16[256,2048]{1,0:T(8,128)(2,1)S(1)}, u32[]{:S(2)}, u32[]{:S(2)}) collective-permute-start(bf16[256,2048]{1,0:T(8,128)(2,1)S(1)} %copy-done.2), channel_id=1, source_target_pairs={{0,1},{1,0},{2,3},{3,2},{4,5},{5,4},{6,7},{7,6},{8,9},{9,8},{10,11... | collective-permute-start | bytes 3145736 | tf_op jit(solution)/shard_map/ppermute | solution.py:394
  209.1 21.4 %collective-permute-start.17 = (bf16[256,2048]{1,0:T(8,128)(2,1)S(1)}, bf16[256,2048]{1,0:T(8,128)(2,1)S(1)}, u32[]{:S(2)}, u32[]{:S(2)}) collective-permute-start(bf16[256,2048]{1,0:T(8,128)(2,1)S(1)} %copy-done.4), channel_id=1, source_target_pairs={{0,1},{1,0},{2,3},{3,2},{4,5},{5,4},{6,7},{7,6},{8,9},{9,8},{10,11... | collective-permute-start | bytes 3145736 | tf_op jit(solution)/shard_map/ppermute | solution.py:394
  209.7 28.3 %collective-permute-start.18 = (bf16[128,2048]{1,0:T(8,128)(2,1)}, bf16[128,2048]{1,0:T(8,128)(2,1)S(1)}, u32[]{:S(2)}, u32[]{:S(2)}) collective-permute-start(bf16[128,2048]{1,0:T(8,128)(2,1)} %copy-done.6), channel_id=1, source_target_pairs={{0,1},{1,0},{2,3},{3,2},{4,5},{5,4},{6,7},{7,6},{8,9},{9,8},{10,11... | collective-permute-start | bytes 1572872 | tf_op jit(solution)/shard_map/ppermute | solution.py:394
  209.7 11.7 %copy-start.8 = (bf16[128,2048]{1,0:T(8,128)(2,1)S(1)}, bf16[128,2048]{1,0:T(8,128)(2,1)}, u32[]{:S(2)}) copy-start(bf16[128,2048]{1,0:T(8,128)(2,1)} %copy-done.7) | copy-start | bytes 1572868
  221.4 16.6 %collective-permute-start.19 = (bf16[128,2048]{1,0:T(8,128)(2,1)S(1)}, bf16[128,2048]{1,0:T(8,128)(2,1)S(1)}, u32[]{:S(2)}, u32[]{:S(2)}) collective-permute-start(bf16[128,2048]{1,0:T(8,128)(2,1)S(1)} %copy-done.8), channel_id=1, source_target_pairs={{0,1},{1,0},{2,3},{3,2},{4,5},{5,4},{6,7},{7,6},{8,9},{9,8},{10,11... | collective-permute-start | bytes 1572872 | tf_op jit(solution)/shard_map/ppermute | solution.py:394
  227.5 10.4 %copy-start.20 = (bf16[256,2048]{1,0:T(8,128)(2,1)}, bf16[256,2048]{1,0:T(8,128)(2,1)S(1)}, u32[]{:S(2)}) copy-start(bf16[256,2048]{1,0:T(8,128)(2,1)S(1)} %collective-permute-done.15.refs_5_) | copy-start | bytes 3145732
  227.5 27.9 %collective-permute-start.31 = (bf16[256,1024]{1,0:T(8,128)(2,1)}, bf16[256,1024]{1,0:T(8,128)(2,1)S(1)}, u32[]{:S(2)}, u32[]{:S(2)}) collective-permute-start(bf16[256,1024]{1,0:T(8,128)(2,1)} %get-tuple-element.73.refs_12_), channel_id=1, source_target_pairs={{0,2},{2,0},{4,6},{6,4},{8,10},{10,8},{12,14},{14,12},{16,18},{18,... | collective-permute-start | bytes 1572872 | tf_op jit(solution)/shard_map/ppermute | solution.py:390
  229.1 8.9 %copy-start.21 = (bf16[256,2048]{1,0:T(8,128)(2,1)}, bf16[256,2048]{1,0:T(8,128)(2,1)S(1)}, u32[]{:S(2)}) copy-start(bf16[256,2048]{1,0:T(8,128)(2,1)S(1)} %collective-permute-done.16.refs_6_) | copy-start | bytes 3145732
  229.1 26.4 %collective-permute-start.32 = (bf16[256,1024]{1,0:T(8,128)(2,1)}, bf16[256,1024]{1,0:T(8,128)(2,1)S(1)}, u32[]{:S(2)}, u32[]{:S(2)}) collective-permute-start(bf16[256,1024]{1,0:T(8,128)(2,1)} %get-tuple-element.79), channel_id=1, source_target_pairs={{0,4},{2,6},{4,0},{6,2},{8,12},{10,14},{12,8},{14,10},{16,20},{18,... | collective-permute-start | bytes 1572872 | tf_op jit(solution)/shard_map/ppermute | solution.py:390
  230.6 7.4 %copy-start.22 = (bf16[256,2048]{1,0:T(8,128)(2,1)}, bf16[256,2048]{1,0:T(8,128)(2,1)S(1)}, u32[]{:S(2)}) copy-start(bf16[256,2048]{1,0:T(8,128)(2,1)S(1)} %collective-permute-done.17.refs_7_) | copy-start | bytes 3145732
  230.6 24.9 %collective-permute-start.33 = (bf16[256,1024]{1,0:T(8,128)(2,1)}, bf16[256,1024]{1,0:T(8,128)(2,1)S(1)}, u32[]{:S(2)}, u32[]{:S(2)}) collective-permute-start(bf16[256,1024]{1,0:T(8,128)(2,1)} %get-tuple-element.80), channel_id=1, source_target_pairs={{0,6},{2,4},{4,2},{6,0},{8,14},{10,12},{12,10},{14,8},{16,22},{18,... | collective-permute-start | bytes 1572872 | tf_op jit(solution)/shard_map/ppermute | solution.py:390
  262.2 21.1 %copy-start.45 = (bf16[256,768]{1,0:T(8,128)(2,1)S(1)}, bf16[256,768]{1,0:T(8,128)(2,1)}, u32[]{:S(2)}) copy-start(bf16[256,768]{1,0:T(8,128)(2,1)} %get-tuple-element.75) | copy-start | bytes 1179652
  262.2 22.3 %copy-start.44 = (bf16[256,768]{1,0:T(8,128)(2,1)S(1)}, bf16[256,768]{1,0:T(8,128)(2,1)}, u32[]{:S(2)}) copy-start(bf16[256,768]{1,0:T(8,128)(2,1)} %get-tuple-element.76) | copy-start | bytes 1179652
  264.5 9.4 %collective-permute-start.34 = (f32[4,128,128]{2,1,0:T(8,128)}, f32[4,128,128]{2,1,0:T(8,128)S(1)}, u32[]{:S(2)}, u32[]{:S(2)}) collective-permute-start(f32[4,128,128]{2,1,0:T(8,128)} %get-tuple-element.91), channel_id=1, source_target_pairs={{0,2},{2,0},{4,6},{6,4},{8,10},{10,8},{12,14},{14,12},{16,18},{18,... | collective-permute-start | bytes 786440 | tf_op jit(solution)/shard_map/ppermute | solution.py:390
  266.0 13.3 %collective-permute-start.35 = (f32[4,128,128]{2,1,0:T(8,128)}, f32[4,128,128]{2,1,0:T(8,128)S(1)}, u32[]{:S(2)}, u32[]{:S(2)}) collective-permute-start(f32[4,128,128]{2,1,0:T(8,128)} %get-tuple-element.92), channel_id=1, source_target_pairs={{0,4},{2,6},{4,0},{6,2},{8,12},{10,14},{12,8},{14,10},{16,20},{18,... | collective-permute-start | bytes 786440 | tf_op jit(solution)/shard_map/ppermute | solution.py:390
  267.5 11.8 %collective-permute-start.36 = (f32[4,128,128]{2,1,0:T(8,128)}, f32[4,128,128]{2,1,0:T(8,128)S(1)}, u32[]{:S(2)}, u32[]{:S(2)}) collective-permute-start(f32[4,128,128]{2,1,0:T(8,128)} %get-tuple-element.93), channel_id=1, source_target_pairs={{0,6},{2,4},{4,2},{6,0},{8,14},{10,12},{12,10},{14,8},{16,22},{18,... | collective-permute-start | bytes 786440 | tf_op jit(solution)/shard_map/ppermute | solution.py:390
  282.0 10.3 %collective-permute-start.37 = (f32[4,128,128]{2,1,0:T(8,128)}, f32[4,128,128]{2,1,0:T(8,128)S(1)}, u32[]{:S(2)}, u32[]{:S(2)}) collective-permute-start(f32[4,128,128]{2,1,0:T(8,128)} %shard_map.110.refs_0_), channel_id=1, source_target_pairs={{8,0},{10,2},{12,4},{14,6},{16,8},{18,10},{20,12},{22,14},{24,16},... | collective-permute-start | bytes 786440 | tf_op jit(solution)/shard_map/ppermute | solution.py:400
  283.3 31.2 %collective-permute-start.28 = (bf16[256,768]{1,0:T(8,128)(2,1)S(1)}, bf16[256,768]{1,0:T(8,128)(2,1)S(1)}, u32[]{:S(2)}, u32[]{:S(2)}) collective-permute-start(bf16[256,768]{1,0:T(8,128)(2,1)S(1)} %copy-done.45), channel_id=1, source_target_pairs={{0,2},{2,0},{4,6},{6,4},{8,10},{10,8},{12,14},{14,12},{16,18},{18,... | collective-permute-start | bytes 1179656 | tf_op jit(solution)/shard_map/ppermute | solution.py:390
  284.5 31.5 %collective-permute-start.29 = (bf16[256,768]{1,0:T(8,128)(2,1)S(1)}, bf16[256,768]{1,0:T(8,128)(2,1)S(1)}, u32[]{:S(2)}, u32[]{:S(2)}) collective-permute-start(bf16[256,768]{1,0:T(8,128)(2,1)S(1)} %copy-done.44), channel_id=1, source_target_pairs={{0,4},{2,6},{4,0},{6,2},{8,12},{10,14},{12,8},{14,10},{16,20},{18,... | collective-permute-start | bytes 1179656 | tf_op jit(solution)/shard_map/ppermute | solution.py:390
  294.8 14.5 %collective-permute-start.38 = (f32[4,128,128]{2,1,0:T(8,128)}, f32[4,128,128]{2,1,0:T(8,128)S(1)}, u32[]{:S(2)}, u32[]{:S(2)}) collective-permute-start(f32[4,128,128]{2,1,0:T(8,128)} %shard_map.111), channel_id=1, source_target_pairs={{16,0},{18,2},{20,4},{22,6},{24,8},{26,10},{28,12},{30,14},{17,1},... | collective-permute-start | bytes 786440 | tf_op jit(solution)/shard_map/ppermute | solution.py:400
  296.1 19.9 %collective-permute-start.30 = (bf16[256,768]{1,0:T(8,128)(2,1)S(1)}, bf16[256,768]{1,0:T(8,128)(2,1)S(1)}, u32[]{:S(2)}, u32[]{:S(2)}) collective-permute-start(bf16[256,768]{1,0:T(8,128)(2,1)S(1)} %copy-done.43), channel_id=1, source_target_pairs={{0,6},{2,4},{4,2},{6,0},{8,14},{10,12},{12,10},{14,8},{16,22},{18,... | collective-permute-start | bytes 1179656 | tf_op jit(solution)/shard_map/ppermute | solution.py:390
  312.4 13.1 %copy-start.42 = (f32[4,128,128]{2,1,0:T(8,128)S(1)}, f32[4,128,128]{2,1,0:T(8,128)}, u32[]{:S(2)}) copy-start(f32[4,128,128]{2,1,0:T(8,128)} %get-tuple-element.94) | copy-start | bytes 786436
  312.4 9.4 %collective-permute-start.39 = (f32[4,128,128]{2,1,0:T(8,128)}, f32[4,128,128]{2,1,0:T(8,128)S(1)}, u32[]{:S(2)}, u32[]{:S(2)}) collective-permute-start(f32[4,128,128]{2,1,0:T(8,128)} %get-tuple-element.95), channel_id=1, source_target_pairs={{0,2},{2,0},{4,6},{6,4},{8,10},{10,8},{12,14},{14,12},{16,18},{18,... | collective-permute-start | bytes 786440 | tf_op jit(solution)/shard_map/ppermute | solution.py:390
  313.0 11.0 %collective-permute-start.40 = (f32[4,128,128]{2,1,0:T(8,128)}, f32[4,128,128]{2,1,0:T(8,128)S(1)}, u32[]{:S(2)}, u32[]{:S(2)}) collective-permute-start(f32[4,128,128]{2,1,0:T(8,128)} %get-tuple-element.96), channel_id=1, source_target_pairs={{0,4},{2,6},{4,0},{6,2},{8,12},{10,14},{12,8},{14,10},{16,20},{18,... | collective-permute-start | bytes 786440 | tf_op jit(solution)/shard_map/ppermute | solution.py:390
  314.5 11.1 %collective-permute-start.41 = (f32[4,128,128]{2,1,0:T(8,128)}, f32[4,128,128]{2,1,0:T(8,128)S(1)}, u32[]{:S(2)}, u32[]{:S(2)}) collective-permute-start(f32[4,128,128]{2,1,0:T(8,128)} %get-tuple-element.97), channel_id=1, source_target_pairs={{0,6},{2,4},{4,2},{6,0},{8,14},{10,12},{12,10},{14,8},{16,22},{18,... | collective-permute-start | bytes 786440 | tf_op jit(solution)/shard_map/ppermute | solution.py:390
  316.1 18.8 %copy-start.11 = (bf16[256,3072]{1,0:T(8,128)(2,1)}, bf16[256,3072]{1,0:T(8,128)(2,1)S(1)}, u32[]{:S(2)}) copy-start(bf16[256,3072]{1,0:T(8,128)(2,1)S(1)} %constant_dynamic-update-slice_fusion.4) | copy-start | bytes 4718596
  (30 other events, 56.6 us)
Sparse Core Ops, SparseCore 0:
  36.3 70.9 all-gather.4
  123.2 78.4 all-gather.6

commit v4 on v3

--- a/solution.py
+++ b/solution.py
@@ -261,13 +261,13 @@
 def others_kernel(pos, cot_ref, w_ref, *refs):
     out_ref = refs[-1]
     for t in range(PLANE):
-        out_ref[t] = mm(cot_ref[t], w_ref[0], NT)
+        out_ref[t] = mm(cot_ref[t], w_ref[0], NT).astype(BF16)
 
 
 def mine_kernel(pos, cot_ref, w_ref, other_ref, *refs):
     own_ref, sent = refs[-4], refs[-3:]
     for t in range(PLANE):
-        total = mm(cot_ref[t], w_ref[0], NT) + other_ref[t]
+        total = mm(cot_ref[t], w_ref[0], NT) + other_ref[t].astype(F32)
         if t == 0:
             own_ref[...] = total
         else:
@@ -287,7 +287,7 @@
 
     in_specs = [pl.BlockSpec(cot.shape, lambda i, pos: (0, 0, 0)), pl.BlockSpec((1, rows, width), plane_of)]
     if taken is None:
-        kernel, out_specs, out_shape, given = others_kernel, block, jax.ShapeDtypeStruct(whole, F32), ()
+        kernel, out_specs, out_shape, given = others_kernel, block, jax.ShapeDtypeStruct(whole, BF16), ()
     else:
         kernel, given = mine_kernel, (taken,)
         in_specs.append(block)

time: 343 us -> 336 us (0.980)
  waiting for transfers between devices: 154 us -> 147 us
    all_gather x2, waiting for transfers between devices: 37.1 us -> 15.3 us  [z_gather(): return lax.all_gather(value, 'ctx', axis_index_groups=lines)]
    ppermute x4, waiting for transfers between devices: 23 us -> 36.1 us  [z_shift(): return lax.ppermute(value, 'ctx', pairs)]
    ppermute x31, waiting for transfers between devices: 88.2 us -> 93 us  [plane_swap(): lax.ppermute(value, 'ctx', [(i, i ^ k) for i in range(PLANE * PLANES)])]
    ppermute x7, waiting for transfers between devices: 6.02 us -> 2.21 us  [core_swap(): return lax.ppermute(value, 'tp', [(0, 1), (1, 0)])]
    unnamed x103 -> x99, local copies, waits for them, and re-layouts: 9.96 us -> 11.6 us
  transfers between devices with their start and end apart: 44 -> 44, of which waited for: 23 -> 25; matrix products, arithmetic and copies ran while one was open for 1% -> 1% of each run, Pallas kernels for 20% -> 22%
where the time goes in v4:
time: 336 us; the launch traced here: 335 us
  waiting for transfers between devices  147 us (44%)
  Pallas kernels  103 us (31%)
  starting transfers between devices  55.2 us (16%)
  between operations  14.5 us (4%)
  local copies, waits for them, and re-layouts  12.2 us (4%)
    ppermute x31, waiting for transfers between devices, plane_swap(): lax.ppermute(value, 'ctx', [(i, i ^ k) for i in range(PLANE * PLANES)])  93 us
    pallas_call x6, Pallas kernels, by_heads(): pl.pallas_call(kernel, grid_spec=pltpu.PrefetchScalarGridSpec(num_scalar_...  40.8 us
    ppermute x4, waiting for transfers between devices, z_shift(): return lax.ppermute(value, 'ctx', pairs)  36.1 us
    ppermute x31, starting transfers between devices, plane_swap(): lax.ppermute(value, 'ctx', [(i, i ^ k) for i in range(PLANE * PLANES)])  35.4 us
    pallas_call x4, Pallas kernels, partial_grads(): pl.pallas_call(kernel, grid_spec=pltpu.PrefetchScalarGridSpec(num_scalar_...  22.4 us
    ppermute x4, starting transfers between devices, z_shift(): return lax.ppermute(value, 'ctx', pairs)  18.5 us
    pallas_call x1, Pallas kernels, mixed_blocks(): pl.pallas_call(mixed_kernel, in_specs=[pl.BlockSpec(memory_space=pltpu.SM...  15.9 us
    all_gather x2, waiting for transfers between devices, z_gather(): return lax.all_gather(value, 'ctx', axis_index_groups=lines)  15.3 us
  transfers between devices with their start and end apart: 44, of which 25 were waited for; matrix products, arithmetic and copies ran while one was open for 1% of the time, Pallas kernels for 22%

profile of v4, /device:TPU:0, one launch (start us, length us, event | category | flops | bytes accessed | tf_op | source)
XLA Modules:
  0.0 334.9 jit_solution(5869342658536415176)
XLA Ops:
  7.8 2.7 shard_map.93
  10.5 2.9 collective-permute-start.20
  13.4 1.5 collective-permute-start.21
  14.9 3.2 shard_map.94
  18.2 5.4 %collective-permute-done.20.refs_1_ = bf16[256,768]{1,0:T(8,128)(2,1)S(1)} collective-permute-done((bf16[256,768]{1,0:T(8,128)(2,1)}, bf16[256,768]{1,0:T(8,128)(2,1)S(1)}, u32[]{:S(2)}, u32[]{:S(2)}) %collective-permute-start.20) | collective-permute-done | bytes 393248 | tf_op jit(solution)/shard_map/ppermute | solution.py:390
  23.6 9.1 %collective-permute-done.21.refs_2_ = bf16[256,768]{1,0:T(8,128)(2,1)S(1)} collective-permute-done((bf16[256,768]{1,0:T(8,128)(2,1)}, bf16[256,768]{1,0:T(8,128)(2,1)S(1)}, u32[]{:S(2)}, u32[]{:S(2)}) %collective-permute-start.21) | collective-permute-done | bytes 393248 | tf_op jit(solution)/shard_map/ppermute | solution.py:390
  33.5 2.9 shard_map.99
  39.3 1.4 collective-permute-start.2
  40.9 1.6 collective-permute-start.5
  43.0 3.5 %collective-permute-done.refs_1_ = f32[4,128,128]{2,1,0:T(8,128)S(1)} collective-permute-done((f32[4,128,128]{2,1,0:T(8,128)S(1)}, f32[4,128,128]{2,1,0:T(8,128)S(1)}, u32[]{:S(2)}, u32[]{:S(2)}) %collective-permute-start) | collective-permute-done | bytes 262176 | tf_op jit(solution)/shard_map/ppermute | solution.py:390
  46.5 1.5 collective-permute-start.6
  48.0 4.3 %collective-permute-done.1.refs_2_ = f32[4,128,128]{2,1,0:T(8,128)S(1)} collective-permute-done((f32[4,128,128]{2,1,0:T(8,128)S(1)}, f32[4,128,128]{2,1,0:T(8,128)S(1)}, u32[]{:S(2)}, u32[]{:S(2)}) %collective-permute-start.1) | collective-permute-done | bytes 262176 | tf_op jit(solution)/shard_map/ppermute | solution.py:390
  53.8 1.9 shard_map.95.refs_0_
  55.8 3.5 %collective-permute-start.3 = (f32[4,128,128]{2,1,0:T(8,128)}, f32[4,128,128]{2,1,0:T(8,128)S(1)}, u32[]{:S(2)}, u32[]{:S(2)}) collective-permute-start(f32[4,128,128]{2,1,0:T(8,128)} %shard_map.95.refs_0_), channel_id=1, source_target_pairs={{0,8},{2,10},{4,12},{6,14},{8,16},{10,18},{12,20},{14,22},{16,24},... | collective-permute-start | bytes 786440 | tf_op jit(solution)/shard_map/ppermute | solution.py:400
  59.2 8.5 %collective-permute-done.5.refs_3_ = bf16[256,768]{1,0:T(8,128)(2,1)S(1)} collective-permute-done((bf16[256,768]{1,0:T(8,128)(2,1)S(1)}, bf16[256,768]{1,0:T(8,128)(2,1)S(1)}, u32[]{:S(2)}, u32[]{:S(2)}) %collective-permute-start.5) | collective-permute-done | bytes 393248 | tf_op jit(solution)/shard_map/ppermute | solution.py:390
  67.8 1.7 collective-permute-done.3.refs_1_.near_ref
  70.2 1.8 shard_map.96
  72.0 12.5 %collective-permute-start.7 = (f32[4,128,128]{2,1,0:T(8,128)}, f32[4,128,128]{2,1,0:T(8,128)S(1)}, u32[]{:S(2)}, u32[]{:S(2)}) collective-permute-start(f32[4,128,128]{2,1,0:T(8,128)} %shard_map.96), channel_id=1, source_target_pairs={{0,16},{2,18},{4,20},{6,22},{8,24},{10,26},{12,28},{14,30},{1,17},... | collective-permute-start | bytes 786440 | tf_op jit(solution)/shard_map/ppermute | solution.py:400
  84.5 9.8 %collective-permute-done.7.far_ref = f32[4,128,128]{2,1,0:T(8,128)S(1)} collective-permute-done((f32[4,128,128]{2,1,0:T(8,128)}, f32[4,128,128]{2,1,0:T(8,128)S(1)}, u32[]{:S(2)}, u32[]{:S(2)}) %collective-permute-start.7) | collective-permute-done | bytes 262176 | tf_op jit(solution)/shard_map/ppermute | solution.py:400
  95.0 2.5 shard_map.97
  97.4 1.9 collective-permute-start.8
  99.3 1.7 collective-permute-start.9
  101.1 1.3 pad_maximum_fusion.cot_ref
  102.5 1.6 collective-permute-done.8
  104.1 4.1 %collective-permute-done.9 = f32[4,128,128]{2,1,0:T(8,128)S(1)} collective-permute-done((f32[4,128,128]{2,1,0:T(8,128)}, f32[4,128,128]{2,1,0:T(8,128)S(1)}, u32[]{:S(2)}, u32[]{:S(2)}) %collective-permute-start.9) | collective-permute-done | bytes 262176 | tf_op jit(solution)/shard_map/ppermute | solution.py:390
  108.1 1.6 collective-permute-done.10
  110.7 7.8 %shard_map.98 = (bf16[256,2048]{1,0:T(8,128)(2,1)}, f32[256,2048]{1,0:T(8,128)}) custom-call(s32[3]{0:T(128)} %pad_add_fusion.pos, bf16[256,2048]{1,0:T(8,128)(2,1)} %q_ref.9, bf16[256,2048]{1,0:T(8,128)(2,1)} %k_ref.9, bf16[256,2048]{1,0:T(8,128)(2,1)} %v_ref.9, f32[1,2048]{1,0:T(1,128)} %bitcast.20, f32[16,128,128]{2,1,0:T(8,128)} %copy-done), custom_call_target="tpu_custom_call" | custom-call | flops 1 | bytes 1 | tf_op jit(solution)/shard_map/pallas_call | solution.py:246
  118.5 5.5 %shard_map.100 = bf16[4,256,1024]{2,1,0:T(8,128)(2,1)} custom-call(s32[3]{0:T(128)} %pad_add_fusion.pos, bf16[4,256,768]{2,1,0:T(8,128)(2,1)} %pad_maximum_fusion.cot_ref, bf16[4,512,768]{2,1,0:T(8,128)(2,1)} %bitcast.11, bf16[256,2048]{1,0:T(8,128)(2,1)} %get-tuple-element.61.refs_0_), custom_call_target="tpu_custom_call" | custom-call | flops 1 | bytes 1 | tf_op jit(solution)/shard_map/pallas_call | solution.py:297
  125.2 24.4 %collective-permute-done.12.refs_1_.refs_2_ = bf16[256,2048]{1,0:T(8,128)(2,1)S(1)} collective-permute-done((bf16[256,2048]{1,0:T(8,128)(2,1)S(1)}, bf16[256,2048]{1,0:T(8,128)(2,1)S(1)}, u32[]{:S(2)}, u32[]{:S(2)}) %collective-permute-start.12) | collective-permute-done | bytes 1048608 | tf_op jit(solution)/shard_map/ppermute | solution.py:390
  150.1 1.3 collective-permute-start.13
  151.5 1.3 copy-done.6
  152.8 5.6 %shard_map.101 = (f32[256,1024]{1,0:T(8,128)}, bf16[256,1024]{1,0:T(8,128)(2,1)}, bf16[256,1024]{1,0:T(8,128)(2,1)}, bf16[256,1024]{1,0:T(8,128)(2,1)}) custom-call(s32[3]{0:T(128)} %pad_add_fusion.pos, bf16[4,256,768]{2,1,0:T(8,128)(2,1)} %pad_maximum_fusion.cot_ref, bf16[4,512,768]{2,1,0:T(8,128)(2,1)} %bitcast.12, bf16[4,256,1024]{2,1,0:T(8,128)(2,1)} %copy-done.6, ...), custom_call_target="tpu_custom_call" | custom-call | flops 1 | bytes 1 | tf_op jit(solution)/shard_map/pallas_call | solution.py:297
  158.4 1.3 collective-permute-start.24
  161.9 2.8 collective-permute-done.14.refs_4_
  165.2 15.3 %all-gather.7.cloned.1.call-done = bf16[2048,768]{1,0:T(8,128)(2,1)} async-done(((bf16[512,768]{1,0:T(8,128)(2,1)}), bf16[2048,768]{1,0:T(8,128)(2,1)}) %all-gather.7.cloned.1.call-update) | async-done | bytes 3145744 | tf_op jit(solution)/shard_map/all_gather | solution.py:405
  180.5 5.5 %collective-permute-done.26.refs_2_.three_ref = bf16[256,1024]{1,0:T(8,128)(2,1)S(1)} collective-permute-done((bf16[256,1024]{1,0:T(8,128)(2,1)}, bf16[256,1024]{1,0:T(8,128)(2,1)S(1)}, u32[]{:S(2)}, u32[]{:S(2)}) %collective-permute-start.26) | collective-permute-done | bytes 524320 | tf_op jit(solution)/shard_map/ppermute | solution.py:390
  186.8 5.5 %shard_map.102.refs_0_ = bf16[4,256,1024]{2,1,0:T(8,128)(2,1)} custom-call(s32[3]{0:T(128)} %pad_add_fusion.pos, bf16[4,256,768]{2,1,0:T(8,128)(2,1)} %pad_maximum_fusion.cot_ref, bf16[4,512,768]{2,1,0:T(8,128)(2,1)} %bitcast.14, bf16[256,1024]{1,0:T(8,128)(2,1)} %copy-done.7, bf16[256,1024]{1,0:T(8,128)(2,1)} %copy-done.8, bf16[256,1024]{1,0:T(8,128)(2,1)} %copy-done.9, ...), custom_call_target="tpu_custom_call" | custom-call | flops 1 | bytes 1 | tf_op jit(solution)/shard_map/pallas_call | solution.py:297
  193.4 5.5 %shard_map.103 = (f32[256,1024]{1,0:T(8,128)}, f32[8,128,128]{2,1,0:T(8,128)}) custom-call(s32[3]{0:T(128)} %pad_add_fusion.pos, bf16[256,2048]{1,0:T(8,128)(2,1)} %q_ref.9, f32[1,2048]{1,0:T(1,128)} %bitcast.21, f32[256,2048]{1,0:T(8,128)} %get-tuple-element.70.attn_ref, f32[256,1024]{1,0:T(8,128)} %get-tuple-element.71.mine_ref, ...), custom_call_target="tpu_custom_call" | custom-call | flops 1 | bytes 1 | tf_op jit(solution)/shard_map/pallas_call | solution.py:246
  198.9 2.2 collective-permute-done.27.other_ref
  201.3 1.2 copy-done.10
  202.5 5.7 %shard_map.104 = (f32[256,1024]{1,0:T(8,128)}, bf16[256,1024]{1,0:T(8,128)(2,1)}, bf16[256,1024]{1,0:T(8,128)(2,1)}, bf16[256,1024]{1,0:T(8,128)(2,1)}) custom-call(s32[3]{0:T(128)} %pad_add_fusion.pos, bf16[4,256,768]{2,1,0:T(8,128)(2,1)} %pad_maximum_fusion.cot_ref, bf16[4,512,768]{2,1,0:T(8,128)(2,1)} %bitcast.15, bf16[4,256,1024]{2,1,0:T(8,128)(2,1)} %copy-done.10, ...), custom_call_target="tpu_custom_call" | custom-call | flops 1 | bytes 1 | tf_op jit(solution)/shard_map/pallas_call | solution.py:297
  208.2 1.3 collective-permute-start.32
  209.5 2.1 collective-permute-start.33
  211.8 6.8 %shard_map.106 = (bf16[256,2048]{1,0:T(8,128)(2,1)}, f32[256,2048]{1,0:T(8,128)}, f32[256,2048]{1,0:T(8,128)}) custom-call(s32[3]{0:T(128)} %pad_add_fusion.pos, bf16[256,2048]{1,0:T(8,128)(2,1)} %q_ref.9, bf16[256,2048]{1,0:T(8,128)(2,1)} %k_ref.9, bf16[256,2048]{1,0:T(8,128)(2,1)} %v_ref.9, f32[256,1024]{1,0:T(8,128)} %get-tuple-element.81.g_ref, ...), custom_call_target="tpu_custom_call" | custom-call | flops 1 | bytes 1 | tf_op jit(solution)/shard_map/pallas_call | solution.py:246
  219.5 15.9 %shard_map.105 = (bf16[256,768]{1,0:T(8,128)(2,1)}, bf16[256,768]{1,0:T(8,128)(2,1)}, bf16[256,768]{1,0:T(8,128)(2,1)}, bf16[256,768]{1,0:T(8,128)(2,1)}) custom-call(s32[3]{0:T(128)} %pad_add_fusion.pos, bf16[256,2048]{1,0:T(8,128)(2,1)} %get-tuple-element.61.refs_0_, bf16[256,2048]{1,0:T(8,128)(2,1)} %copy-done.3, bf16[256,2048]{1,0:T(8,128)(2,1)} %copy-done.1, ...), custom_call_target="tpu_custom_call" | custom-call | flops 1 | bytes 1 | tf_op jit(solution)/shard_map/pallas_call | solution.py:373
  236.6 5.5 %shard_map.107 = (f32[256,1024]{1,0:T(8,128)}, f32[8,128,128]{2,1,0:T(8,128)}) custom-call(s32[3]{0:T(128)} %pad_add_fusion.pos, bf16[256,2048]{1,0:T(8,128)(2,1)} %q_ref.9, f32[1,2048]{1,0:T(1,128)} %bitcast.22, f32[256,2048]{1,0:T(8,128)} %get-tuple-element.70.attn_ref, f32[256,1024]{1,0:T(8,128)} %get-tuple-element.78.mine_ref, ...), custom_call_target="tpu_custom_call" | custom-call | flops 1 | bytes 1 | tf_op jit(solution)/shard_map/pallas_call | solution.py:246
  242.1 2.3 shard_map.109
  244.4 1.9 collective-permute-start.34
  247.9 6.0 %collective-permute-done.34.refs_1_ = f32[4,128,128]{2,1,0:T(8,128)S(1)} collective-permute-done((f32[4,128,128]{2,1,0:T(8,128)}, f32[4,128,128]{2,1,0:T(8,128)S(1)}, u32[]{:S(2)}, u32[]{:S(2)}) %collective-permute-start.34) | collective-permute-done | bytes 262176 | tf_op jit(solution)/shard_map/ppermute | solution.py:390
  253.9 5.5 %collective-permute-done.35.refs_2_ = f32[4,128,128]{2,1,0:T(8,128)S(1)} collective-permute-done((f32[4,128,128]{2,1,0:T(8,128)}, f32[4,128,128]{2,1,0:T(8,128)S(1)}, u32[]{:S(2)}, u32[]{:S(2)}) %collective-permute-start.35) | collective-permute-done | bytes 262176 | tf_op jit(solution)/shard_map/ppermute | solution.py:390
  260.2 2.0 shard_map.110.refs_0_
  262.1 1.3 collective-permute-start.37
  263.9 1.2 collective-permute-start.29
  265.1 6.8 %shard_map.108 = (bf16[256,2048]{1,0:T(8,128)(2,1)}, f32[256,2048]{1,0:T(8,128)}, f32[256,2048]{1,0:T(8,128)}) custom-call(s32[3]{0:T(128)} %pad_add_fusion.pos, bf16[256,2048]{1,0:T(8,128)(2,1)} %q_ref.9, bf16[256,2048]{1,0:T(8,128)(2,1)} %k_ref.9, bf16[256,2048]{1,0:T(8,128)(2,1)} %v_ref.9, ...), custom_call_target="tpu_custom_call", output_to_operand_aliasing={{0}: (7, {}), {1}: (8, {}), {2}: (9, {})} | custom-call | flops 1 | bytes 1 | tf_op jit(solution)/shard_map/pallas_call | solution.py:246
  272.0 11.2 %collective-permute-done.37.refs_1_.near_ref = f32[4,128,128]{2,1,0:T(8,128)S(1)} collective-permute-done((f32[4,128,128]{2,1,0:T(8,128)}, f32[4,128,128]{2,1,0:T(8,128)S(1)}, u32[]{:S(2)}, u32[]{:S(2)}) %collective-permute-start.37) | collective-permute-done | bytes 262176 | tf_op jit(solution)/shard_map/ppermute | solution.py:400
  283.9 1.8 shard_map.111
  285.7 1.3 collective-permute-start.38
  287.0 1.6 collective-permute-start.30
  288.9 13.4 %collective-permute-done.38.far_ref = f32[4,128,128]{2,1,0:T(8,128)S(1)} collective-permute-done((f32[4,128,128]{2,1,0:T(8,128)}, f32[4,128,128]{2,1,0:T(8,128)S(1)}, u32[]{:S(2)}, u32[]{:S(2)}) %collective-permute-start.38) | collective-permute-done | bytes 262176 | tf_op jit(solution)/shard_map/ppermute | solution.py:400
  303.0 2.4 shard_map.112
  307.2 1.7 collective-permute-start.41
  309.1 5.8 %collective-permute-done.39 = f32[4,128,128]{2,1,0:T(8,128)S(1)} collective-permute-done((f32[4,128,128]{2,1,0:T(8,128)}, f32[4,128,128]{2,1,0:T(8,128)S(1)}, u32[]{:S(2)}, u32[]{:S(2)}) %collective-permute-start.39) | collective-permute-done | bytes 262176 | tf_op jit(solution)/shard_map/ppermute | solution.py:390
  315.1 3.6 %collective-permute-done.41 = f32[4,128,128]{2,1,0:T(8,128)S(1)} collective-permute-done((f32[4,128,128]{2,1,0:T(8,128)}, f32[4,128,128]{2,1,0:T(8,128)S(1)}, u32[]{:S(2)}, u32[]{:S(2)}) %collective-permute-start.41) | collective-permute-done | bytes 262176 | tf_op jit(solution)/shard_map/ppermute | solution.py:390
  319.7 8.3 %shard_map.113 = (bf16[256,2048]{1,0:T(8,128)(2,1)}, bf16[256,2048]{1,0:T(8,128)(2,1)}) custom-call(s32[3]{0:T(128)} %pad_add_fusion.pos, bf16[256,2048]{1,0:T(8,128)(2,1)} %k_ref.9, bf16[256,2048]{1,0:T(8,128)(2,1)} %v_ref.9, f32[256,2048]{1,0:T(8,128)} %get-tuple-element.87.gk_ref, f32[256,2048]{1,0:T(8,128)} %get-tuple-element.88.gv_ref, ...), custom_call_target="tpu_custom_call" | custom-call | flops 1 | bytes 1 | tf_op jit(solution)/shard_map/pallas_call | solution.py:246
  (158 shorter events, 25.5 us)
Async XLA Ops:
  7.2 111.3 %all-gather.5.cloned.1.call-start = ((), (), s32[]{:S(2)}) async-start(), calls=%async_computation | async-start | bytes 3932160 | tf_op jit(solution)/shard_map/all_gather | solution.py:405
  10.5 13.1 %collective-permute-start.20 = (bf16[256,768]{1,0:T(8,128)(2,1)}, bf16[256,768]{1,0:T(8,128)(2,1)S(1)}, u32[]{:S(2)}, u32[]{:S(2)}) collective-permute-start(bf16[256,768]{1,0:T(8,128)(2,1)} %get-tuple-element.62), channel_id=1, source_target_pairs={{0,2},{2,0},{4,6},{6,4},{8,10},{10,8},{12,14},{14,12},{16,18},{18,... | collective-permute-start | bytes 1179656 | tf_op jit(solution)/shard_map/ppermute | solution.py:390
  13.4 19.2 %collective-permute-start.21 = (bf16[256,768]{1,0:T(8,128)(2,1)}, bf16[256,768]{1,0:T(8,128)(2,1)S(1)}, u32[]{:S(2)}, u32[]{:S(2)}) collective-permute-start(bf16[256,768]{1,0:T(8,128)(2,1)} %get-tuple-element.63), channel_id=1, source_target_pairs={{0,4},{2,6},{4,0},{6,2},{8,12},{10,14},{12,8},{14,10},{16,20},{18,... | collective-permute-start | bytes 1179656 | tf_op jit(solution)/shard_map/ppermute | solution.py:390
  14.9 17.7 %collective-permute-start.22 = (bf16[256,768]{1,0:T(8,128)(2,1)}, bf16[256,768]{1,0:T(8,128)(2,1)S(1)}, u32[]{:S(2)}, u32[]{:S(2)}) collective-permute-start(bf16[256,768]{1,0:T(8,128)(2,1)} %get-tuple-element.64), channel_id=1, source_target_pairs={{0,6},{2,4},{4,2},{6,0},{8,14},{10,12},{12,10},{14,8},{16,22},{18,... | collective-permute-start | bytes 1179656 | tf_op jit(solution)/shard_map/ppermute | solution.py:390
  23.6 9.1 %copy-start.34 = (bf16[256,768]{1,0:T(8,128)(2,1)}, bf16[256,768]{1,0:T(8,128)(2,1)S(1)}, u32[]{:S(2)}) copy-start(bf16[256,768]{1,0:T(8,128)(2,1)S(1)} %collective-permute-done.20.refs_1_) | copy-start | bytes 1179652
  33.5 5.8 %copy-start.44 = (f32[4,128,128]{2,1,0:T(8,128)S(1)}, f32[4,128,128]{2,1,0:T(8,128)}, u32[]{:S(2)}) copy-start(f32[4,128,128]{2,1,0:T(8,128)} %get-tuple-element.56) | copy-start | bytes 786436
  33.5 7.3 %copy-start.13 = (bf16[256,3072]{1,0:T(8,128)(2,1)S(1)}, bf16[256,3072]{1,0:T(8,128)(2,1)}, u32[]{:S(2)}) copy-start(bf16[256,3072]{1,0:T(8,128)(2,1)} %param.11) | copy-start | bytes 4718596
  36.4 144.0 %all-gather.7.cloned.1.call-start = ((), (), s32[]{:S(2)}) async-start(), calls=%async_computation.1 | async-start | bytes 3932160 | tf_op jit(solution)/shard_map/all_gather | solution.py:405
  37.2 9.3 %collective-permute-start = (f32[4,128,128]{2,1,0:T(8,128)S(1)}, f32[4,128,128]{2,1,0:T(8,128)S(1)}, u32[]{:S(2)}, u32[]{:S(2)}) collective-permute-start(f32[4,128,128]{2,1,0:T(8,128)S(1)} %copy-done.46), channel_id=1, source_target_pairs={{0,2},{2,0},{4,6},{6,4},{8,10},{10,8},{12,14},{14,12},{16,18},{18,... | collective-permute-start | bytes 786440 | tf_op jit(solution)/shard_map/ppermute | solution.py:390
  38.4 13.9 %collective-permute-start.1 = (f32[4,128,128]{2,1,0:T(8,128)S(1)}, f32[4,128,128]{2,1,0:T(8,128)S(1)}, u32[]{:S(2)}, u32[]{:S(2)}) collective-permute-start(f32[4,128,128]{2,1,0:T(8,128)S(1)} %copy-done.45), channel_id=1, source_target_pairs={{0,4},{2,6},{4,0},{6,2},{8,12},{10,14},{12,8},{14,10},{16,20},{18,... | collective-permute-start | bytes 786440 | tf_op jit(solution)/shard_map/ppermute | solution.py:390
  39.3 13.8 %collective-permute-start.2 = (f32[4,128,128]{2,1,0:T(8,128)S(1)}, f32[4,128,128]{2,1,0:T(8,128)S(1)}, u32[]{:S(2)}, u32[]{:S(2)}) collective-permute-start(f32[4,128,128]{2,1,0:T(8,128)S(1)} %copy-done.44), channel_id=1, source_target_pairs={{0,6},{2,4},{4,2},{6,0},{8,14},{10,12},{12,10},{14,8},{16,22},{18,... | collective-permute-start | bytes 786440 | tf_op jit(solution)/shard_map/ppermute | solution.py:390
  40.9 26.8 %collective-permute-start.5 = (bf16[256,768]{1,0:T(8,128)(2,1)S(1)}, bf16[256,768]{1,0:T(8,128)(2,1)S(1)}, u32[]{:S(2)}, u32[]{:S(2)}) collective-permute-start(bf16[256,768]{1,0:T(8,128)(2,1)S(1)} %get-tuple-element.101), channel_id=1, source_target_pairs={{0,4},{2,6},{4,0},{6,2},{8,12},{10,14},{12,8},{14,10},{16,20},{18,... | collective-permute-start | bytes 1179656 | tf_op jit(solution)/shard_map/ppermute | solution.py:390
  42.5 25.2 %collective-permute-start.4 = (bf16[256,768]{1,0:T(8,128)(2,1)S(1)}, bf16[256,768]{1,0:T(8,128)(2,1)S(1)}, u32[]{:S(2)}, u32[]{:S(2)}) collective-permute-start(bf16[256,768]{1,0:T(8,128)(2,1)S(1)} %get-tuple-element.102), channel_id=1, source_target_pairs={{0,2},{2,0},{4,6},{6,4},{8,10},{10,8},{12,14},{14,12},{16,18},{18,... | collective-permute-start | bytes 1179656 | tf_op jit(solution)/shard_map/ppermute | solution.py:390
  46.5 6.6 %copy-start.22 = (f32[4,128,128]{2,1,0:T(8,128)}, f32[4,128,128]{2,1,0:T(8,128)S(1)}, u32[]{:S(2)}) copy-start(f32[4,128,128]{2,1,0:T(8,128)S(1)} %collective-permute-done.refs_1_) | copy-start | bytes 786436
  46.5 21.2 %collective-permute-start.6 = (bf16[256,768]{1,0:T(8,128)(2,1)S(1)}, bf16[256,768]{1,0:T(8,128)(2,1)S(1)}, u32[]{:S(2)}, u32[]{:S(2)}) collective-permute-start(bf16[256,768]{1,0:T(8,128)(2,1)S(1)} %get-tuple-element.103), channel_id=1, source_target_pairs={{0,6},{2,4},{4,2},{6,0},{8,14},{10,12},{12,10},{14,8},{16,22},{18,... | collective-permute-start | bytes 1179656 | tf_op jit(solution)/shard_map/ppermute | solution.py:390
  55.8 13.7 %collective-permute-start.3 = (f32[4,128,128]{2,1,0:T(8,128)}, f32[4,128,128]{2,1,0:T(8,128)S(1)}, u32[]{:S(2)}, u32[]{:S(2)}) collective-permute-start(f32[4,128,128]{2,1,0:T(8,128)} %shard_map.95.refs_0_), channel_id=1, source_target_pairs={{0,8},{2,10},{4,12},{6,14},{8,16},{10,18},{12,20},{14,22},{16,24},... | collective-permute-start | bytes 786440 | tf_op jit(solution)/shard_map/ppermute | solution.py:400
  72.0 29.1 %copy-start.15 = (bf16[256,768]{1,0:T(8,128)(2,1)S(1)}, bf16[256,768]{1,0:T(8,128)(2,1)}, u32[]{:S(2)}) copy-start(bf16[256,768]{1,0:T(8,128)(2,1)} %copy-done.14) | copy-start | bytes 1179652
  72.0 29.1 %copy-start.17 = (bf16[256,768]{1,0:T(8,128)(2,1)S(1)}, bf16[256,768]{1,0:T(8,128)(2,1)}, u32[]{:S(2)}) copy-start(bf16[256,768]{1,0:T(8,128)(2,1)} %copy-done.16) | copy-start | bytes 1179652
  72.0 29.1 %copy-start.19 = (bf16[256,768]{1,0:T(8,128)(2,1)S(1)}, bf16[256,768]{1,0:T(8,128)(2,1)}, u32[]{:S(2)}) copy-start(bf16[256,768]{1,0:T(8,128)(2,1)} %copy-done.18) | copy-start | bytes 1179652
  72.0 22.2 %collective-permute-start.7 = (f32[4,128,128]{2,1,0:T(8,128)}, f32[4,128,128]{2,1,0:T(8,128)S(1)}, u32[]{:S(2)}, u32[]{:S(2)}) collective-permute-start(f32[4,128,128]{2,1,0:T(8,128)} %shard_map.96), channel_id=1, source_target_pairs={{0,16},{2,18},{4,20},{6,22},{8,24},{10,26},{12,28},{14,30},{1,17},... | collective-permute-start | bytes 786440 | tf_op jit(solution)/shard_map/ppermute | solution.py:400
  97.4 6.6 %collective-permute-start.8 = (f32[4,128,128]{2,1,0:T(8,128)}, f32[4,128,128]{2,1,0:T(8,128)S(1)}, u32[]{:S(2)}, u32[]{:S(2)}) collective-permute-start(f32[4,128,128]{2,1,0:T(8,128)} %get-tuple-element.58), channel_id=1, source_target_pairs={{0,2},{2,0},{4,6},{6,4},{8,10},{10,8},{12,14},{14,12},{16,18},{18,... | collective-permute-start | bytes 786440 | tf_op jit(solution)/shard_map/ppermute | solution.py:390
  99.3 8.8 %collective-permute-start.9 = (f32[4,128,128]{2,1,0:T(8,128)}, f32[4,128,128]{2,1,0:T(8,128)S(1)}, u32[]{:S(2)}, u32[]{:S(2)}) collective-permute-start(f32[4,128,128]{2,1,0:T(8,128)} %get-tuple-element.59), channel_id=1, source_target_pairs={{0,4},{2,6},{4,0},{6,2},{8,12},{10,14},{12,8},{14,10},{16,20},{18,... | collective-permute-start | bytes 786440 | tf_op jit(solution)/shard_map/ppermute | solution.py:390
  102.4 7.3 %collective-permute-start.10 = (f32[4,128,128]{2,1,0:T(8,128)S(1)}, f32[4,128,128]{2,1,0:T(8,128)S(1)}, u32[]{:S(2)}, u32[]{:S(2)}) collective-permute-start(f32[4,128,128]{2,1,0:T(8,128)S(1)} %copy-done.47), channel_id=1, source_target_pairs={{0,6},{2,4},{4,2},{6,0},{8,14},{10,12},{12,10},{14,8},{16,22},{18,... | collective-permute-start | bytes 786440 | tf_op jit(solution)/shard_map/ppermute | solution.py:390
  118.5 5.6 %copy-start.5 = (bf16[256,2048]{1,0:T(8,128)(2,1)S(1)}, bf16[256,2048]{1,0:T(8,128)(2,1)}, u32[]{:S(2)}) copy-start(bf16[256,2048]{1,0:T(8,128)(2,1)} %get-tuple-element.61.refs_0_) | copy-start | bytes 3145732
  124.0 27.4 %collective-permute-start.23 = (bf16[4,256,1024]{2,1,0:T(8,128)(2,1)}, bf16[4,256,1024]{2,1,0:T(8,128)(2,1)S(1)}, u32[]{:S(2)}, u32[]{:S(2)}) collective-permute-start(bf16[4,256,1024]{2,1,0:T(8,128)(2,1)} %shard_map.100), channel_id=1, source_target_pairs={{0,1},{1,0},{2,3},{3,2},{4,5},{5,4},{6,7},{7,6},{8,9},{9,8},{10,11... | collective-permute-start | bytes 6291464 | tf_op jit(solution)/shard_map/ppermute | solution.py:394
  124.0 25.6 %collective-permute-start.12 = (bf16[256,2048]{1,0:T(8,128)(2,1)S(1)}, bf16[256,2048]{1,0:T(8,128)(2,1)S(1)}, u32[]{:S(2)}, u32[]{:S(2)}) collective-permute-start(bf16[256,2048]{1,0:T(8,128)(2,1)S(1)} %copy-done.5), channel_id=1, source_target_pairs={{0,4},{2,6},{4,0},{6,2},{8,12},{10,14},{12,8},{14,10},{16,20},{18,... | collective-permute-start | bytes 3145736 | tf_op jit(solution)/shard_map/ppermute | solution.py:390
  124.9 25.2 %collective-permute-start.11 = (bf16[256,2048]{1,0:T(8,128)(2,1)S(1)}, bf16[256,2048]{1,0:T(8,128)(2,1)S(1)}, u32[]{:S(2)}, u32[]{:S(2)}) collective-permute-start(bf16[256,2048]{1,0:T(8,128)(2,1)S(1)} %copy-done.5), channel_id=1, source_target_pairs={{0,2},{2,0},{4,6},{6,4},{8,10},{10,8},{12,14},{14,12},{16,18},{18,... | collective-permute-start | bytes 3145736 | tf_op jit(solution)/shard_map/ppermute | solution.py:390
  149.6 15.0 %collective-permute-start.14 = (bf16[128,2048]{1,0:T(8,128)(2,1)S(1)}, bf16[128,2048]{1,0:T(8,128)(2,1)}, u32[]{:S(2)}, u32[]{:S(2)}) collective-permute-start(bf16[128,2048]{1,0:T(8,128)(2,1)S(1)} %slice.9), channel_id=1, source_target_pairs={{0,2},{2,0},{4,6},{6,4},{8,10},{10,8},{12,14},{14,12},{16,18},{18,... | collective-permute-start | bytes 1572872 | tf_op jit(solution)/shard_map/ppermute | solution.py:390
  150.1 15.0 %collective-permute-start.13 = (bf16[128,2048]{1,0:T(8,128)(2,1)S(1)}, bf16[128,2048]{1,0:T(8,128)(2,1)}, u32[]{:S(2)}, u32[]{:S(2)}) collective-permute-start(bf16[128,2048]{1,0:T(8,128)(2,1)S(1)} %slice.8), channel_id=1, source_target_pairs={{0,4},{2,6},{4,0},{6,2},{8,12},{10,14},{12,8},{14,10},{16,20},{18,... | collective-permute-start | bytes 1572872 | tf_op jit(solution)/shard_map/ppermute | solution.py:390
  158.4 22.1 %collective-permute-start.24 = (bf16[256,1024]{1,0:T(8,128)(2,1)}, bf16[256,1024]{1,0:T(8,128)(2,1)S(1)}, u32[]{:S(2)}, u32[]{:S(2)}) collective-permute-start(bf16[256,1024]{1,0:T(8,128)(2,1)} %get-tuple-element.67), channel_id=1, source_target_pairs={{0,2},{2,0},{4,6},{6,4},{8,10},{10,8},{12,14},{14,12},{16,18},{18,... | collective-permute-start | bytes 1572872 | tf_op jit(solution)/shard_map/ppermute | solution.py:390
  159.6 20.8 %collective-permute-start.25 = (bf16[256,1024]{1,0:T(8,128)(2,1)}, bf16[256,1024]{1,0:T(8,128)(2,1)S(1)}, u32[]{:S(2)}, u32[]{:S(2)}) collective-permute-start(bf16[256,1024]{1,0:T(8,128)(2,1)} %get-tuple-element.68), channel_id=1, source_target_pairs={{0,4},{2,6},{4,0},{6,2},{8,12},{10,14},{12,8},{14,10},{16,20},{18,... | collective-permute-start | bytes 1572872 | tf_op jit(solution)/shard_map/ppermute | solution.py:390
  160.8 25.2 %collective-permute-start.26 = (bf16[256,1024]{1,0:T(8,128)(2,1)}, bf16[256,1024]{1,0:T(8,128)(2,1)S(1)}, u32[]{:S(2)}, u32[]{:S(2)}) collective-permute-start(bf16[256,1024]{1,0:T(8,128)(2,1)} %get-tuple-element.69), channel_id=1, source_target_pairs={{0,6},{2,4},{4,2},{6,0},{8,14},{10,12},{12,10},{14,8},{16,22},{18,... | collective-permute-start | bytes 1572872 | tf_op jit(solution)/shard_map/ppermute | solution.py:390
  180.5 5.5 %copy-start.7 = (bf16[256,1024]{1,0:T(8,128)(2,1)}, bf16[256,1024]{1,0:T(8,128)(2,1)S(1)}, u32[]{:S(2)}) copy-start(bf16[256,1024]{1,0:T(8,128)(2,1)S(1)} %collective-permute-done.24.refs_0_.one_ref) | copy-start | bytes 1572868
  180.5 5.5 %copy-start.8 = (bf16[256,1024]{1,0:T(8,128)(2,1)}, bf16[256,1024]{1,0:T(8,128)(2,1)S(1)}, u32[]{:S(2)}) copy-start(bf16[256,1024]{1,0:T(8,128)(2,1)S(1)} %collective-permute-done.25.refs_1_.two_ref) | copy-start | bytes 1572868
  186.8 6.0 %copy-start.2 = (bf16[256,2048]{1,0:T(8,128)(2,1)S(1)}, bf16[256,2048]{1,0:T(8,128)(2,1)}, u32[]{:S(2)}) copy-start(bf16[256,2048]{1,0:T(8,128)(2,1)} %copy-done.1) | copy-start | bytes 3145732
  186.8 6.0 %copy-start.4 = (bf16[256,2048]{1,0:T(8,128)(2,1)S(1)}, bf16[256,2048]{1,0:T(8,128)(2,1)}, u32[]{:S(2)}) copy-start(bf16[256,2048]{1,0:T(8,128)(2,1)} %copy-done.3) | copy-start | bytes 3145732
  192.3 8.8 %collective-permute-start.27 = (bf16[4,256,1024]{2,1,0:T(8,128)(2,1)}, bf16[4,256,1024]{2,1,0:T(8,128)(2,1)S(1)}, u32[]{:S(2)}, u32[]{:S(2)}) collective-permute-start(bf16[4,256,1024]{2,1,0:T(8,128)(2,1)} %shard_map.102.refs_0_), channel_id=1, source_target_pairs={{0,1},{1,0},{2,3},{3,2},{4,5},{5,4},{6,7},{7,6},{8,9},{9,8},{10,11... | collective-permute-start | bytes 6291464 | tf_op jit(solution)/shard_map/ppermute | solution.py:394
  192.3 15.9 %collective-permute-start.15 = (bf16[256,2048]{1,0:T(8,128)(2,1)S(1)}, bf16[256,2048]{1,0:T(8,128)(2,1)S(1)}, u32[]{:S(2)}, u32[]{:S(2)}) collective-permute-start(bf16[256,2048]{1,0:T(8,128)(2,1)S(1)} %copy-done.5), channel_id=1, source_target_pairs={{0,1},{1,0},{2,3},{3,2},{4,5},{5,4},{6,7},{7,6},{8,9},{9,8},{10,11... | collective-permute-start | bytes 3145736 | tf_op jit(solution)/shard_map/ppermute | solution.py:394
  192.8 16.7 %collective-permute-start.17 = (bf16[256,2048]{1,0:T(8,128)(2,1)S(1)}, bf16[256,2048]{1,0:T(8,128)(2,1)S(1)}, u32[]{:S(2)}, u32[]{:S(2)}) collective-permute-start(bf16[256,2048]{1,0:T(8,128)(2,1)S(1)} %copy-done.2), channel_id=1, source_target_pairs={{0,1},{1,0},{2,3},{3,2},{4,5},{5,4},{6,7},{7,6},{8,9},{9,8},{10,11... | collective-permute-start | bytes 3145736 | tf_op jit(solution)/shard_map/ppermute | solution.py:394
  192.9 18.8 %collective-permute-start.16 = (bf16[256,2048]{1,0:T(8,128)(2,1)S(1)}, bf16[256,2048]{1,0:T(8,128)(2,1)}, u32[]{:S(2)}, u32[]{:S(2)}) collective-permute-start(bf16[256,2048]{1,0:T(8,128)(2,1)S(1)} %copy-done.4), channel_id=1, source_target_pairs={{0,1},{1,0},{2,3},{3,2},{4,5},{5,4},{6,7},{7,6},{8,9},{9,8},{10,11... | collective-permute-start | bytes 3145736 | tf_op jit(solution)/shard_map/ppermute | solution.py:394
  193.4 25.3 %collective-permute-start.19 = (bf16[128,2048]{1,0:T(8,128)(2,1)}, bf16[128,2048]{1,0:T(8,128)(2,1)S(1)}, u32[]{:S(2)}, u32[]{:S(2)}) collective-permute-start(bf16[128,2048]{1,0:T(8,128)(2,1)} %collective-permute-done.14.refs_4_), channel_id=1, source_target_pairs={{0,1},{1,0},{2,3},{3,2},{4,5},{5,4},{6,7},{7,6},{8,9},{9,8},{10,11... | collective-permute-start | bytes 1572872 | tf_op jit(solution)/shard_map/ppermute | solution.py:394
  201.1 17.5 %collective-permute-start.18 = (bf16[128,2048]{1,0:T(8,128)(2,1)}, bf16[128,2048]{1,0:T(8,128)(2,1)}, u32[]{:S(2)}, u32[]{:S(2)}) collective-permute-start(bf16[128,2048]{1,0:T(8,128)(2,1)} %collective-permute-done.13.refs_3_), channel_id=1, source_target_pairs={{0,1},{1,0},{2,3},{3,2},{4,5},{5,4},{6,7},{7,6},{8,9},{9,8},{10,11... | collective-permute-start | bytes 1572872 | tf_op jit(solution)/shard_map/ppermute | solution.py:394
  208.2 10.4 %copy-start.20 = (bf16[256,2048]{1,0:T(8,128)(2,1)}, bf16[256,2048]{1,0:T(8,128)(2,1)S(1)}, u32[]{:S(2)}) copy-start(bf16[256,2048]{1,0:T(8,128)(2,1)S(1)} %collective-permute-done.15.refs_5_) | copy-start | bytes 3145732
  208.2 27.2 %collective-permute-start.32 = (bf16[256,1024]{1,0:T(8,128)(2,1)}, bf16[256,1024]{1,0:T(8,128)(2,1)S(1)}, u32[]{:S(2)}, u32[]{:S(2)}) collective-permute-start(bf16[256,1024]{1,0:T(8,128)(2,1)} %get-tuple-element.79), channel_id=1, source_target_pairs={{0,4},{2,6},{4,0},{6,2},{8,12},{10,14},{12,8},{14,10},{16,20},{18,... | collective-permute-start | bytes 1572872 | tf_op jit(solution)/shard_map/ppermute | solution.py:390
  209.5 9.1 %copy-start.21 = (bf16[256,2048]{1,0:T(8,128)(2,1)}, bf16[256,2048]{1,0:T(8,128)(2,1)S(1)}, u32[]{:S(2)}) copy-start(bf16[256,2048]{1,0:T(8,128)(2,1)S(1)} %collective-permute-done.17.refs_7_) | copy-start | bytes 3145732
  209.5 25.9 %collective-permute-start.33 = (bf16[256,1024]{1,0:T(8,128)(2,1)}, bf16[256,1024]{1,0:T(8,128)(2,1)S(1)}, u32[]{:S(2)}, u32[]{:S(2)}) collective-permute-start(bf16[256,1024]{1,0:T(8,128)(2,1)} %get-tuple-element.80), channel_id=1, source_target_pairs={{0,6},{2,4},{4,2},{6,0},{8,14},{10,12},{12,10},{14,8},{16,22},{18,... | collective-permute-start | bytes 1572872 | tf_op jit(solution)/shard_map/ppermute | solution.py:390
  211.6 23.8 %collective-permute-start.31 = (bf16[256,1024]{1,0:T(8,128)(2,1)}, bf16[256,1024]{1,0:T(8,128)(2,1)S(1)}, u32[]{:S(2)}, u32[]{:S(2)}) collective-permute-start(bf16[256,1024]{1,0:T(8,128)(2,1)} %get-tuple-element.73.refs_12_), channel_id=1, source_target_pairs={{0,2},{2,0},{4,6},{6,4},{8,10},{10,8},{12,14},{14,12},{16,18},{18,... | collective-permute-start | bytes 1572872 | tf_op jit(solution)/shard_map/ppermute | solution.py:390
  242.1 21.4 %copy-start.43 = (bf16[256,768]{1,0:T(8,128)(2,1)S(1)}, bf16[256,768]{1,0:T(8,128)(2,1)}, u32[]{:S(2)}) copy-start(bf16[256,768]{1,0:T(8,128)(2,1)} %get-tuple-element.75) | copy-start | bytes 1179652
  242.1 21.8 %copy-start.42 = (bf16[256,768]{1,0:T(8,128)(2,1)S(1)}, bf16[256,768]{1,0:T(8,128)(2,1)}, u32[]{:S(2)}) copy-start(bf16[256,768]{1,0:T(8,128)(2,1)} %get-tuple-element.76) | copy-start | bytes 1179652
  244.4 9.5 %collective-permute-start.34 = (f32[4,128,128]{2,1,0:T(8,128)}, f32[4,128,128]{2,1,0:T(8,128)S(1)}, u32[]{:S(2)}, u32[]{:S(2)}) collective-permute-start(f32[4,128,128]{2,1,0:T(8,128)} %get-tuple-element.91), channel_id=1, source_target_pairs={{0,2},{2,0},{4,6},{6,4},{8,10},{10,8},{12,14},{14,12},{16,18},{18,... | collective-permute-start | bytes 786440 | tf_op jit(solution)/shard_map/ppermute | solution.py:390
  246.3 13.1 %collective-permute-start.35 = (f32[4,128,128]{2,1,0:T(8,128)}, f32[4,128,128]{2,1,0:T(8,128)S(1)}, u32[]{:S(2)}, u32[]{:S(2)}) collective-permute-start(f32[4,128,128]{2,1,0:T(8,128)} %get-tuple-element.92), channel_id=1, source_target_pairs={{0,4},{2,6},{4,0},{6,2},{8,12},{10,14},{12,8},{14,10},{16,20},{18,... | collective-permute-start | bytes 786440 | tf_op jit(solution)/shard_map/ppermute | solution.py:390
  247.1 12.3 %collective-permute-start.36 = (f32[4,128,128]{2,1,0:T(8,128)}, f32[4,128,128]{2,1,0:T(8,128)S(1)}, u32[]{:S(2)}, u32[]{:S(2)}) collective-permute-start(f32[4,128,128]{2,1,0:T(8,128)} %get-tuple-element.93), channel_id=1, source_target_pairs={{0,6},{2,4},{4,2},{6,0},{8,14},{10,12},{12,10},{14,8},{16,22},{18,... | collective-permute-start | bytes 786440 | tf_op jit(solution)/shard_map/ppermute | solution.py:390
  253.9 5.5 %copy-start.25 = (f32[4,128,128]{2,1,0:T(8,128)}, f32[4,128,128]{2,1,0:T(8,128)S(1)}, u32[]{:S(2)}) copy-start(f32[4,128,128]{2,1,0:T(8,128)S(1)} %collective-permute-done.34.refs_1_) | copy-start | bytes 786436
  262.1 21.0 %collective-permute-start.37 = (f32[4,128,128]{2,1,0:T(8,128)}, f32[4,128,128]{2,1,0:T(8,128)S(1)}, u32[]{:S(2)}, u32[]{:S(2)}) collective-permute-start(f32[4,128,128]{2,1,0:T(8,128)} %shard_map.110.refs_0_), channel_id=1, source_target_pairs={{8,0},{10,2},{12,4},{14,6},{16,8},{18,10},{20,12},{22,14},{24,16},... | collective-permute-start | bytes 786440 | tf_op jit(solution)/shard_map/ppermute | solution.py:400
  263.4 43.8 %collective-permute-start.28 = (bf16[256,768]{1,0:T(8,128)(2,1)S(1)}, bf16[256,768]{1,0:T(8,128)(2,1)S(1)}, u32[]{:S(2)}, u32[]{:S(2)}) collective-permute-start(bf16[256,768]{1,0:T(8,128)(2,1)S(1)} %copy-done.43), channel_id=1, source_target_pairs={{0,2},{2,0},{4,6},{6,4},{8,10},{10,8},{12,14},{14,12},{16,18},{18,... | collective-permute-start | bytes 1179656 | tf_op jit(solution)/shard_map/ppermute | solution.py:390
  263.9 45.1 %collective-permute-start.29 = (bf16[256,768]{1,0:T(8,128)(2,1)S(1)}, bf16[256,768]{1,0:T(8,128)(2,1)S(1)}, u32[]{:S(2)}, u32[]{:S(2)}) collective-permute-start(bf16[256,768]{1,0:T(8,128)(2,1)S(1)} %copy-done.42), channel_id=1, source_target_pairs={{0,4},{2,6},{4,0},{6,2},{8,12},{10,14},{12,8},{14,10},{16,20},{18,... | collective-permute-start | bytes 1179656 | tf_op jit(solution)/shard_map/ppermute | solution.py:390
  272.0 15.0 %copy-start.41 = (bf16[256,768]{1,0:T(8,128)(2,1)S(1)}, bf16[256,768]{1,0:T(8,128)(2,1)}, u32[]{:S(2)}) copy-start(bf16[256,768]{1,0:T(8,128)(2,1)} %get-tuple-element.77) | copy-start | bytes 1179652
  285.7 16.6 %collective-permute-start.38 = (f32[4,128,128]{2,1,0:T(8,128)}, f32[4,128,128]{2,1,0:T(8,128)S(1)}, u32[]{:S(2)}, u32[]{:S(2)}) collective-permute-start(f32[4,128,128]{2,1,0:T(8,128)} %shard_map.111), channel_id=1, source_target_pairs={{16,0},{18,2},{20,4},{22,6},{24,8},{26,10},{28,12},{30,14},{17,1},... | collective-permute-start | bytes 786440 | tf_op jit(solution)/shard_map/ppermute | solution.py:400
  287.0 22.1 %collective-permute-start.30 = (bf16[256,768]{1,0:T(8,128)(2,1)S(1)}, bf16[256,768]{1,0:T(8,128)(2,1)S(1)}, u32[]{:S(2)}, u32[]{:S(2)}) collective-permute-start(bf16[256,768]{1,0:T(8,128)(2,1)S(1)} %copy-done.41), channel_id=1, source_target_pairs={{0,6},{2,4},{4,2},{6,0},{8,14},{10,12},{12,10},{14,8},{16,22},{18,... | collective-permute-start | bytes 1179656 | tf_op jit(solution)/shard_map/ppermute | solution.py:390
  305.4 13.2 %copy-start.40 = (f32[4,128,128]{2,1,0:T(8,128)S(1)}, f32[4,128,128]{2,1,0:T(8,128)}, u32[]{:S(2)}) copy-start(f32[4,128,128]{2,1,0:T(8,128)} %get-tuple-element.94) | copy-start | bytes 786436
  305.4 9.5 %collective-permute-start.39 = (f32[4,128,128]{2,1,0:T(8,128)}, f32[4,128,128]{2,1,0:T(8,128)S(1)}, u32[]{:S(2)}, u32[]{:S(2)}) collective-permute-start(f32[4,128,128]{2,1,0:T(8,128)} %get-tuple-element.95), channel_id=1, source_target_pairs={{0,2},{2,0},{4,6},{6,4},{8,10},{10,8},{12,14},{14,12},{16,18},{18,... | collective-permute-start | bytes 786440 | tf_op jit(solution)/shard_map/ppermute | solution.py:390
  306.2 8.9 %collective-permute-start.40 = (f32[4,128,128]{2,1,0:T(8,128)}, f32[4,128,128]{2,1,0:T(8,128)S(1)}, u32[]{:S(2)}, u32[]{:S(2)}) collective-permute-start(f32[4,128,128]{2,1,0:T(8,128)} %get-tuple-element.96), channel_id=1, source_target_pairs={{0,4},{2,6},{4,0},{6,2},{8,12},{10,14},{12,8},{14,10},{16,20},{18,... | collective-permute-start | bytes 786440 | tf_op jit(solution)/shard_map/ppermute | solution.py:390
  307.2 11.4 %collective-permute-start.41 = (f32[4,128,128]{2,1,0:T(8,128)}, f32[4,128,128]{2,1,0:T(8,128)S(1)}, u32[]{:S(2)}, u32[]{:S(2)}) collective-permute-start(f32[4,128,128]{2,1,0:T(8,128)} %get-tuple-element.97), channel_id=1, source_target_pairs={{0,6},{2,4},{4,2},{6,0},{8,14},{10,12},{12,10},{14,8},{16,22},{18,... | collective-permute-start | bytes 786440 | tf_op jit(solution)/shard_map/ppermute | solution.py:390
  309.1 19.0 %copy-start.11 = (bf16[256,3072]{1,0:T(8,128)(2,1)}, bf16[256,3072]{1,0:T(8,128)(2,1)S(1)}, u32[]{:S(2)}) copy-start(bf16[256,3072]{1,0:T(8,128)(2,1)S(1)} %constant_dynamic-update-slice_fusion.4) | copy-start | bytes 4718596
  (28 other events, 40.3 us)
Sparse Core Ops, SparseCore 0:
  36.6 71.0 all-gather.4
  109.2 71.2 all-gather.6
